TPU v7x, 128 devices: a whole 4x4x4 slice. The times are simulated.
128 devices in a mesh: gx: 16 (over y, z_hi, core), gy: 8 (over z_lo, x).
Axes of the slice: x: 4, y: 4, z: 4 (z_hi: 2, z_lo: 2; z = z_hi * 2 + z_lo), core: 2. Of those that a mesh axis runs over, the one named last changes fastest.
Arguments:
- tokens: bfloat16 [1024, 16384], P(('gx', 'gy')), may hold values from -6 to 6
- queries: bfloat16 [1024, 16384], P(('gx', 'gy')), may hold values from -240 to 240
- page_pool: bfloat16 [4096, 2, 16, 1024], P(('gx', 'gy')), may hold values from -6 to 6
- new_pages: bfloat16 [2048, 2, 16, 1024], P(('gx', 'gy')), may hold values from -6 to 6
- page_table: int32 [2048, 2], P(('gx', 'gy')), may hold values from 0 to 15, as said below
- block_table: int32 [1024, 8], P(('gx', 'gy')), may hold values from 0 to 63, as said below
- context: int32 [1024], P(('gx', 'gy')), may hold values from 1 to 128, as said below
- norm_gain: float32 [16384], replicated, may hold values from 0.1 to 1.9
- gate_weight: bfloat16 [16384, 26624], P('gy', 'gx'), may hold values from -0.046875 to 0.046875
- up_weight: bfloat16 [16384, 26624], P('gy', 'gx'), may hold values from -0.046875 to 0.046875
- down_weight: bfloat16 [26624, 16384], P('gx', 'gy'), may hold values from -0.0390625 to 0.0390625
Outputs:
- layer_out: bfloat16 [1024, 16384], P('gx', 'gy')
Inputs may be any that keep to these rules, and one draw needn't show every extreme that they name: `page_table`: column 0 is an owner index along gx, column 1 a slot below 2; the new pages of one device name distinct (owner, slot) pairs, and each device fills all 2 slots of some owner. `block_table`: an entry below 32 names a resident page; 32 + s * 2 + r names the page that the device with gx index s placed at slot r; only filled slots are named. `context`: every device has a row of length 128.
All inputs are finite; a program needn't handle non-finite values.
Results may differ from a plain program's by a relative error of at most 0.006.
Values may be sent and summed in bfloat16 or wider, within the bound.
No kernel may reach another device: no remote copies, remote signals or barrier semaphores. Data moves between devices by JAX's collectives and lax.ppermute only.
A program may use at most 128 MiB of HBM per device.

v0:
```python
import jax
import jax.numpy as jnp
from jax import lax
from jax.sharding import PartitionSpec as P

HD = 128
KVH = 8
PAGE = 16
CAP = 2


def score_keys(grouped, page_keys):
    return jnp.einsum("rkgd,rlkd->rkgl", grouped, page_keys, preferred_element_type=jnp.float32) * (
        1.0 / HD**0.5
    )


def page_rows(page_store, table_rows, key_span):
    picked = page_store[table_rows]
    row_count = table_rows.shape[0]
    page_keys = picked[:, :, 0].reshape(row_count, key_span, KVH, HD)
    page_values = picked[:, :, 1].reshape(row_count, key_span, KVH, HD)
    return (page_keys, page_values)


def on_device(
    tokens,
    queries,
    page_pool,
    new_pages,
    page_table,
    block_table,
    context,
    norm_gain,
    gate_weight,
    up_weight,
    down_weight,
):
    row_count = tokens.shape[0]
    model_width = tokens.shape[1]
    area_size = lax.axis_size("gx") * CAP
    send_slot = page_table[:, 0] * CAP + page_table[:, 1]
    outgoing = (
        jnp.zeros((area_size,) + new_pages.shape[1:], jnp.bfloat16).at[send_slot].set(new_pages)
    )
    arrived = lax.all_to_all(outgoing, "gx", split_axis=0, concat_axis=0, tiled=True)
    grouped = queries.reshape(row_count, KVH, model_width // (KVH * HD), HD)
    key_span = block_table.shape[1] * PAGE
    page_store = jnp.concatenate([page_pool, arrived], axis=0)
    page_keys, page_values = page_rows(page_store, block_table, key_span)
    scores = score_keys(grouped, page_keys)
    visible = jnp.arange(key_span, dtype=jnp.int32)[None, :] < context[:, None]
    scores = jnp.where(visible[:, None, None, :], scores, jnp.float32(-1e30))
    probs = jax.nn.softmax(scores, axis=-1).astype(jnp.bfloat16)
    attended = jnp.einsum(
        "rkgl,rlkd->rkgd", probs, page_values, preferred_element_type=jnp.float32
    ).reshape(row_count, model_width)
    mixed_rows = (tokens.astype(jnp.float32) + attended).astype(jnp.bfloat16)
    mixed_wide = mixed_rows.astype(jnp.float32)
    normed = (
        mixed_wide
        * lax.rsqrt(jnp.mean(mixed_wide * mixed_wide, axis=-1, keepdims=True) + 1e-05)
        * norm_gain
    ).astype(jnp.bfloat16)
    resid_block, normed_block = (
        lax.all_to_all(mixed_rows, "gy", split_axis=1, concat_axis=0, tiled=True),
        lax.all_to_all(normed, "gy", split_axis=1, concat_axis=0, tiled=True),
    )
    piece = lax.all_gather(normed_block, "gx", axis=0, tiled=True)
    gate_part = jnp.dot(piece, gate_weight, preferred_element_type=jnp.float32)
    up_part = jnp.dot(piece, up_weight, preferred_element_type=jnp.float32)
    partial_sums = jnp.concatenate([gate_part, up_part], axis=1)
    hidden_width = gate_weight.shape[1]
    total_sums = lax.psum(partial_sums, "gy")
    hidden = (jax.nn.silu(total_sums[:, :hidden_width]) * total_sums[:, hidden_width:]).astype(
        jnp.bfloat16
    )
    ffn_block = lax.psum_scatter(
        jnp.dot(hidden, down_weight, preferred_element_type=jnp.float32),
        "gx",
        scatter_dimension=0,
        tiled=True,
    )
    return (resid_block.astype(jnp.float32) + ffn_block).astype(jnp.bfloat16)


def solution(mesh):
    return jax.shard_map(
        on_device,
        mesh=mesh,
        in_specs=(
            P(("gx", "gy"), None),
            P(("gx", "gy"), None),
            P(("gx", "gy"), None, None, None),
            P(("gx", "gy"), None, None, None),
            P(("gx", "gy"), None),
            P(("gx", "gy"), None),
            P(("gx", "gy")),
            P(),
            P("gy", "gx"),
            P("gy", "gx"),
            P("gx", "gy"),
        ),
        out_specs=P("gx", "gy"),
        check_vma=False,
    )
```

profile of v0, /device:TPU:24, one launch (start us, length us, event | category | flops | bytes accessed | tf_op | source)
XLA Modules:
  0.0 567.8 jit_solution(11511745825059385316)
XLA Ops:
  6.5 0.0 copy-start
  6.5 0.8 fusion.26
  7.3 1.6 broadcast_in_dim.17
  8.9 0.0 copy-start.4
  8.9 0.0 copy-start.6
  8.9 3.4 scatter_fusion
  12.3 8.0 %all-to-all-start = ((bf16[32,2,16,1024]{3,2,1,0:T(8,128)(2,1)}), bf16[32,2,16,1024]{3,2,1,0:T(8,128)(2,1)S(1)}, u32[]{:S(2)}, u32[]{:S(2)}) async-start(bf16[32,2,16,1024]{3,2,1,0:T(8,128)(2,1)} %scatter_fusion), calls=%async_computation | async-start | bytes 4194304 | tf_op jit(solution)/shard_map/all_to_all | solution.py:46
  20.3 0.0 all-gather.2.cloned.1.call-start
  20.4 0.0 copy-done.4
  20.4 0.1 reshape.47
  20.5 0.0 copy-done.6
  20.5 0.1 iota_compare_fusion
  20.6 26.8 %all-to-all-done = bf16[32,2,16,1024]{3,2,1,0:T(8,128)(2,1)S(1)} async-done(((bf16[32,2,16,1024]{3,2,1,0:T(8,128)(2,1)}), bf16[32,2,16,1024]{3,2,1,0:T(8,128)(2,1)S(1)}, u32[]{:S(2)}, u32[]{:S(2)}) %all-to-all-start) | async-done | bytes 2097184 | tf_op jit(solution)/shard_map/all_to_all | solution.py:46
  47.4 3.9 pad_maximum_fusion.1
  51.2 5.0 gather_fusion
  56.2 2.7 fusion.30
  58.9 0.6 copy.20
  59.5 0.6 copy.21
  60.1 0.0 copy-done
  60.2 0.0 copy-start.3
  60.2 1.2 fusion.16
  61.4 0.0 copy-start.2
  61.4 0.4 fusion.31
  61.7 1.9 fusion.4
  63.6 0.0 copy-done.2
  63.6 0.4 fusion.19
  64.0 0.0 copy-done.3
  64.0 0.1 fusion.21
  64.2 11.9 %all_to_all.37 = bf16[8,8,2048]{2,0,1:T(8,128)(2,1)} all-to-all(bf16[8,8,2048]{2,0,1:T(8,128)(2,1)S(1)} %bitcast.54), channel_id=1, replica_groups=mesh['gx'=16,'gy'=8] {'gy'}, dimensions={1} | all-to-all | bytes 524288 | tf_op jit(solution)/shard_map/all_to_all | solution.py:67
  76.1 0.0 all-gather.2.cloned.1.call-update
  76.1 0.2 all-reduce.2.cloned.1.call-start
  76.3 55.9 %all-gather.2.cloned.1.call-done = bf16[1024,2048]{1,0:T(8,128)(2,1)} async-done(((bf16[64,2048]{1,0:T(8,128)(2,1)}), bf16[1024,2048]{1,0:T(8,128)(2,1)}) %all-gather.2.cloned.1.call-update) | async-done | bytes 4194320 | tf_op jit(solution)/shard_map/all_gather | solution.py:69
  132.2 0.0 copy-start.5
  132.2 11.6 %fusion.33 = f32[1024,1664]{1,0:T(8,128)S(1)} fusion(bf16[1024,2048]{1,0:T(8,128)(2,1)} %all-gather.2.cloned.1.call-done, bf16[2048,1664]{1,0:T(8,128)(2,1)} %param.20), kind=kOutput, calls=%fused_computation.40 | convolution fusion | flops 6979321856 | bytes 17825792 | tf_op jit(solution)/shard_map/dot_general | solution.py:71
  143.9 0.0 copy-done.5
  143.9 10.7 %fusion.32 = f32[1024,1664]{1,0:T(8,128)S(1)} fusion(bf16[1024,2048]{1,0:T(8,128)(2,1)S(1)} %copy-done.5, bf16[2048,1664]{1,0:T(8,128)(2,1)} %param.19), kind=kOutput, calls=%fused_computation.39 | convolution fusion | flops 6979321856 | bytes 17825792 | tf_op jit(solution)/shard_map/dot_general | solution.py:70
  154.6 5.3 pad_maximum_fusion
  159.8 0.0 all-reduce.2.cloned.1.call-update
  159.8 0.0 reduce-scatter.2.cloned.1.call-start
  159.9 282.2 %all-reduce.2.cloned.1.call-done = f32[1024,3328]{1,0:T(8,128)} async-done(((f32[1024,3328]{1,0:T(8,128)}), f32[1024,3328]{1,0:T(8,128)}) %all-reduce.2.cloned.1.call-update) | async-done | bytes 13631504 | tf_op jit(solution)/shard_map/psum | solution.py:74
  442.1 16.0 %fusion.2 = f32[1024,2048]{1,0:T(8,128)} fusion(bf16[1664,2048]{1,0:T(8,128)(2,1)} %param.21, f32[1024,3328]{1,0:T(8,128)} %all-reduce.2.cloned.1.call-done), kind=kOutput, calls=%fused_computation.7 | convolution fusion | flops 6989545472 | bytes 28835840 | tf_op jit(solution)/shard_map/dot_general | solution.py:79
  458.0 0.0 copy-start.1
  458.0 0.0 reduce-scatter.2.cloned.1.call-update
  458.1 10.2 %all_to_all.38 = bf16[8,8,2048]{2,0,1:T(8,128)(2,1)S(1)} all-to-all(bf16[8,8,2048]{2,0,1:T(8,128)(2,1)S(1)} %bitcast.50), channel_id=1, replica_groups=mesh['gx'=16,'gy'=8] {'gy'}, dimensions={1} | all-to-all | bytes 524288 | tf_op jit(solution)/shard_map/all_to_all | solution.py:66
  468.2 91.3 %reduce-scatter.2.cloned.1.call-done = f32[64,2048]{1,0:T(8,128)} async-done(((f32[1024,2048]{1,0:T(8,128)}), f32[64,2048]{1,0:T(8,128)}) %reduce-scatter.2.cloned.1.call-update) | async-done | bytes 524304 | tf_op jit(solution)/shard_map/reduce_scatter | solution.py:78
  559.5 1.8 fusion.23
  561.3 0.0 copy-done.1
  (3 shorter events, 0.0 us)
Async XLA Ops:
  6.5 53.6 %copy-start = (bf16[8,16384]{1,0:T(8,128)(2,1)S(1)}, bf16[8,16384]{1,0:T(8,128)(2,1)}, u32[]{:S(2)}) copy-start(bf16[8,16384]{1,0:T(8,128)(2,1)} %param.12) | copy-start | bytes 786436
  8.9 11.5 %copy-start.4 = (s32[8,8]{1,0:T(8,128)S(1)}, s32[8,8]{1,0:T(8,128)}, u32[]{:S(2)}) copy-start(s32[8,8]{1,0:T(8,128)} %param.16) | copy-start | bytes 772
  8.9 11.6 %copy-start.6 = (s32[8]{0:T(128)S(1)}, s32[8]{0:T(128)}, u32[]{:S(2)}) copy-start(s32[8]{0:T(128)} %param.17) | copy-start | bytes 100
  12.3 35.0 %all-to-all-start = ((bf16[32,2,16,1024]{3,2,1,0:T(8,128)(2,1)}), bf16[32,2,16,1024]{3,2,1,0:T(8,128)(2,1)S(1)}, u32[]{:S(2)}, u32[]{:S(2)}) async-start(bf16[32,2,16,1024]{3,2,1,0:T(8,128)(2,1)} %scatter_fusion), calls=%async_computation | async-start | bytes 4194304 | tf_op jit(solution)/shard_map/all_to_all | solution.py:46
  20.3 111.9 %all-gather.2.cloned.1.call-start = ((), (), s32[]{:S(2)}) async-start(), calls=%async_computation.4 | async-start | bytes 4456448 | tf_op jit(solution)/shard_map/all_gather | solution.py:69
  60.2 3.9 copy-start.3
  61.4 2.2 copy-start.2
  76.1 365.9 %all-reduce.2.cloned.1.call-start = ((), (), s32[]{:S(2)}) async-start(), calls=%async_computation.5 | async-start | bytes 27262976 | tf_op jit(solution)/shard_map/psum | solution.py:74
  132.2 11.7 %copy-start.5 = (bf16[1024,2048]{1,0:T(8,128)(2,1)S(1)}, bf16[1024,2048]{1,0:T(8,128)(2,1)}, u32[]{:S(2)}) copy-start(bf16[1024,2048]{1,0:T(8,128)(2,1)} %all-gather.2.cloned.1.call-done) | copy-start | bytes 12582916
  159.8 399.7 %reduce-scatter.2.cloned.1.call-start = ((), (), s32[]{:S(2)}) async-start(), calls=%async_computation.6 | async-start | bytes 8912896 | tf_op jit(solution)/shard_map/reduce_scatter | solution.py:78
  458.0 103.3 %copy-start.1 = (bf16[8,16384]{1,0:T(8,128)(2,1)S(1)}, bf16[8,16384]{1,0:T(8,128)(2,1)}, u32[]{:S(2)}) copy-start(bf16[8,16384]{1,0:T(8,128)(2,1)} %param.12) | copy-start | bytes 786436
Sparse Core Ops, SparseCore 0:
  76.2 55.9 all-gather.1
  160.0 282.0 all-reduce.1
  458.2 101.2 reduce-scatter.1
where the time goes:
time: 569 us; the launch traced here: 568 us
  waiting for transfers between devices  456 us (80%)
  matrix products  41.3 us (7%)
  blocking collectives  22.1 us (4%)
  local copies, waits for them, and re-layouts  14 us (2%)
  between operations  13.2 us (2%)
  other arithmetic  12.7 us (2%)
  starting transfers between devices  8.32 us (1%)
    psum x1, waiting for transfers between devices, on_device(): total_sums = lax.psum(partial_sums, 'gy')  282 us
    reduce_scatter x1, waiting for transfers between devices, on_device(): lax.psum_scatter(jnp.dot(hidden, down_weight, preferred_element_type=jnp....  91.3 us
    all_gather x1, waiting for transfers between devices, on_device(): piece = lax.all_gather(normed_block, 'gx', axis=0, tiled=True)  55.9 us
    all_to_all x1, waiting for transfers between devices, on_device(): lax.all_to_all(outgoing, 'gx', split_axis=0, concat_axis=0, tiled=True)  26.8 us
    dot_general x1, matrix products, on_device(): jnp.dot(hidden, down_weight, preferred_element_type=jnp.float32)  16 us
    all_to_all x1, blocking collectives, on_device(): lax.all_to_all(normed, 'gy', split_axis=1, concat_axis=0, tiled=True)  11.9 us
    dot_general x1, matrix products, on_device(): up_part = jnp.dot(piece, up_weight, preferred_element_type=jnp.float32)  11.6 us
  transfers between devices with their start and end apart: 4, of which 4 were waited for; matrix products, arithmetic and copies ran while one was open for 0% of the time, Pallas kernels for 0%

commit v1 on v0

v1 whole, which is shorter than its diff:
```python
import jax
import jax.numpy as jnp
from jax import lax
from jax.sharding import Mesh, PartitionSpec as P

HD = 128
KVH = 8
PAGE = 16
CAP = 2
GX = ("y", "zh", "c")
GY = ("zl", "x")
CHIPS = ("y", "zh")
SWAP = [(0, 1), (1, 0)]


def score_keys(grouped, page_keys):
    return jnp.einsum("rkgd,rlkd->rkgl", grouped, page_keys, preferred_element_type=jnp.float32) * (
        1.0 / HD**0.5
    )


def page_rows(page_store, table_rows, key_span):
    picked = page_store[table_rows]
    row_count = table_rows.shape[0]
    page_keys = picked[:, :, 0].reshape(row_count, key_span, KVH, HD)
    page_values = picked[:, :, 1].reshape(row_count, key_span, KVH, HD)
    return (page_keys, page_values)


def attend(tokens, queries, page_pool, new_pages, page_table, block_table, context):
    row_count, model_width = tokens.shape
    area_size = lax.axis_size(GX) * CAP
    send_slot = page_table[:, 0] * CAP + page_table[:, 1]
    holder = jnp.argmax(jnp.arange(area_size)[:, None] == send_slot[None, :], axis=1)
    arrived = lax.all_to_all(new_pages[holder], GX, split_axis=0, concat_axis=0, tiled=True)
    grouped = queries.reshape(row_count, KVH, model_width // (KVH * HD), HD)
    key_span = block_table.shape[1] * PAGE
    page_store = jnp.concatenate([page_pool, arrived], axis=0)
    page_keys, page_values = page_rows(page_store, block_table, key_span)
    scores = score_keys(grouped, page_keys)
    visible = jnp.arange(key_span, dtype=jnp.int32)[None, :] < context[:, None]
    scores = jnp.where(visible[:, None, None, :], scores, jnp.float32(-1e30))
    probs = jax.nn.softmax(scores, axis=-1).astype(jnp.bfloat16)
    attended = jnp.einsum(
        "rkgl,rlkd->rkgd", probs, page_values, preferred_element_type=jnp.float32
    ).reshape(row_count, model_width)
    return (tokens.astype(jnp.float32) + attended).astype(jnp.bfloat16)


def spread(mixed_rows, norm_gain):
    row_count, model_width = mixed_rows.shape
    parts = lax.axis_size(GY)
    width = model_width // parts
    mixed_wide = mixed_rows.astype(jnp.float32)
    scale = lax.rsqrt(jnp.mean(mixed_wide * mixed_wide, axis=-1, keepdims=True) + 1e-05)
    high = scale.astype(jnp.bfloat16)
    rest = scale - high.astype(jnp.float32)
    middle = rest.astype(jnp.bfloat16)
    low = (rest - middle.astype(jnp.float32)).astype(jnp.bfloat16)
    terms = jnp.concatenate([high, middle, low, jnp.zeros((row_count, 125), jnp.bfloat16)], axis=1)
    payload = jnp.concatenate(
        [
            mixed_rows.reshape(row_count, parts, width),
            jnp.broadcast_to(terms[:, None, :], (row_count, parts, 128)),
        ],
        axis=2,
    )
    block = lax.all_to_all(payload, GY, split_axis=1, concat_axis=0, tiled=True)
    block = block.reshape(row_count * parts, width + 128)
    resid = block[:, :width].astype(jnp.float32)
    scale = (
        block[:, width : width + 1].astype(jnp.float32)
        + block[:, width + 1 : width + 2].astype(jnp.float32)
        + block[:, width + 2 : width + 3].astype(jnp.float32)
    )
    gain = lax.dynamic_slice(norm_gain, (lax.axis_index(GY) * width,), (width,))
    return resid, (resid * scale * gain).astype(jnp.bfloat16)


def on_device(
    tokens,
    queries,
    page_pool,
    new_pages,
    page_table,
    block_table,
    context,
    norm_gain,
    gate_weight,
    up_weight,
    down_weight,
):
    mixed_rows = attend(tokens, queries, page_pool, new_pages, page_table, block_table, context)
    resid, normed_block = spread(mixed_rows, norm_gain)

    return feed_forward(resid, normed_block, gate_weight, up_weight, down_weight)


def dot(a, b):
    return jnp.dot(a, b, preferred_element_type=jnp.float32)


def wide(a):
    return a.astype(jnp.float32)


def narrow(a):
    return a.astype(jnp.bfloat16)


def swap(a, axis):
    return lax.ppermute(a, axis, [(0, 1), (1, 0)])


def halves(a, axis):
    rows = a.shape[0] // 2
    me = lax.axis_index(axis)
    mine = lax.dynamic_slice_in_dim(a, me * rows, rows, 0)
    theirs = lax.dynamic_slice_in_dim(a, (1 - me) * rows, rows, 0)
    return mine, theirs


def join(mine, axis):
    came = swap(mine, axis)
    first = lax.axis_index(axis) == 0
    return jnp.concatenate([jnp.where(first, mine, came), jnp.where(first, came, mine)], axis=0)


def x_sum(part):
    rows, width = part.shape
    came = lax.all_to_all(part.reshape(4, rows // 4, width), "x", split_axis=0, concat_axis=0, tiled=True)
    return jnp.sum(wide(came), axis=0)


def x_gather(a):
    rows, width = a.shape
    came = lax.all_to_all(
        jnp.broadcast_to(a[None], (4, rows, width)), "x", split_axis=0, concat_axis=0, tiled=True
    )
    return came.reshape(4 * rows, width)


def hidden_of(sums):
    width = sums.shape[1] // 2
    return narrow(jax.nn.silu(sums[:, :width]) * sums[:, width:])


def hidden_x_first(part):
    mine, theirs = halves(x_sum(part), "zl")
    sums = mine + wide(swap(narrow(theirs), "zl"))
    return x_gather(join(hidden_of(sums), "zl"))


def hidden_z_first(part):
    mine, theirs = halves(part, "zl")
    half = narrow(wide(mine) + wide(swap(theirs, "zl")))
    return join(x_gather(hidden_of(x_sum(half))), "zl")


def feed_forward(resid, normed_block, gate_weight, up_weight, down_weight):
    rows, width = normed_block.shape
    weight = jnp.concatenate([gate_weight, up_weight], axis=1)
    chip = jnp.concatenate([normed_block, swap(normed_block, "c")], axis=0)
    quad = jnp.concatenate([chip, swap(chip, "zh")], axis=0)
    total = jnp.zeros((2, rows, width), jnp.float32)
    for shift, hidden_from in ((0, hidden_x_first), (1, hidden_z_first), (3, hidden_x_first), (2, hidden_z_first)):
        piece = quad
        if shift:
            piece = lax.ppermute(quad, "y", [((i + shift) % 4, i) for i in range(4)])
        hidden = hidden_from(narrow(dot(piece, weight)))
        down = dot(hidden, down_weight).reshape(2, 2, rows, width)
        came = swap(narrow(down[:, 1]), "c")
        part = down[:, 0] + wide(came)
        if shift:
            part = wide(lax.ppermute(narrow(part), "y", [(i, (i + shift) % 4) for i in range(4)]))
        total = total + part
    ffn_block = total[0] + wide(swap(narrow(total[1]), "zh"))
    return narrow(resid + ffn_block)


def solution(mesh):
    fine = Mesh(mesh.devices.reshape(4, 2, 2, 2, 4), GX + GY)
    rows = P(GX + GY)
    return jax.shard_map(
        on_device,
        mesh=fine,
        in_specs=(rows,) * 7 + (P(), P(GY, GX), P(GY, GX), P(GX, GY)),
        out_specs=P(GX, GY),
        check_vma=False,
    )
```

time: 569 us -> 328 us (0.58)
  waiting for transfers between devices: 456 us -> 147 us
  starting transfers between devices: 8.32 us -> 61.4 us
  local copies, waits for them, and re-layouts: 14 us -> 36.3 us
  blocking collectives: 22.1 us -> 0 us
  matrix products: 41.3 us -> 58.5 us
  between operations: 13.2 us -> 0.58 us
  other arithmetic: 12.7 us -> 21.5 us
    psum x1 -> x0, waiting for transfers between devices: 282 us -> none  [on_device(): total_sums = lax.psum(partial_sums, 'gy')]
    reduce_scatter x1 -> x0, waiting for transfers between devices: 91.3 us -> none  [on_device(): lax.psum_scatter(jnp.dot(hidden, down_weight, preferred_element_type=jnp....]
    ppermute x0 -> x21, waiting for transfers between devices: none -> 73.1 us  [the longest x15 30 us: swap(): return lax.ppermute(a, axis, [(0, 1), (1, 0)])]
    all_gather x1 -> x0, waiting for transfers between devices: 55.9 us -> none  [on_device(): piece = lax.all_gather(normed_block, 'gx', axis=0, tiled=True)]
    all_to_all x1 -> x10, waiting for transfers between devices: 26.8 us -> 73.9 us  [the longest x1 26.8 us: attend(): lax.all_to_all(new_pages[holder], GX, split_axis=0, concat_axis=0, tiled=...]
    all_to_all x1 -> x10, starting transfers between devices: 8.02 us -> 41.9 us  [the longest x4 15 us: x_sum(): lax.all_to_all(part.reshape(4, rows // 4, width), 'x', split_axis=0, conc...]
    all_to_all x2 -> x0, blocking collectives: 22.1 us -> none  [the longest x1 11.9 us: on_device(): lax.all_to_all(normed, 'gy', split_axis=1, concat_axis=0, tiled=True)]
    ppermute x0 -> x21, starting transfers between devices: none -> 19.5 us  [the longest x15 11.9 us: swap(): return lax.ppermute(a, axis, [(0, 1), (1, 0)])]
  transfers between devices with their start and end apart: 4 -> 31, of which waited for: 4 -> 17; matrix products, arithmetic and copies ran while one was open for 0% -> 27% of each run, Pallas kernels for 0% -> 0%
where the time goes in v1:
time: 328 us; the launch traced here: 325 us
  waiting for transfers between devices  147 us (45%)
  starting transfers between devices  61.4 us (19%)
  matrix products  58.5 us (18%)
  local copies, waits for them, and re-layouts  36.3 us (11%)
  other arithmetic  21.5 us (7%)
    dot_general x8, matrix products, dot(): return jnp.dot(a, b, preferred_element_type=jnp.float32)  55.5 us
    ppermute x15, waiting for transfers between devices, swap(): return lax.ppermute(a, axis, [(0, 1), (1, 0)])  30 us
    all_to_all x1, waiting for transfers between devices, attend(): lax.all_to_all(new_pages[holder], GX, split_axis=0, concat_axis=0, tiled=...  26.8 us
    ppermute x3, waiting for transfers between devices, feed_forward(): lax.ppermute(narrow(part), 'y', [(i, (i + shift) % 4) for i in range(4)])  22.8 us
    all_to_all x4, waiting for transfers between devices, x_sum(): lax.all_to_all(part.reshape(4, rows // 4, width), 'x', split_axis=0, conc...  20.5 us
    ppermute x3, waiting for transfers between devices, feed_forward(): piece = lax.ppermute(quad, 'y', [((i + shift) % 4, i) for i in range(4)])  20.3 us
    all_to_all x4, waiting for transfers between devices, x_gather(): lax.all_to_all(jnp.broadcast_to(a[None], (4, rows, width)), 'x', split_ax...  20 us
    all_to_all x4, starting transfers between devices, x_sum(): lax.all_to_all(part.reshape(4, rows // 4, width), 'x', split_axis=0, conc...  15 us
  transfers between devices with their start and end apart: 31, of which 17 were waited for; matrix products, arithmetic and copies ran while one was open for 27% of the time, Pallas kernels for 0%

profile of v1, /device:TPU:24, one launch (start us, length us, event | category | flops | bytes accessed | tf_op | source)
XLA Modules:
  0.0 325.3 jit_solution(3603824190607374339)
XLA Ops:
  1.4 2.0 gather_fusion
  3.4 8.2 %all-to-all-start = ((bf16[32,2,16,1024]{3,2,1,0:T(8,128)(2,1)}), bf16[32,2,16,1024]{3,2,1,0:T(8,128)(2,1)S(1)}, u32[]{:S(2)}, u32[]{:S(2)}) async-start(bf16[32,2,16,1024]{3,2,1,0:T(8,128)(2,1)} %gather_fusion), calls=%async_computation | async-start | bytes 4194304 | tf_op jit(solution)/shard_map/all_to_all | solution.py:35
  11.9 26.8 %all-to-all-done = bf16[32,2,16,1024]{3,2,1,0:T(8,128)(2,1)S(1)} async-done(((bf16[32,2,16,1024]{3,2,1,0:T(8,128)(2,1)}), bf16[32,2,16,1024]{3,2,1,0:T(8,128)(2,1)S(1)}, u32[]{:S(2)}, u32[]{:S(2)}) %all-to-all-start) | async-done | bytes 2097184 | tf_op jit(solution)/shard_map/all_to_all | solution.py:35
  38.6 3.9 %pad_maximum_fusion = bf16[64,2,16,1024]{3,2,1,0:T(8,128)(2,1)} fusion(bf16[32,2,16,1024]{3,2,1,0:T(8,128)(2,1)S(1)} %all-to-all-done, bf16[32,2,16,1024]{3,2,1,0:T(8,128)(2,1)} %param.13), kind=kLoop, calls=%fused_computation.11 | loop fusion | flops 2097152 | bytes 8388608 | tf_op jit(solution)/shard_map/concatenate | solution.py:38
  42.5 5.0 %gather_fusion.1 = bf16[64,2,16,1024]{3,2,1,0:T(8,128)(2,1)} fusion(bf16[64,2,16,1024]{3,2,1,0:T(8,128)(2,1)} %pad_maximum_fusion, s32[1024]{0:T(1024)S(1)} %pad_clamp_fusion), kind=kCustom, calls=%fused_computation.1 | custom fusion | bytes 8388864 | tf_op jit(solution)/shard_map/gather | solution.py:23
  47.6 2.7 fusion.60
  53.4 1.9 fusion.5
  56.8 4.8 %all-to-all-start.1 = ((bf16[8,8,2176]{2,0,1:T(8,128)(2,1)}), bf16[8,8,2176]{2,0,1:T(8,128)(2,1)S(1)}, u32[]{:S(2)}, u32[]{:S(2)}) async-start(bf16[8,8,2176]{2,0,1:T(8,128)(2,1)} %pad_maximum_fusion.3), calls=%async_computation.1 | async-start | bytes 557056 | tf_op jit(solution)/shard_map/all_to_all | solution.py:68
  62.3 6.7 %all-to-all-done.1 = bf16[8,8,2176]{2,0,1:T(8,128)(2,1)S(1)} async-done(((bf16[8,8,2176]{2,0,1:T(8,128)(2,1)}), bf16[8,8,2176]{2,0,1:T(8,128)(2,1)S(1)}, u32[]{:S(2)}, u32[]{:S(2)}) %all-to-all-start.1) | async-done | bytes 278560 | tf_op jit(solution)/shard_map/all_to_all | solution.py:68
  69.3 6.4 %constant_dynamic-update-slice_fusion.1 = bf16[2048,3328]{1,0:T(8,128)(2,1)} fusion(bf16[2048,1664]{1,0:T(8,128)(2,1)} %param.19), kind=kLoop, calls=%fused_computation.105 | loop fusion | bytes 13631488
  77.4 6.3 %constant_dynamic-update-slice_fusion = bf16[2048,3328]{1,0:T(8,128)(2,1)} fusion(bf16[2048,3328]{1,0:T(8,128)(2,1)} %constant_dynamic-update-slice_fusion.1, bf16[2048,1664]{1,0:T(8,128)(2,1)} %param.20), kind=kLoop, calls=%fused_computation.104 | loop fusion | bytes 13631488 | tf_op jit(solution)/shard_map/concatenate | solution.py:162
  83.7 8.0 %collective-permute-done.1 = bf16[128,2048]{1,0:T(8,128)(2,1)S(1)} collective-permute-done((bf16[128,2048]{1,0:T(8,128)(2,1)S(1)}, bf16[128,2048]{1,0:T(8,128)(2,1)S(1)}, u32[]{:S(2)}, u32[]{:S(2)}) %collective-permute-start.1) | collective-permute-done | bytes 524320 | tf_op jit(solution)/shard_map/ppermute | solution.py:112
  94.4 2.8 collective-permute-start.15
  97.5 10.2 %convolution_convert_fusion.3 = bf16[256,3328]{1,0:T(8,128)(2,1)} fusion(bf16[2048,3328]{1,0:T(8,128)(2,1)} %constant_dynamic-update-slice_fusion, bf16[128,2048]{1,0:T(8,128)(2,1)S(1)} %collective-permute-done.1, bf16[64,2048]{1,0:T(8,128)(2,1)S(1)} %collective-permute-done, bf16[64,2048]{1,0:T(8,128)(2,1)S(1)} %fusion.40), kind=kOutput, calls=%fused_computation.10 | convolution fusion | flops 3493658624 | bytes 16384000 | tf_op jit(solution)/shard_map/dot_general | solution.py:100
  107.7 3.8 %all-to-all-start.2 = ((bf16[4,64,3328]{2,1,0:T(8,128)(2,1)}), bf16[4,64,3328]{2,1,0:T(8,128)(2,1)S(1)}, u32[]{:S(2)}, u32[]{:S(2)}) async-start(bf16[4,64,3328]{2,1,0:T(8,128)(2,1)} %bitcast.134), calls=%async_computation.2 | async-start | bytes 3407872 | tf_op jit(solution)/shard_map/all_to_all | solution.py:131
  111.4 7.8 %collective-permute-done.5 = bf16[256,2048]{1,0:T(8,128)(2,1)} collective-permute-done((bf16[256,2048]{1,0:T(8,128)(2,1)}, bf16[256,2048]{1,0:T(8,128)(2,1)}, u32[]{:S(2)}, u32[]{:S(2)}) %collective-permute-start.5) | collective-permute-done | bytes 1048608 | tf_op jit(solution)/shard_map/ppermute | solution.py:169
  119.2 8.9 %convolution_convert_fusion.2 = bf16[256,3328]{1,0:T(8,128)(2,1)S(1)} fusion(bf16[256,2048]{1,0:T(8,128)(2,1)} %collective-permute-done.5, bf16[2048,3328]{1,0:T(8,128)(2,1)} %constant_dynamic-update-slice_fusion), kind=kOutput, calls=%fused_computation.9 | convolution fusion | flops 3490512896 | bytes 16384000 | tf_op jit(solution)/shard_map/dot_general | solution.py:100
  130.3 12.5 %collective-permute-done.15 = bf16[256,2048]{1,0:T(8,128)(2,1)} collective-permute-done((bf16[256,2048]{1,0:T(8,128)(2,1)}, bf16[256,2048]{1,0:T(8,128)(2,1)}, u32[]{:S(2)}, u32[]{:S(2)}) %collective-permute-start.15) | collective-permute-done | bytes 1048608 | tf_op jit(solution)/shard_map/ppermute | solution.py:169
  142.9 8.9 %convolution_convert_fusion = bf16[256,3328]{1,0:T(8,128)(2,1)S(1)} fusion(bf16[256,2048]{1,0:T(8,128)(2,1)} %collective-permute-done.15, bf16[2048,3328]{1,0:T(8,128)(2,1)} %constant_dynamic-update-slice_fusion), kind=kOutput, calls=%fused_computation.7 | convolution fusion | flops 3490512896 | bytes 16384000 | tf_op jit(solution)/shard_map/dot_general | solution.py:100
  153.6 2.1 collective-permute-start.2
  155.7 10.1 %convolution_convert_fusion.1 = bf16[256,3328]{1,0:T(8,128)(2,1)} fusion(bf16[256,2048]{1,0:T(8,128)(2,1)} %collective-permute-done.10, bf16[2048,3328]{1,0:T(8,128)(2,1)} %constant_dynamic-update-slice_fusion), kind=kOutput, calls=%fused_computation.8 | convolution fusion | flops 3490512896 | bytes 16384000 | tf_op jit(solution)/shard_map/dot_general | solution.py:100
  165.8 3.6 %all-to-all-start.6 = ((bf16[4,64,3328]{2,1,0:T(8,128)(2,1)}), bf16[4,64,3328]{2,1,0:T(8,128)(2,1)S(1)}, u32[]{:S(2)}, u32[]{:S(2)}) async-start(bf16[4,64,3328]{2,1,0:T(8,128)(2,1)} %bitcast.135), calls=%async_computation.6 | async-start | bytes 3407872 | tf_op jit(solution)/shard_map/all_to_all | solution.py:131
  169.4 8.6 %collective-permute-done.2 = bf16[32,3328]{1,0:T(8,128)(2,1)S(1)} collective-permute-done((bf16[32,3328]{1,0:T(8,128)(2,1)S(1)}, bf16[32,3328]{1,0:T(8,128)(2,1)S(1)}, u32[]{:S(2)}, u32[]{:S(2)}) %collective-permute-start.2) | collective-permute-done | bytes 213024 | tf_op jit(solution)/shard_map/ppermute | solution.py:112
  179.4 2.5 add_convert_fusion.1
  182.0 8.4 %all-to-all-done.6 = bf16[4,64,3328]{2,1,0:T(8,128)(2,1)S(1)} async-done(((bf16[4,64,3328]{2,1,0:T(8,128)(2,1)}), bf16[4,64,3328]{2,1,0:T(8,128)(2,1)S(1)}, u32[]{:S(2)}, u32[]{:S(2)}) %all-to-all-start.6) | async-done | bytes 1703968 | tf_op jit(solution)/shard_map/all_to_all | solution.py:131
  190.4 4.2 %all-to-all-start.4 = ((bf16[4,32,3328]{2,1,0:T(8,128)(2,1)}), bf16[4,32,3328]{2,1,0:T(8,128)(2,1)}, u32[]{:S(2)}, u32[]{:S(2)}) async-start(bf16[4,32,3328]{2,1,0:T(8,128)(2,1)} %bitcast.128), calls=%async_computation.4 | async-start | bytes 1703936 | tf_op jit(solution)/shard_map/all_to_all | solution.py:131
  196.1 2.3 add_convert_fusion
  198.4 2.6 collective-permute-done.11
  201.1 4.6 %all-to-all-done.4 = bf16[4,32,3328]{2,1,0:T(8,128)(2,1)} async-done(((bf16[4,32,3328]{2,1,0:T(8,128)(2,1)}), bf16[4,32,3328]{2,1,0:T(8,128)(2,1)}, u32[]{:S(2)}, u32[]{:S(2)}) %all-to-all-start.4) | async-done | bytes 852000 | tf_op jit(solution)/shard_map/all_to_all | solution.py:131
  205.7 3.5 %all-to-all-start.8 = ((bf16[4,32,3328]{2,1,0:T(8,128)(2,1)}), bf16[4,32,3328]{2,1,0:T(8,128)(2,1)S(1)}, u32[]{:S(2)}, u32[]{:S(2)}) async-start(bf16[4,32,3328]{2,1,0:T(8,128)(2,1)} %bitcast.26), calls=%async_computation.8 | async-start | bytes 1703936 | tf_op jit(solution)/shard_map/all_to_all | solution.py:131
  211.4 7.5 %all-to-all-done.8 = bf16[4,32,3328]{2,1,0:T(8,128)(2,1)S(1)} async-done(((bf16[4,32,3328]{2,1,0:T(8,128)(2,1)}), bf16[4,32,3328]{2,1,0:T(8,128)(2,1)S(1)}, u32[]{:S(2)}, u32[]{:S(2)}) %all-to-all-start.8) | async-done | bytes 852000 | tf_op jit(solution)/shard_map/all_to_all | solution.py:131
  219.8 3.5 %all-to-all-start.5 = ((bf16[4,32,1664]{2,1,0:T(8,128)(2,1)}), bf16[4,32,1664]{2,1,0:T(8,128)(2,1)S(1)}, u32[]{:S(2)}, u32[]{:S(2)}) async-start(bf16[4,32,1664]{2,1,0:T(8,128)(2,1)} %broadcast_in_dim.35), calls=%async_computation.5 | async-start | bytes 851968 | tf_op jit(solution)/shard_map/all_to_all | solution.py:137
  223.4 7.3 %all-to-all-done.5 = bf16[4,32,1664]{2,1,0:T(8,128)(2,1)S(1)} async-done(((bf16[4,32,1664]{2,1,0:T(8,128)(2,1)}), bf16[4,32,1664]{2,1,0:T(8,128)(2,1)S(1)}, u32[]{:S(2)}, u32[]{:S(2)}) %all-to-all-start.5) | async-done | bytes 426016 | tf_op jit(solution)/shard_map/all_to_all | solution.py:137
  231.6 3.5 %all-to-all-start.9 = ((bf16[4,32,1664]{2,1,0:T(8,128)(2,1)}), bf16[4,32,1664]{2,1,0:T(8,128)(2,1)S(1)}, u32[]{:S(2)}, u32[]{:S(2)}) async-start(bf16[4,32,1664]{2,1,0:T(8,128)(2,1)} %broadcast_in_dim.37), calls=%async_computation.9 | async-start | bytes 851968 | tf_op jit(solution)/shard_map/all_to_all | solution.py:137
  236.8 5.7 %all-to-all-done.9 = bf16[4,32,1664]{2,1,0:T(8,128)(2,1)S(1)} async-done(((bf16[4,32,1664]{2,1,0:T(8,128)(2,1)}), bf16[4,32,1664]{2,1,0:T(8,128)(2,1)S(1)}, u32[]{:S(2)}, u32[]{:S(2)}) %all-to-all-start.9) | async-done | bytes 426016 | tf_op jit(solution)/shard_map/all_to_all | solution.py:137
  244.5 3.5 %all-to-all-start.7 = ((bf16[4,64,1664]{2,1,0:T(8,128)(2,1)}), bf16[4,64,1664]{2,1,0:T(8,128)(2,1)S(1)}, u32[]{:S(2)}, u32[]{:S(2)}) async-start(bf16[4,64,1664]{2,1,0:T(8,128)(2,1)} %broadcast_in_dim.36), calls=%async_computation.7 | async-start | bytes 1703936 | tf_op jit(solution)/shard_map/all_to_all | solution.py:137
  248.0 3.7 %collective-permute-done.17 = bf16[128,1664]{1,0:T(8,128)(2,1)S(1)} collective-permute-done((bf16[128,1664]{1,0:T(8,128)(2,1)S(1)}, bf16[128,1664]{1,0:T(8,128)(2,1)S(1)}, u32[]{:S(2)}, u32[]{:S(2)}) %collective-permute-start.17) | collective-permute-done | bytes 426016 | tf_op jit(solution)/shard_map/ppermute | solution.py:112
  252.0 5.3 %fusion.30 = f32[256,2048]{1,0:T(8,128)S(1)} fusion(bf16[1664,2048]{1,0:T(8,128)(2,1)} %param.21, bf16[128,1664]{1,0:T(8,128)(2,1)S(1)} %get-tuple-element.21, bf16[128,1664]{1,0:T(8,128)(2,1)S(1)} %get-tuple-element.22), kind=kOutput, calls=%fused_computation.46 | convolution fusion | flops 1746534400 | bytes 9764864 | tf_op jit(solution)/shard_map/dot_general | solution.py:100
  258.8 2.1 fusion.34
  263.4 3.5 %all-to-all-start.3 = ((bf16[4,64,1664]{2,1,0:T(8,128)(2,1)}), bf16[4,64,1664]{2,1,0:T(8,128)(2,1)S(1)}, u32[]{:S(2)}, u32[]{:S(2)}) async-start(bf16[4,64,1664]{2,1,0:T(8,128)(2,1)} %broadcast_in_dim.34), calls=%async_computation.3 | async-start | bytes 1703936 | tf_op jit(solution)/shard_map/all_to_all | solution.py:137
  266.9 5.0 %fusion.3 = f32[2,2,64,2048]{3,2,0,1:T(8,128)S(1)} fusion(bf16[1664,2048]{1,0:T(8,128)(2,1)} %param.21, bf16[2,2,64,1664]{3,2,1,0:T(8,128)(2,1)S(1)} %bitcast.143), kind=kOutput, calls=%fused_computation.5 | convolution fusion | flops 1744830464 | bytes 9764864 | tf_op jit(solution)/shard_map/dot_general | solution.py:100
  273.9 6.9 %all-to-all-done.3 = bf16[4,64,1664]{2,1,0:T(8,128)(2,1)S(1)} async-done(((bf16[4,64,1664]{2,1,0:T(8,128)(2,1)}), bf16[4,64,1664]{2,1,0:T(8,128)(2,1)S(1)}, u32[]{:S(2)}, u32[]{:S(2)}) %all-to-all-start.3) | async-done | bytes 852000 | tf_op jit(solution)/shard_map/all_to_all | solution.py:137
  280.8 5.1 %fusion.1 = f32[2,2,64,2048]{3,2,1,0:T(8,128)S(1)} fusion(bf16[2,2,64,1664]{3,2,1,0:T(8,128)(2,1)S(1)} %bitcast.144, bf16[1664,2048]{1,0:T(8,128)(2,1)} %param.21), kind=kOutput, calls=%fused_computation.3 | convolution fusion | flops 1744830464 | bytes 9764864 | tf_op jit(solution)/shard_map/dot_general | solution.py:100
  287.8 2.0 collective-permute-start.14
  291.8 10.4 %collective-permute-done.9 = bf16[2,64,2048]{2,1,0:T(8,128)(2,1)S(1)} collective-permute-done((bf16[2,64,2048]{2,1,0:T(8,128)(2,1)S(1)}, bf16[2,64,2048]{2,1,0:T(8,128)(2,1)S(1)}, u32[]{:S(2)}, u32[]{:S(2)}) %collective-permute-start.9) | collective-permute-done | bytes 524320 | tf_op jit(solution)/shard_map/ppermute | solution.py:175
  302.2 12.4 %collective-permute-done.14 = bf16[2,64,2048]{2,1,0:T(8,128)(2,1)S(1)} collective-permute-done((bf16[2,64,2048]{2,1,0:T(8,128)(2,1)S(1)}, bf16[2,64,2048]{2,1,0:T(8,128)(2,1)S(1)}, u32[]{:S(2)}, u32[]{:S(2)}) %collective-permute-start.14) | collective-permute-done | bytes 524320 | tf_op jit(solution)/shard_map/ppermute | solution.py:175
  315.0 2.4 collective-permute-start.20
  317.5 7.0 %collective-permute-done.20 = bf16[64,2048]{1,0:T(8,128)(2,1)S(1)} collective-permute-done((bf16[64,2048]{1,0:T(8,128)(2,1)S(1)}, bf16[64,2048]{1,0:T(8,128)(2,1)S(1)}, u32[]{:S(2)}, u32[]{:S(2)}) %collective-permute-start.20) | collective-permute-done | bytes 262176 | tf_op jit(solution)/shard_map/ppermute | solution.py:112
  (130 shorter events, 38.1 us)
Async XLA Ops:
  0.0 1.4 copy-start
  3.4 8.2 %copy-start.14 = (s32[8,8]{1,0:T(8,128)S(1)}, s32[8,8]{1,0:T(8,128)}, u32[]{:S(2)}) copy-start(s32[8,8]{1,0:T(8,128)} %param.16) | copy-start | bytes 772
  3.4 8.3 %copy-start.16 = (s32[8]{0:T(128)S(1)}, s32[8]{0:T(128)}, u32[]{:S(2)}) copy-start(s32[8]{0:T(128)} %param.17) | copy-start | bytes 100
  3.4 35.2 %all-to-all-start = ((bf16[32,2,16,1024]{3,2,1,0:T(8,128)(2,1)}), bf16[32,2,16,1024]{3,2,1,0:T(8,128)(2,1)S(1)}, u32[]{:S(2)}, u32[]{:S(2)}) async-start(bf16[32,2,16,1024]{3,2,1,0:T(8,128)(2,1)} %gather_fusion), calls=%async_computation | async-start | bytes 4194304 | tf_op jit(solution)/shard_map/all_to_all | solution.py:35
  53.4 1.9 copy-start.13
  56.8 12.1 %all-to-all-start.1 = ((bf16[8,8,2176]{2,0,1:T(8,128)(2,1)}), bf16[8,8,2176]{2,0,1:T(8,128)(2,1)S(1)}, u32[]{:S(2)}, u32[]{:S(2)}) async-start(bf16[8,8,2176]{2,0,1:T(8,128)(2,1)} %pad_maximum_fusion.3), calls=%async_computation.1 | async-start | bytes 557056 | tf_op jit(solution)/shard_map/all_to_all | solution.py:68
  69.3 6.5 %collective-permute-start = (bf16[64,2048]{1,0:T(8,128)(2,1)S(1)}, bf16[64,2048]{1,0:T(8,128)(2,1)S(1)}, u32[]{:S(2)}, u32[]{:S(2)}) collective-permute-start(bf16[64,2048]{1,0:T(8,128)(2,1)S(1)} %fusion.40), channel_id=1, source_target_pairs={{0,8},{8,0},{1,9},{9,1},{2,10},{10,2},{3,11},{11,3},{4,12},{12,4},... | collective-permute-start | bytes 786440 | tf_op jit(solution)/shard_map/ppermute | solution.py:112
  75.8 15.9 %collective-permute-start.1 = (bf16[128,2048]{1,0:T(8,128)(2,1)S(1)}, bf16[128,2048]{1,0:T(8,128)(2,1)S(1)}, u32[]{:S(2)}, u32[]{:S(2)}) collective-permute-start(bf16[128,2048]{1,0:T(8,128)(2,1)S(1)} %pad_maximum_fusion.2), channel_id=1, source_target_pairs={{0,16},{16,0},{1,17},{17,1},{2,18},{18,2},{3,19},{19,3},{4,20},{20... | collective-permute-start | bytes 1572872 | tf_op jit(solution)/shard_map/ppermute | solution.py:112
  92.8 26.4 %collective-permute-start.5 = (bf16[256,2048]{1,0:T(8,128)(2,1)}, bf16[256,2048]{1,0:T(8,128)(2,1)}, u32[]{:S(2)}, u32[]{:S(2)}) collective-permute-start(bf16[256,2048]{1,0:T(8,128)(2,1)} %pad_maximum_fusion.1), channel_id=1, source_target_pairs={{32,0},{64,32},{96,64},{0,96},{33,1},{65,33},{97,65},{1,97},{34,2}... | collective-permute-start | bytes 3145736 | tf_op jit(solution)/shard_map/ppermute | solution.py:169
  94.4 48.5 %collective-permute-start.15 = (bf16[256,2048]{1,0:T(8,128)(2,1)}, bf16[256,2048]{1,0:T(8,128)(2,1)}, u32[]{:S(2)}, u32[]{:S(2)}) collective-permute-start(bf16[256,2048]{1,0:T(8,128)(2,1)} %pad_maximum_fusion.1), channel_id=1, source_target_pairs={{64,0},{96,32},{0,64},{32,96},{65,1},{97,33},{1,65},{33,97},{66,2}... | collective-permute-start | bytes 3145736 | tf_op jit(solution)/shard_map/ppermute | solution.py:169
  97.1 58.6 %collective-permute-start.10 = (bf16[256,2048]{1,0:T(8,128)(2,1)}, bf16[256,2048]{1,0:T(8,128)(2,1)}, u32[]{:S(2)}, u32[]{:S(2)}) collective-permute-start(bf16[256,2048]{1,0:T(8,128)(2,1)} %pad_maximum_fusion.1), channel_id=1, source_target_pairs={{96,0},{0,32},{32,64},{64,96},{97,1},{1,33},{33,65},{65,97},{98,2}... | collective-permute-start | bytes 3145736 | tf_op jit(solution)/shard_map/ppermute | solution.py:169
  107.7 45.6 %all-to-all-start.2 = ((bf16[4,64,3328]{2,1,0:T(8,128)(2,1)}), bf16[4,64,3328]{2,1,0:T(8,128)(2,1)S(1)}, u32[]{:S(2)}, u32[]{:S(2)}) async-start(bf16[4,64,3328]{2,1,0:T(8,128)(2,1)} %bitcast.134), calls=%async_computation.2 | async-start | bytes 3407872 | tf_op jit(solution)/shard_map/all_to_all | solution.py:131
  128.1 2.2 copy-start.5
  129.1 50.3 %collective-permute-start.6 = (bf16[128,3328]{1,0:T(8,128)(2,1)}, bf16[128,3328]{1,0:T(8,128)(2,1)}, u32[]{:S(2)}, u32[]{:S(2)}) collective-permute-start(bf16[128,3328]{1,0:T(8,128)(2,1)} %constant_dynamic-slice_fusion.1), channel_id=1, source_target_pairs={{0,4},{4,0},{1,5},{5,1},{2,6},{6,2},{3,7},{7,3},{8,12},{12,8},{9,1... | collective-permute-start | bytes 2555912 | tf_op jit(solution)/shard_map/ppermute | solution.py:112
  151.8 1.5 copy-start.3
  153.3 42.3 %collective-permute-start.16 = (bf16[128,3328]{1,0:T(8,128)(2,1)}, bf16[128,3328]{1,0:T(8,128)(2,1)}, u32[]{:S(2)}, u32[]{:S(2)}) collective-permute-start(bf16[128,3328]{1,0:T(8,128)(2,1)} %constant_dynamic-slice_fusion), channel_id=1, source_target_pairs={{0,4},{4,0},{1,5},{5,1},{2,6},{6,2},{3,7},{7,3},{8,12},{12,8},{9,1... | collective-permute-start | bytes 2555912 | tf_op jit(solution)/shard_map/ppermute | solution.py:112
  153.5 12.3 %copy-start.2 = (f32[64,3328]{1,0:T(8,128)}, f32[64,3328]{1,0:T(8,128)S(1)}, u32[]{:S(2)}) copy-start(f32[64,3328]{1,0:T(8,128)S(1)} %convert_reduce_fusion.1) | copy-start | bytes 2555908
  153.6 24.4 %collective-permute-start.2 = (bf16[32,3328]{1,0:T(8,128)(2,1)S(1)}, bf16[32,3328]{1,0:T(8,128)(2,1)S(1)}, u32[]{:S(2)}, u32[]{:S(2)}) collective-permute-start(bf16[32,3328]{1,0:T(8,128)(2,1)S(1)} %dynamic-slice_convert_fusion.1), channel_id=1, source_target_pairs={{0,4},{4,0},{1,5},{5,1},{2,6},{6,2},{3,7},{7,3},{8,12},{12,8},{9,1... | collective-permute-start | bytes 638984 | tf_op jit(solution)/shard_map/ppermute | solution.py:112
  165.8 24.6 %all-to-all-start.6 = ((bf16[4,64,3328]{2,1,0:T(8,128)(2,1)}), bf16[4,64,3328]{2,1,0:T(8,128)(2,1)S(1)}, u32[]{:S(2)}, u32[]{:S(2)}) async-start(bf16[4,64,3328]{2,1,0:T(8,128)(2,1)} %bitcast.135), calls=%async_computation.6 | async-start | bytes 3407872 | tf_op jit(solution)/shard_map/all_to_all | solution.py:131
  179.1 56.0 %collective-permute-start.3 = (bf16[32,1664]{1,0:T(8,128)(2,1)S(1)}, bf16[32,1664]{1,0:T(8,128)(2,1)S(1)}, u32[]{:S(2)}, u32[]{:S(2)}) collective-permute-start(bf16[32,1664]{1,0:T(8,128)(2,1)S(1)} %fusion.54), channel_id=1, source_target_pairs={{0,4},{4,0},{1,5},{5,1},{2,6},{6,2},{3,7},{7,3},{8,12},{12,8},{9,1... | collective-permute-start | bytes 319496 | tf_op jit(solution)/shard_map/ppermute | solution.py:112
  190.4 15.3 %all-to-all-start.4 = ((bf16[4,32,3328]{2,1,0:T(8,128)(2,1)}), bf16[4,32,3328]{2,1,0:T(8,128)(2,1)}, u32[]{:S(2)}, u32[]{:S(2)}) async-start(bf16[4,32,3328]{2,1,0:T(8,128)(2,1)} %bitcast.128), calls=%async_computation.4 | async-start | bytes 1703936 | tf_op jit(solution)/shard_map/all_to_all | solution.py:131
  194.6 1.5 copy-start.4
  194.9 6.1 %collective-permute-start.11 = (bf16[32,3328]{1,0:T(8,128)(2,1)S(1)}, bf16[32,3328]{1,0:T(8,128)(2,1)S(1)}, u32[]{:S(2)}, u32[]{:S(2)}) collective-permute-start(bf16[32,3328]{1,0:T(8,128)(2,1)S(1)} %dynamic-slice_convert_fusion), channel_id=1, source_target_pairs={{0,4},{4,0},{1,5},{5,1},{2,6},{6,2},{3,7},{7,3},{8,12},{12,8},{9,1... | collective-permute-start | bytes 638984 | tf_op jit(solution)/shard_map/ppermute | solution.py:112
  205.7 13.3 %all-to-all-start.8 = ((bf16[4,32,3328]{2,1,0:T(8,128)(2,1)}), bf16[4,32,3328]{2,1,0:T(8,128)(2,1)S(1)}, u32[]{:S(2)}, u32[]{:S(2)}) async-start(bf16[4,32,3328]{2,1,0:T(8,128)(2,1)} %bitcast.26), calls=%async_computation.8 | async-start | bytes 1703936 | tf_op jit(solution)/shard_map/all_to_all | solution.py:131
  209.2 25.8 %collective-permute-start.12 = (bf16[32,1664]{1,0:T(8,128)(2,1)S(1)}, bf16[32,1664]{1,0:T(8,128)(2,1)S(1)}, u32[]{:S(2)}, u32[]{:S(2)}) collective-permute-start(bf16[32,1664]{1,0:T(8,128)(2,1)S(1)} %fusion.52), channel_id=1, source_target_pairs={{0,4},{4,0},{1,5},{5,1},{2,6},{6,2},{3,7},{7,3},{8,12},{12,8},{9,1... | collective-permute-start | bytes 319496 | tf_op jit(solution)/shard_map/ppermute | solution.py:112
  219.8 11.0 %all-to-all-start.5 = ((bf16[4,32,1664]{2,1,0:T(8,128)(2,1)}), bf16[4,32,1664]{2,1,0:T(8,128)(2,1)S(1)}, u32[]{:S(2)}, u32[]{:S(2)}) async-start(bf16[4,32,1664]{2,1,0:T(8,128)(2,1)} %broadcast_in_dim.35), calls=%async_computation.5 | async-start | bytes 851968 | tf_op jit(solution)/shard_map/all_to_all | solution.py:137
  231.6 11.0 %all-to-all-start.9 = ((bf16[4,32,1664]{2,1,0:T(8,128)(2,1)}), bf16[4,32,1664]{2,1,0:T(8,128)(2,1)S(1)}, u32[]{:S(2)}, u32[]{:S(2)}) async-start(bf16[4,32,1664]{2,1,0:T(8,128)(2,1)} %broadcast_in_dim.37), calls=%async_computation.9 | async-start | bytes 851968 | tf_op jit(solution)/shard_map/all_to_all | solution.py:137
  235.9 12.1 %copy-start.12 = (bf16[32,1664]{1,0:T(8,128)(2,1)S(1)}, bf16[32,1664]{1,0:T(8,128)(2,1)}, u32[]{:S(2)}) copy-start(bf16[32,1664]{1,0:T(8,128)(2,1)} %get-tuple-element.24) | copy-start | bytes 319492
  235.9 12.2 %collective-permute-start.7 = (bf16[128,1664]{1,0:T(8,128)(2,1)S(1)}, bf16[128,1664]{1,0:T(8,128)(2,1)S(1)}, u32[]{:S(2)}, u32[]{:S(2)}) collective-permute-start(bf16[128,1664]{1,0:T(8,128)(2,1)S(1)} %bitcast.136), channel_id=1, source_target_pairs={{0,4},{4,0},{1,5},{5,1},{2,6},{6,2},{3,7},{7,3},{8,12},{12,8},{9,1... | collective-permute-start | bytes 1277960 | tf_op jit(solution)/shard_map/ppermute | solution.py:112
  242.6 9.2 %collective-permute-start.17 = (bf16[128,1664]{1,0:T(8,128)(2,1)S(1)}, bf16[128,1664]{1,0:T(8,128)(2,1)S(1)}, u32[]{:S(2)}, u32[]{:S(2)}) collective-permute-start(bf16[128,1664]{1,0:T(8,128)(2,1)S(1)} %bitcast.137), channel_id=1, source_target_pairs={{0,4},{4,0},{1,5},{5,1},{2,6},{6,2},{3,7},{7,3},{8,12},{12,8},{9,1... | collective-permute-start | bytes 1277960 | tf_op jit(solution)/shard_map/ppermute | solution.py:112
  244.5 17.9 %all-to-all-start.7 = ((bf16[4,64,1664]{2,1,0:T(8,128)(2,1)}), bf16[4,64,1664]{2,1,0:T(8,128)(2,1)S(1)}, u32[]{:S(2)}, u32[]{:S(2)}) async-start(bf16[4,64,1664]{2,1,0:T(8,128)(2,1)} %broadcast_in_dim.36), calls=%async_computation.7 | async-start | bytes 1703936 | tf_op jit(solution)/shard_map/all_to_all | solution.py:137
  251.8 7.1 %slice-start = ((s8[6815744]{0:T(1024)(128)(4,1)}), s8[4194304]{0:T(1024)(128)(4,1)S(1)}, s32[]{:S(2)}) async-start(s8[6815744]{0:T(1024)(128)(4,1)} %bitcast.146), calls=%async_computation.10 | async-start | bytes 8388608
  252.0 6.8 %slice-start.1 = ((s8[6815744]{0:T(1024)(128)(4,1)}), s8[2621440]{0:T(1024)(128)(4,1)S(1)}, s32[]{:S(2)}) async-start(s8[6815744]{0:T(1024)(128)(4,1)} %bitcast.146), calls=%async_computation.11 | async-start | bytes 5242880
  257.3 1.5 copy-start.8
  258.3 27.8 %collective-permute-start.8 = (bf16[2,64,2048]{2,1,0:T(8,128)(2,1)}, bf16[2,64,2048]{2,1,0:T(8,128)(2,1)}, u32[]{:S(2)}, u32[]{:S(2)}) collective-permute-start(bf16[2,64,2048]{2,1,0:T(8,128)(2,1)} %fusion.44), channel_id=1, source_target_pairs={{0,8},{8,0},{1,9},{9,1},{2,10},{10,2},{3,11},{11,3},{4,12},{12,4},... | collective-permute-start | bytes 1572872 | tf_op jit(solution)/shard_map/ppermute | solution.py:112
  262.3 27.4 %collective-permute-start.18 = (bf16[2,64,2048]{2,1,0:T(8,128)(2,1)S(1)}, bf16[2,64,2048]{2,1,0:T(8,128)(2,1)}, u32[]{:S(2)}, u32[]{:S(2)}) collective-permute-start(bf16[2,64,2048]{2,1,0:T(8,128)(2,1)S(1)} %fusion.45), channel_id=1, source_target_pairs={{0,8},{8,0},{1,9},{9,1},{2,10},{10,2},{3,11},{11,3},{4,12},{12,4},... | collective-permute-start | bytes 1572872 | tf_op jit(solution)/shard_map/ppermute | solution.py:112
  263.4 17.4 %all-to-all-start.3 = ((bf16[4,64,1664]{2,1,0:T(8,128)(2,1)}), bf16[4,64,1664]{2,1,0:T(8,128)(2,1)S(1)}, u32[]{:S(2)}, u32[]{:S(2)}) async-start(bf16[4,64,1664]{2,1,0:T(8,128)(2,1)} %broadcast_in_dim.34), calls=%async_computation.3 | async-start | bytes 1703936 | tf_op jit(solution)/shard_map/all_to_all | solution.py:137
  271.9 1.4 copy-start.10
  273.3 14.2 %collective-permute-start.13 = (bf16[2,64,2048]{2,1,0:T(8,128)(2,1)S(1)}, bf16[2,64,2048]{2,1,0:T(8,128)(2,1)S(1)}, u32[]{:S(2)}, u32[]{:S(2)}) collective-permute-start(bf16[2,64,2048]{2,1,0:T(8,128)(2,1)S(1)} %fusion.43), channel_id=1, source_target_pairs={{0,8},{8,0},{1,9},{9,1},{2,10},{10,2},{3,11},{11,3},{4,12},{12,4},... | collective-permute-start | bytes 1572872 | tf_op jit(solution)/shard_map/ppermute | solution.py:112
  280.8 5.3 %copy-start.9 = (f32[256,2048]{1,0:T(8,128)S(1)}, f32[256,2048]{1,0:T(8,128)}, u32[]{:S(2)}) copy-start(f32[256,2048]{1,0:T(8,128)} %copy-done.8) | copy-start | bytes 6291460
  285.9 1.7 copy-start.11
  286.0 3.7 %copy-start.7 = (f32[256,2048]{1,0:T(8,128)S(1)}, f32[256,2048]{1,0:T(8,128)}, u32[]{:S(2)}) copy-start(f32[256,2048]{1,0:T(8,128)} %copy-done.6) | copy-start | bytes 6291460
  286.0 5.8 %collective-permute-start.4 = (bf16[2,64,2048]{2,1,0:T(8,128)(2,1)S(1)}, bf16[2,64,2048]{2,1,0:T(8,128)(2,1)S(1)}, u32[]{:S(2)}, u32[]{:S(2)}) collective-permute-start(bf16[2,64,2048]{2,1,0:T(8,128)(2,1)S(1)} %fusion.42), channel_id=1, source_target_pairs={{0,8},{8,0},{1,9},{9,1},{2,10},{10,2},{3,11},{11,3},{4,12},{12,4},... | collective-permute-start | bytes 1572872 | tf_op jit(solution)/shard_map/ppermute | solution.py:112
  287.4 14.8 %collective-permute-start.9 = (bf16[2,64,2048]{2,1,0:T(8,128)(2,1)S(1)}, bf16[2,64,2048]{2,1,0:T(8,128)(2,1)S(1)}, u32[]{:S(2)}, u32[]{:S(2)}) collective-permute-start(bf16[2,64,2048]{2,1,0:T(8,128)(2,1)S(1)} %fusion.23), channel_id=1, source_target_pairs={{0,32},{32,64},{64,96},{96,0},{1,33},{33,65},{65,97},{97,1},{2,34}... | collective-permute-start | bytes 1572872 | tf_op jit(solution)/shard_map/ppermute | solution.py:175
  287.8 26.8 %collective-permute-start.14 = (bf16[2,64,2048]{2,1,0:T(8,128)(2,1)S(1)}, bf16[2,64,2048]{2,1,0:T(8,128)(2,1)S(1)}, u32[]{:S(2)}, u32[]{:S(2)}) collective-permute-start(bf16[2,64,2048]{2,1,0:T(8,128)(2,1)S(1)} %fusion.25), channel_id=1, source_target_pairs={{0,96},{32,0},{64,32},{96,64},{1,97},{33,1},{65,33},{97,65},{2,98}... | collective-permute-start | bytes 1572872 | tf_op jit(solution)/shard_map/ppermute | solution.py:175
  289.7 35.6 %copy-start.1 = (bf16[16,2,16,1024]{3,2,1,0:T(8,128)(2,1)S(1)}, bf16[16,2,16,1024]{3,2,1,0:T(8,128)(2,1)}, u32[]{:S(2)}) copy-start(bf16[16,2,16,1024]{3,2,1,0:T(8,128)(2,1)} %param.14) | copy-start | bytes 3145732
  291.0 23.6 %collective-permute-start.19 = (bf16[2,64,2048]{2,1,0:T(8,128)(2,1)S(1)}, bf16[2,64,2048]{2,1,0:T(8,128)(2,1)S(1)}, u32[]{:S(2)}, u32[]{:S(2)}) collective-permute-start(bf16[2,64,2048]{2,1,0:T(8,128)(2,1)S(1)} %fusion.21), channel_id=1, source_target_pairs={{0,64},{32,96},{64,0},{96,32},{1,65},{33,97},{65,1},{97,33},{2,66}... | collective-permute-start | bytes 1572872 | tf_op jit(solution)/shard_map/ppermute | solution.py:175
  315.0 9.5 %collective-permute-start.20 = (bf16[64,2048]{1,0:T(8,128)(2,1)S(1)}, bf16[64,2048]{1,0:T(8,128)(2,1)S(1)}, u32[]{:S(2)}, u32[]{:S(2)}) collective-permute-start(bf16[64,2048]{1,0:T(8,128)(2,1)S(1)} %fusion.48), channel_id=1, source_target_pairs={{0,16},{16,0},{1,17},{17,1},{2,18},{18,2},{3,19},{19,3},{4,20},{20... | collective-permute-start | bytes 786440 | tf_op jit(solution)/shard_map/ppermute | solution.py:112
  (2 other events, 2.3 us)

commit v2 on v1

v2 whole, which is shorter than its diff:
```python
import functools

import jax
import jax.numpy as jnp
from jax import lax
from jax.experimental import pallas as pl
from jax.experimental.pallas import tpu as pltpu
from jax.sharding import Mesh, PartitionSpec as P

HD = 128
KVH = 8
PAGE = 16
CAP = 2
GX = ("y", "zh", "c")
GY = ("zl", "x")
CHIPS = ("y", "zh")
SWAP = [(0, 1), (1, 0)]


def attend_kernel(table, context, queries, pool, arrived, _, out, store, sems):
    row_count, blocks = table.shape
    resident = pool.shape[0]
    heads = queries.shape[1] // KVH
    span = blocks * PAGE

    @pl.loop(0, row_count)
    def _(t):
        for i in range(blocks):
            page = table[t, i]
            place = store.at[t, :, pl.ds(i * PAGE, PAGE)]

            @pl.when(page < resident)
            def _():
                pltpu.make_async_copy(pool.at[page], place, sems.at[t]).start()

            @pl.when(page >= resident)
            def _():
                pltpu.make_async_copy(arrived.at[page - resident], place, sems.at[t]).start()

    @pl.loop(0, row_count)
    def _(t):
        pltpu.make_async_copy(store.at[t], store.at[t], sems.at[t]).wait()
        scores = jnp.concatenate(
            [
                lax.dot_general(
                    queries[t, k * heads : (k + 1) * heads, :],
                    store[t, 0, :, k * HD : (k + 1) * HD],
                    (((1,), (1,)), ((), ())),
                    preferred_element_type=jnp.float32,
                )
                for k in range(KVH)
            ],
            axis=0,
        ) * (1.0 / HD**0.5)
        visible = lax.broadcasted_iota(jnp.int32, scores.shape, 1) < context[t]
        scores = jnp.where(visible, scores, jnp.float32(-1e30))
        weights = jnp.exp(scores - jnp.max(scores, axis=1, keepdims=True))
        probs = narrow(weights / jnp.sum(weights, axis=1, keepdims=True))
        for k in range(KVH):
            rows = slice(k * heads, (k + 1) * heads)
            out[t, rows, :] = dot(probs[rows], store[t, 1, :, k * HD : (k + 1) * HD])


def attend(tokens, queries, page_pool, new_pages, page_table, block_table, context, after):
    row_count, model_width = tokens.shape
    area_size = lax.axis_size(GX) * CAP
    send_slot = page_table[:, 0] * CAP + page_table[:, 1]
    holder = jnp.argmax(jnp.arange(area_size)[:, None] == send_slot[None, :], axis=1)
    arrived = lax.all_to_all(new_pages[holder], GX, split_axis=0, concat_axis=0, tiled=True)
    heads = model_width // HD
    span = block_table.shape[1] * PAGE
    smem, vmem, anywhere = (pl.BlockSpec(memory_space=m) for m in (pltpu.SMEM, pltpu.VMEM, pl.ANY))
    attended = pl.pallas_call(
        attend_kernel,
        name="attend",
        out_shape=jax.ShapeDtypeStruct((row_count, heads, HD), jnp.float32),
        in_specs=[smem, smem, vmem] + [anywhere] * 3,
        out_specs=vmem,
        scratch_shapes=[
            pltpu.VMEM((row_count, 2, span, KVH * HD), jnp.bfloat16),
            pltpu.SemaphoreType.DMA((row_count,)),
        ],
        cost_estimate=pl.CostEstimate(flops=2**27, bytes_accessed=2**23, transcendentals=2**17),
        compiler_params=pltpu.CompilerParams(vmem_limit_bytes=8 * 2**20),
    )(block_table, context, queries.reshape(row_count, heads, HD), page_pool, arrived, after)
    return narrow(wide(tokens) + attended.reshape(row_count, model_width))


def spread(mixed_rows, norm_gain):
    row_count, model_width = mixed_rows.shape
    parts = lax.axis_size(GY)
    width = model_width // parts
    mixed_wide = mixed_rows.astype(jnp.float32)
    scale = lax.rsqrt(jnp.mean(mixed_wide * mixed_wide, axis=-1, keepdims=True) + 1e-05)
    high = scale.astype(jnp.bfloat16)
    rest = scale - high.astype(jnp.float32)
    middle = rest.astype(jnp.bfloat16)
    low = (rest - middle.astype(jnp.float32)).astype(jnp.bfloat16)
    terms = jnp.concatenate([high, middle, low, jnp.zeros((row_count, 125), jnp.bfloat16)], axis=1)
    payload = jnp.concatenate(
        [
            mixed_rows.reshape(row_count, parts, width),
            jnp.broadcast_to(terms[:, None, :], (row_count, parts, 128)),
        ],
        axis=2,
    )
    block = lax.all_to_all(payload, GY, split_axis=1, concat_axis=0, tiled=True)
    block = block.reshape(row_count * parts, width + 128)
    resid = block[:, :width].astype(jnp.float32)
    scale = (
        block[:, width : width + 1].astype(jnp.float32)
        + block[:, width + 1 : width + 2].astype(jnp.float32)
        + block[:, width + 2 : width + 3].astype(jnp.float32)
    )
    gain = lax.dynamic_slice(norm_gain, (lax.axis_index(GY) * width,), (width,))
    return resid, (resid * scale * gain).astype(jnp.bfloat16)


def on_device(
    tokens,
    queries,
    page_pool,
    new_pages,
    page_table,
    block_table,
    context,
    norm_gain,
    gate_weight,
    up_weight,
    down_weight,
):
    gate_weight, up_weight, down_weight, mark = load(gate_weight, up_weight, down_weight)
    mixed_rows = attend(tokens, queries, page_pool, new_pages, page_table, block_table, context, mark)
    resid, normed_block = spread(mixed_rows, norm_gain)

    return feed_forward(resid, normed_block, gate_weight, up_weight, down_weight)


def dot(a, b):
    return jnp.dot(a, b, preferred_element_type=jnp.float32)


def wide(a):
    return a.astype(jnp.float32)


def narrow(a):
    return a.astype(jnp.bfloat16)


def swap(a, axis):
    return lax.ppermute(a, axis, [(0, 1), (1, 0)])


def send(a, axis, shift):
    return lax.ppermute(a, axis, [(i, (i + shift) % 4) for i in range(4)])


def call(kernel, name, outs, *operands, after=()):
    count = len(operands)
    vmem, anywhere = pl.BlockSpec(memory_space=pltpu.VMEM), pl.BlockSpec(memory_space=pl.ANY)
    return pl.pallas_call(
        lambda *refs: kernel(*refs[:count], *refs[count + len(after) :]),
        name=name,
        out_shape=[jax.ShapeDtypeStruct(shape, dtype) for shape, dtype in outs],
        in_specs=[vmem] * count + [anywhere] * len(after),
        out_specs=[vmem] * len(outs),
        cost_estimate=pl.CostEstimate(flops=2**34, bytes_accessed=1024, transcendentals=0),
        compiler_params=pltpu.CompilerParams(vmem_limit_bytes=8 * 2**20),
    )(*operands, *after)


def load_kernel(*refs):
    mark, sems = refs[-2:]
    count = len(refs) // 2 - 1
    mark[...] = jnp.zeros_like(mark)
    copies = [pltpu.make_async_copy(refs[i], refs[count + i], sems.at[i]) for i in range(count)]
    for copy in copies:
        copy.start()
    for copy in copies:
        copy.wait()


def load(*weights):
    return pl.pallas_call(
        load_kernel,
        name="load",
        out_shape=[pltpu.VMEM(w.shape, w.dtype) for w in weights] + [jax.ShapeDtypeStruct((8, 128), jnp.float32)],
        in_specs=[pl.BlockSpec(memory_space=pltpu.HBM)] * len(weights),
        out_specs=[pl.BlockSpec(memory_space=pltpu.VMEM)] * (len(weights) + 1),
        scratch_shapes=[pltpu.SemaphoreType.DMA((len(weights),))],
        cost_estimate=pl.CostEstimate(flops=0, bytes_accessed=2**25, transcendentals=0),
        compiler_params=pltpu.CompilerParams(vmem_limit_bytes=8 * 2**20),
    )(*weights)


def span(masks):
    names = [0]
    for mask in masks:
        names = names + [name ^ mask for name in names]
    return names


def exchange(a, mask):
    if mask == 4:
        return lax.ppermute(a, "zl", [(0, 1), (1, 0)])
    return lax.ppermute(a, "x", [(i, i ^ mask) for i in range(4)])


def up_kernel(masks, own, other, gate, up, keep, away):
    width = gate.shape[1]
    whole = width // 256 * 256
    kept = span(masks[1:])

    def put(columns, block):
        for h in range(2):
            for j in range(2):
                for d in range(4):
                    name, row = h * 4 + d, ((h * 2 + j) * 4 + d) * 16
                    out = keep if name in kept else away
                    place = kept.index(name if name in kept else name ^ masks[0]) * 32 + j * 16
                    out[place : place + 16, columns] = block[row : row + 16].astype(out.dtype)

    rows = jnp.concatenate([core[h * 64 : (h + 1) * 64, :] for h in range(2) for core in (own, other)], axis=0)

    @pl.loop(0, whole // 256)
    def _(i):
        start = pl.multiple_of(i * 256, 256)
        put(pl.ds(start, 256), dot(rows, gate[:, pl.ds(start, 256)]))
        put(pl.ds(pl.multiple_of(width + start, 128), 256), dot(rows, up[:, pl.ds(start, 256)]))

    last = dot(rows, jnp.concatenate([gate[:, whole:], up[:, whole:]], axis=1))
    put(pl.ds(whole, width - whole), last[:, : width - whole])
    put(pl.ds(width + whole, width - whole), last[:, width - whole :])


def add_kernel(masks, mine, came, keep, away):
    names, kept = span(masks), span(masks[1:])
    for out, flip in ((keep, 0), (away, masks[0])):
        for place, name in enumerate(kept):
            row = names.index(name ^ flip) * 32
            total = mine[row : row + 32, :] + wide(came[row : row + 32, :])
            out[place * 32 : (place + 1) * 32, :] = total.astype(out.dtype)


def hidden_kernel(mine, came, out):
    width = out.shape[1]

    def total(columns):
        return mine[:, columns] + wide(came[:, columns])

    gate = total(slice(0, width))
    out[...] = narrow(gate * (1.0 / (1.0 + jnp.exp(-gate))) * total(slice(width, 2 * width)))


def join_kernel(mine, came, out):
    rows = mine.shape[0]
    out[:rows, :] = mine[...]
    out[rows:, :] = came[...]


def down_kernel(masks, mine, came, weight, keep, away):
    names, rows = span(masks), []
    for h in range(2):
        for j in range(2):
            for d in range(4):
                half, place = divmod(names.index(h * 4 + d), 4)
                row = place * 32 + j * 16
                rows.append((mine, came)[half][row : row + 16, :])
    rows = jnp.concatenate(rows, axis=0)

    @pl.loop(0, weight.shape[1] // 256)
    def _(i):
        columns = pl.ds(pl.multiple_of(i * 256, 256), 256)
        block = dot(rows, weight[:, columns])
        for h in range(2):
            keep[h * 64 : (h + 1) * 64, columns] = block[h * 128 : h * 128 + 64]
            away[h * 64 : (h + 1) * 64, columns] = narrow(block[h * 128 + 64 : (h + 1) * 128])


def copy_kernel(piece, out):
    out[...] = piece[...]


def total_kernel(*refs):
    terms = [wide(ref[...]) for ref in refs[:-1]]
    refs[-1][...] = sum(terms[1:], terms[0])


def fold_kernel(keep, came, out):
    out[...] = (keep[...] + wide(came[...])).astype(out.dtype)


SHIFTS = (1, 3, 2, 0)
SUM_MASKS = ((4, 1, 3), (1, 4, 3), (3, 1, 4), (3, 4, 1))
GATHER_MASKS = ((4, 1, 3), (3, 4, 1), (1, 3, 4), (1, 3, 4))
ORDER = (
    "P3", "U3", "P0", "P1", "Q2", "U0", "U1", "P2", "A3", "U2", "A0", "A1",
    "B3", "B0", "A2", "B1", "S3", "S0", "S1", "J0", "B2", "J3", "J1", "K0",
    "S2", "K3", "K1", "J2", "D0", "K2", "D1", "F0", "D3", "F1", "D2", "F3",
    "F2",
)


def by_x(a):
    x = lax.axis_index("x")
    b = [a[k * 16 : (k + 1) * 16] for k in range(4)]
    odd = x % 2 == 1
    b = [jnp.where(odd, b[k ^ 1], b[k]) for k in range(4)]
    high = x // 2 == 1
    b = [jnp.where(high, b[k ^ 2], b[k]) for k in range(4)]
    return jnp.concatenate(b, axis=0)


def feed_forward(resid, normed_block, gate_weight, up_weight, down_weight):
    rows, width = normed_block.shape
    hidden_width = gate_weight.shape[1]
    z = lax.axis_index("zl")
    b16, f32 = jnp.bfloat16, jnp.float32
    normed_block = by_x(normed_block)
    near = swap(normed_block, "zh")
    pair = jnp.concatenate([jnp.where(z == 0, normed_block, near), jnp.where(z == 0, near, normed_block)], axis=0)
    pieces = [send(pair, "y", -shift) if shift % 2 else pair for shift in SHIFTS]
    state, parts = {}, {}
    last = ()

    def run(kernel, name, outs, *operands):
        nonlocal last
        outs = call(kernel, name, outs, *operands, after=last)
        last = (outs[0],)
        return outs

    def reduce(kernel, name, k, step, *operands):
        masks = SUM_MASKS[k][step:]
        part = (128 >> step, 2 * hidden_width)
        keep, away = run(functools.partial(kernel, masks), name, [(part, f32), (part, b16)], *operands)
        state[k] = [keep, exchange(away, masks[0])]

    def gather(kernel, name, k, step):
        (out,) = run(kernel, name, [((32 << step, hidden_width), b16)], *state[k])
        state[k] = [out, exchange(out, GATHER_MASKS[k][step])]

    for step in ORDER:
        kind, k = step[0], int(step[1])
        if kind == "Q":
            (piece,) = run(copy_kernel, "far", [((128, width), b16)], pair)
            pieces[k] = send(piece, "y", -SHIFTS[k])
        elif kind == "P":
            (piece,) = run(copy_kernel, "piece", [((128, width), b16)], pieces[k])
            state[k] = [piece, swap(piece, "c")]
        elif kind == "U":
            reduce(up_kernel, "up", k, 0, *state[k], gate_weight, up_weight)
        elif kind in "AB":
            reduce(add_kernel, "add", k, 1 + "AB".index(kind), *state[k])
        elif kind == "S":
            gather(hidden_kernel, "hidden", k, 0)
        elif kind in "JK":
            gather(join_kernel, "join", k, 1 + "JK".index(kind))
        elif kind == "D":
            part = (128, width)
            kernel = functools.partial(down_kernel, GATHER_MASKS[k])
            keep, away = run(kernel, "down", [(part, f32), (part, b16)], *state[k], down_weight)
            state[k] = [keep, swap(away, "c")]
        else:
            (part,) = run(fold_kernel, "fold", [((128, width), b16 if SHIFTS[k] else f32)], *state[k])
            parts[k] = send(part, "y", SHIFTS[k]) if SHIFTS[k] else part
    (total,) = run(total_kernel, "total", [((128, width), f32)], *parts.values())
    total = total.reshape(2, rows, width)
    mine = jnp.where(z == 0, total[0], total[1])
    theirs = jnp.where(z == 0, total[1], total[0])
    ffn_block = by_x(mine + wide(swap(narrow(theirs), "zh")))
    return narrow(resid + ffn_block)


def solution(mesh):
    fine = Mesh(mesh.devices.reshape(4, 2, 2, 2, 4), GX + GY)
    rows = P(GX + GY)
    return jax.shard_map(
        on_device,
        mesh=fine,
        in_specs=(rows,) * 7 + (P(), P(GY, GX), P(GY, GX), P(GX, GY)),
        out_specs=P(GX, GY),
        check_vma=False,
    )
```

time: 328 us -> 233 us (0.71)
  matrix products: 58.5 us -> 0 us
  Pallas kernels: 0 us -> 45.2 us
  waiting for transfers between devices: 147 us -> 112 us
  other arithmetic: 21.5 us -> 4.1 us
  local copies, waits for them, and re-layouts: 36.3 us -> 22.6 us
  starting transfers between devices: 61.4 us -> 48 us
    dot_general x10 -> x0, matrix products: 58.5 us -> none  [the longest x8 55.5 us: dot(): return jnp.dot(a, b, preferred_element_type=jnp.float32)]
    pallas_call x0 -> x40, Pallas kernels: none -> 45.2 us  [the longest x38 35.2 us: call(): pl.pallas_call(lambda *refs: kernel(*refs[:count], *refs[count + len(afte...]
    all_to_all x8 -> x0, waiting for transfers between devices: 40.5 us -> none  [the longest x4 20.5 us: x_sum(): lax.all_to_all(part.reshape(4, rows // 4, width), 'x', split_axis=0, conc...]
    ppermute x6 -> x30, waiting for transfers between devices: 43.1 us -> 81.8 us  [the longest x16 42.9 us: exchange(): return lax.ppermute(a, 'x', [(i, i ^ mask) for i in range(4)])]
    all_to_all x8 -> x0, starting transfers between devices: 28.9 us -> none  [the longest x4 15 us: x_sum(): lax.all_to_all(part.reshape(4, rows // 4, width), 'x', split_axis=0, conc...]
    ppermute x6 -> x30, starting transfers between devices: 7.59 us -> 28.7 us  [the longest x6 13.8 us: send(): return lax.ppermute(a, axis, [(i, (i + shift) % 4) for i in range(4)])]
    all_to_all x1, waiting for transfers between devices: 26.8 us -> 8.34 us  [attend(): lax.all_to_all(new_pages[holder], GX, split_axis=0, concat_axis=0, tiled=...]
    ppermute x15 -> x10, waiting for transfers between devices: 30 us -> 15.7 us  [swap(): return lax.ppermute(a, axis, [(0, 1), (1, 0)])]
  transfers between devices with their start and end apart: 31 -> 42, of which waited for: 17 -> 24; matrix products, arithmetic and copies ran while one was open for 27% -> 0% of each run, Pallas kernels for 0% -> 16%
where the time goes in v2:
time: 233 us
  waiting for transfers between devices  112 us (48%)
  starting transfers between devices  48 us (21%)
  Pallas kernels  45.2 us (19%)
  local copies, waits for them, and re-layouts  22.6 us (10%)
  other arithmetic  4.1 us (2%)
    ppermute x16, waiting for transfers between devices, exchange(): return lax.ppermute(a, 'x', [(i, i ^ mask) for i in range(4)])  42.9 us
    pallas_call x38, Pallas kernels, call(): pl.pallas_call(lambda *refs: kernel(*refs[:count], *refs[count + len(afte...  35.2 us
    ppermute x6, waiting for transfers between devices, send(): return lax.ppermute(a, axis, [(i, (i + shift) % 4) for i in range(4)])  31.7 us
    unnamed x43, local copies, waits for them, and re-layouts  19.5 us
    ppermute x10, waiting for transfers between devices, swap(): return lax.ppermute(a, axis, [(0, 1), (1, 0)])  15.7 us
    ppermute x6, starting transfers between devices, send(): return lax.ppermute(a, axis, [(i, (i + shift) % 4) for i in range(4)])  13.8 us
    pallas_call x1, Pallas kernels, attend(): pl.pallas_call(attend_kernel, name='attend', out_shape=jax.ShapeDtypeStru...  8.54 us
    all_to_all x1, waiting for transfers between devices, attend(): lax.all_to_all(new_pages[holder], GX, split_axis=0, concat_axis=0, tiled=...  8.34 us
  transfers between devices with their start and end apart: 42, of which 24 were waited for; matrix products, arithmetic and copies ran while one was open for 0% of the time, Pallas kernels for 16%

profile of v2, /device:TPU:24, one launch (start us, length us, event | category | flops | bytes accessed | tf_op | source)
XLA Modules:
  0.0 233.0 jit_solution(18050914493057083407)
XLA Ops:
  1.4 2.1 gather_fusion
  3.5 8.2 %all-to-all-start = ((bf16[32,2,16,1024]{3,2,1,0:T(8,128)(2,1)}), bf16[32,2,16,1024]{3,2,1,0:T(8,128)(2,1)S(1)}, u32[]{:S(2)}, u32[]{:S(2)}) async-start(bf16[32,2,16,1024]{3,2,1,0:T(8,128)(2,1)} %gather_fusion), calls=%async_computation | async-start | bytes 4194304 | tf_op jit(solution)/shard_map/all_to_all | solution.py:69
  11.8 2.9 %copy-done.2 = bf16[2048,1664]{1,0:T(8,128)(2,1)S(1)} copy-done((bf16[2048,1664]{1,0:T(8,128)(2,1)S(1)}, bf16[2048,1664]{1,0:T(8,128)(2,1)}, u32[]{:S(2)}) %copy-start.2) | copy-done | bytes 6815768
  14.7 2.9 %copy-done.3 = bf16[2048,1664]{1,0:T(8,128)(2,1)S(1)} copy-done((bf16[2048,1664]{1,0:T(8,128)(2,1)S(1)}, bf16[2048,1664]{1,0:T(8,128)(2,1)}, u32[]{:S(2)}) %copy-start.3) | copy-done | bytes 6815768
  17.6 2.9 %copy-done.4 = bf16[1664,2048]{1,0:T(8,128)(2,1)S(1)} copy-done((bf16[1664,2048]{1,0:T(8,128)(2,1)S(1)}, bf16[1664,2048]{1,0:T(8,128)(2,1)}, u32[]{:S(2)}) %copy-start.4) | copy-done | bytes 6815768
  22.0 2.7 %copy-done.8 = bf16[1664,2048]{1,0:T(8,128)(2,1)} copy-done((bf16[1664,2048]{1,0:T(8,128)(2,1)}, bf16[1664,2048]{1,0:T(8,128)(2,1)S(1)}, u32[]{:S(2)}) %copy-start.8) | copy-done | bytes 6815768
  24.7 2.8 %copy-done.9 = bf16[2048,1664]{1,0:T(8,128)(2,1)} copy-done((bf16[2048,1664]{1,0:T(8,128)(2,1)}, bf16[2048,1664]{1,0:T(8,128)(2,1)S(1)}, u32[]{:S(2)}) %copy-start.9) | copy-done | bytes 6815768
  27.6 2.8 %copy-done.10 = bf16[2048,1664]{1,0:T(8,128)(2,1)} copy-done((bf16[2048,1664]{1,0:T(8,128)(2,1)}, bf16[2048,1664]{1,0:T(8,128)(2,1)S(1)}, u32[]{:S(2)}) %copy-start.10) | copy-done | bytes 6815768
  30.3 8.3 %all-to-all-done.arrived = bf16[32,2,16,1024]{3,2,1,0:T(8,128)(2,1)S(1)} async-done(((bf16[32,2,16,1024]{3,2,1,0:T(8,128)(2,1)}), bf16[32,2,16,1024]{3,2,1,0:T(8,128)(2,1)S(1)}, u32[]{:S(2)}, u32[]{:S(2)}) %all-to-all-start) | async-done | bytes 2097184 | tf_op jit(solution)/shard_map/all_to_all | solution.py:69
  38.7 1.6 copy-done.5
  40.3 8.5 %attend.2 = f32[8,128,128]{2,1,0:T(8,128)S(1)} custom-call(s32[8,8]{1,0:T(8,128)S(1)} %copy-done.6, s32[8]{0:T(128)S(1)} %copy-done.7, bf16[8,128,128]{2,1,0:T(8,128)(2,1)S(1)} %bitcast.32, bf16[32,2,16,1024]{3,2,1,0:T(8,128)(2,1)S(1)} %copy-done.5, bf16[32,2,16,1024]{3,2,1,0:T(8,128)(2,1)S(1)} %all-to-all-done.arrived, f32[8,128]{1,0:T(8,128)S(1)} %get-tuple-element.43._), custom_call_target="tpu_custom_call" | custom-call | flops 134217728 | bytes 8388608 | tf_op jit(solution)/shard_map/attend/pallas_call | solution.py:73
  50.4 4.8 %all-to-all-start.1 = ((bf16[8,8,2176]{2,0,1:T(8,128)(2,1)}), bf16[8,8,2176]{2,0,1:T(8,128)(2,1)S(1)}, u32[]{:S(2)}, u32[]{:S(2)}) async-start(bf16[8,8,2176]{2,0,1:T(8,128)(2,1)} %pad_maximum_fusion.1), calls=%async_computation.1 | async-start | bytes 557056 | tf_op jit(solution)/shard_map/all_to_all | solution.py:107
  55.8 6.7 %all-to-all-done.1 = bf16[8,8,2176]{2,0,1:T(8,128)(2,1)S(1)} async-done(((bf16[8,8,2176]{2,0,1:T(8,128)(2,1)}), bf16[8,8,2176]{2,0,1:T(8,128)(2,1)S(1)}, u32[]{:S(2)}, u32[]{:S(2)}) %all-to-all-start.1) | async-done | bytes 278560 | tf_op jit(solution)/shard_map/all_to_all | solution.py:107
  62.9 1.6 collective-permute-start
  64.5 6.7 %collective-permute-done = bf16[64,2048]{1,0:T(8,128)(2,1)S(1)} collective-permute-done((bf16[64,2048]{1,0:T(8,128)(2,1)S(1)}, bf16[64,2048]{1,0:T(8,128)(2,1)S(1)}, u32[]{:S(2)}, u32[]{:S(2)}) %collective-permute-start) | collective-permute-done | bytes 262176 | tf_op jit(solution)/shard_map/ppermute | solution.py:152
  71.6 4.0 %collective-permute-start.4 = (bf16[128,2048]{1,0:T(8,128)(2,1)S(1)}, bf16[128,2048]{1,0:T(8,128)(2,1)S(1)}, u32[]{:S(2)}, u32[]{:S(2)}) collective-permute-start(bf16[128,2048]{1,0:T(8,128)(2,1)S(1)} %pad_maximum_fusion.refs_0_), channel_id=1, source_target_pairs={{0,32},{32,64},{64,96},{96,0},{1,33},{33,65},{65,97},{97,1},{2,34}... | collective-permute-start | bytes 1572872 | tf_op jit(solution)/shard_map/ppermute | solution.py:156
  76.4 4.9 %up.4 = (f32[128,3328]{1,0:T(8,128)S(1)}, bf16[128,3328]{1,0:T(8,128)(2,1)S(1)}) custom-call(bf16[128,2048]{1,0:T(8,128)(2,1)S(1)} %piece.4.refs_0_.refs_4_, bf16[128,2048]{1,0:T(8,128)(2,1)S(1)} %collective-permute-done.2.refs_1_, bf16[2048,1664]{1,0:T(8,128)(2,1)S(1)} %bitcast.36, bf16[2048,1664]{1,0:T(8,128)(2,1)S(1)} %bitcast.38, ...), custom_call_target="tpu_custom_call" | custom-call | flops 17179869184 | bytes 1024 | tf_op jit(solution)/shard_map/up/pallas_call | solution.py:162
  81.2 9.6 %collective-permute-done.1.refs_0_ = bf16[128,2048]{1,0:T(8,128)(2,1)S(1)} collective-permute-done((bf16[128,2048]{1,0:T(8,128)(2,1)S(1)}, bf16[128,2048]{1,0:T(8,128)(2,1)S(1)}, u32[]{:S(2)}, u32[]{:S(2)}) %collective-permute-start.1) | collective-permute-done | bytes 524320 | tf_op jit(solution)/shard_map/ppermute | solution.py:156
  92.9 4.9 %up.5 = (f32[128,3328]{1,0:T(8,128)S(1)}, bf16[128,3328]{1,0:T(8,128)(2,1)S(1)}) custom-call(bf16[128,2048]{1,0:T(8,128)(2,1)S(1)} %piece.5.refs_1_.refs_0_, bf16[128,2048]{1,0:T(8,128)(2,1)S(1)} %collective-permute-done.3.refs_1_, bf16[2048,1664]{1,0:T(8,128)(2,1)S(1)} %bitcast.36, bf16[2048,1664]{1,0:T(8,128)(2,1)S(1)} %bitcast.38, ...), custom_call_target="tpu_custom_call" | custom-call | flops 17179869184 | bytes 1024 | tf_op jit(solution)/shard_map/up/pallas_call | solution.py:162
  97.9 4.9 %up.6 = (f32[128,3328]{1,0:T(8,128)S(1)}, bf16[128,3328]{1,0:T(8,128)(2,1)S(1)}) custom-call(bf16[128,2048]{1,0:T(8,128)(2,1)S(1)} %piece.6.refs_1_.refs_0_, bf16[128,2048]{1,0:T(8,128)(2,1)S(1)} %collective-permute-done.7.refs_1_, bf16[2048,1664]{1,0:T(8,128)(2,1)S(1)} %bitcast.36, bf16[2048,1664]{1,0:T(8,128)(2,1)S(1)} %bitcast.38, ...), custom_call_target="tpu_custom_call" | custom-call | flops 17179869184 | bytes 1024 | tf_op jit(solution)/shard_map/up/pallas_call | solution.py:162
  102.8 4.3 %collective-permute-done.6.refs_0_ = bf16[128,2048]{1,0:T(8,128)(2,1)S(1)} collective-permute-done((bf16[128,2048]{1,0:T(8,128)(2,1)S(1)}, bf16[128,2048]{1,0:T(8,128)(2,1)S(1)}, u32[]{:S(2)}, u32[]{:S(2)}) %collective-permute-start.6) | collective-permute-done | bytes 524320 | tf_op jit(solution)/shard_map/ppermute | solution.py:156
  107.4 6.5 %collective-permute-done.9.refs_1_ = bf16[128,3328]{1,0:T(8,128)(2,1)S(1)} collective-permute-done((bf16[128,3328]{1,0:T(8,128)(2,1)S(1)}, bf16[128,3328]{1,0:T(8,128)(2,1)S(1)}, u32[]{:S(2)}, u32[]{:S(2)}) %collective-permute-start.9) | collective-permute-done | bytes 852000 | tf_op jit(solution)/shard_map/ppermute | solution.py:207
  114.1 4.9 %up.7 = (f32[128,3328]{1,0:T(8,128)S(1)}, bf16[128,3328]{1,0:T(8,128)(2,1)S(1)}) custom-call(bf16[128,2048]{1,0:T(8,128)(2,1)S(1)} %piece.7.refs_2_.refs_0_, bf16[128,2048]{1,0:T(8,128)(2,1)S(1)} %collective-permute-done.8.refs_1_, bf16[2048,1664]{1,0:T(8,128)(2,1)S(1)} %bitcast.36, bf16[2048,1664]{1,0:T(8,128)(2,1)S(1)} %bitcast.38, ...), custom_call_target="tpu_custom_call" | custom-call | flops 17179869184 | bytes 1024 | tf_op jit(solution)/shard_map/up/pallas_call | solution.py:162
  119.9 9.1 %collective-permute-done.12.refs_1_ = bf16[128,3328]{1,0:T(8,128)(2,1)S(1)} collective-permute-done((bf16[128,3328]{1,0:T(8,128)(2,1)S(1)}, bf16[128,3328]{1,0:T(8,128)(2,1)S(1)}, u32[]{:S(2)}, u32[]{:S(2)}) %collective-permute-start.12) | collective-permute-done | bytes 852000 | tf_op jit(solution)/shard_map/ppermute | solution.py:207
  129.5 8.7 %collective-permute-done.10.refs_1_ = bf16[64,3328]{1,0:T(8,128)(2,1)S(1)} collective-permute-done((bf16[64,3328]{1,0:T(8,128)(2,1)S(1)}, bf16[64,3328]{1,0:T(8,128)(2,1)S(1)}, u32[]{:S(2)}, u32[]{:S(2)}) %collective-permute-start.10) | collective-permute-done | bytes 426016 | tf_op jit(solution)/shard_map/ppermute | solution.py:207
  138.3 2.2 collective-permute-done.16.refs_1_
  140.8 1.9 collective-permute-done.14.refs_1_
  144.3 1.6 collective-permute-done.13.refs_1_
  146.0 1.4 collective-permute-start.17
  147.4 3.4 %collective-permute-done.18.refs_1_ = bf16[32,3328]{1,0:T(8,128)(2,1)S(1)} collective-permute-done((bf16[32,3328]{1,0:T(8,128)(2,1)S(1)}, bf16[32,3328]{1,0:T(8,128)(2,1)S(1)}, u32[]{:S(2)}, u32[]{:S(2)}) %collective-permute-start.18) | collective-permute-done | bytes 213024 | tf_op jit(solution)/shard_map/ppermute | solution.py:207
  153.2 2.2 collective-permute-done.21.refs_1_
  155.5 2.5 %collective-permute-done.20.refs_1_ = bf16[32,1664]{1,0:T(8,128)(2,1)S(1)} collective-permute-done((bf16[32,1664]{1,0:T(8,128)(2,1)S(1)}, bf16[32,1664]{1,0:T(8,128)(2,1)S(1)}, u32[]{:S(2)}, u32[]{:S(2)}) %collective-permute-start.20) | collective-permute-done | bytes 106528 | tf_op jit(solution)/shard_map/ppermute | solution.py:207
  161.0 7.1 %collective-permute-done.24.refs_1_ = bf16[32,3328]{1,0:T(8,128)(2,1)S(1)} collective-permute-done((bf16[32,3328]{1,0:T(8,128)(2,1)S(1)}, bf16[32,3328]{1,0:T(8,128)(2,1)S(1)}, u32[]{:S(2)}, u32[]{:S(2)}) %collective-permute-start.24) | collective-permute-done | bytes 213024 | tf_op jit(solution)/shard_map/ppermute | solution.py:206
  168.4 1.8 collective-permute-start.33
  170.3 2.1 collective-permute-start.29
  174.0 3.4 %down.4 = (f32[128,2048]{1,0:T(8,128)S(1)}, bf16[128,2048]{1,0:T(8,128)(2,1)S(1)}) custom-call(bf16[128,1664]{1,0:T(8,128)(2,1)S(1)} %join.11.refs_2_.refs_0_, bf16[128,1664]{1,0:T(8,128)(2,1)S(1)} %collective-permute-done.23.refs_1_, bf16[1664,2048]{1,0:T(8,128)(2,1)S(1)} %bitcast.34, bf16[64,1664]{1,0:T(8,128)(2,1)S(1)} %join.14.refs_3_.refs_0_), custom_call_target="tpu_custom_call" | custom-call | flops 17179869184 | bytes 1024 | tf_op jit(solution)/shard_map/down/pallas_call | solution.py:162
  177.5 2.7 %collective-permute-done.30.refs_1_ = bf16[64,1664]{1,0:T(8,128)(2,1)S(1)} collective-permute-done((bf16[64,1664]{1,0:T(8,128)(2,1)S(1)}, bf16[64,1664]{1,0:T(8,128)(2,1)S(1)}, u32[]{:S(2)}, u32[]{:S(2)}) %collective-permute-start.30) | collective-permute-done | bytes 213024 | tf_op jit(solution)/shard_map/ppermute | solution.py:207
  180.2 1.8 collective-permute-start.36
  182.1 3.4 %down.5 = (f32[128,2048]{1,0:T(8,128)S(1)}, bf16[128,2048]{1,0:T(8,128)(2,1)S(1)}) custom-call(bf16[128,1664]{1,0:T(8,128)(2,1)S(1)} %join.13.refs_2_.refs_0_, bf16[128,1664]{1,0:T(8,128)(2,1)S(1)} %collective-permute-done.29.refs_1_, bf16[1664,2048]{1,0:T(8,128)(2,1)S(1)} %bitcast.34, bf16[128,1664]{1,0:T(8,128)(2,1)S(1)} %join.15.refs_3_.refs_0_), custom_call_target="tpu_custom_call" | custom-call | flops 17179869184 | bytes 1024 | tf_op jit(solution)/shard_map/down/pallas_call | solution.py:162
  185.7 5.0 %collective-permute-start.31 = (bf16[128,2048]{1,0:T(8,128)(2,1)S(1)}, bf16[128,2048]{1,0:T(8,128)(2,1)S(1)}, u32[]{:S(2)}, u32[]{:S(2)}) collective-permute-start(bf16[128,2048]{1,0:T(8,128)(2,1)S(1)} %fold.4.refs_3_), channel_id=1, source_target_pairs={{0,32},{32,64},{64,96},{96,0},{1,33},{33,65},{65,97},{97,1},{2,34}... | collective-permute-start | bytes 1572872 | tf_op jit(solution)/shard_map/ppermute | solution.py:156
  190.7 3.4 %down.6 = (f32[128,2048]{1,0:T(8,128)S(1)}, bf16[128,2048]{1,0:T(8,128)(2,1)S(1)}) custom-call(bf16[128,1664]{1,0:T(8,128)(2,1)S(1)} %join.12.refs_2_.refs_0_, bf16[128,1664]{1,0:T(8,128)(2,1)S(1)} %collective-permute-done.33.refs_1_, bf16[1664,2048]{1,0:T(8,128)(2,1)S(1)} %bitcast.34, bf16[128,2048]{1,0:T(8,128)(2,1)S(1)} %fold.4.refs_3_), custom_call_target="tpu_custom_call" | custom-call | flops 17179869184 | bytes 1024 | tf_op jit(solution)/shard_map/down/pallas_call | solution.py:162
  194.7 3.4 %down.7 = (f32[128,2048]{1,0:T(8,128)S(1)}, bf16[128,2048]{1,0:T(8,128)(2,1)S(1)}) custom-call(bf16[128,1664]{1,0:T(8,128)(2,1)S(1)} %join.15.refs_3_.refs_0_, bf16[128,1664]{1,0:T(8,128)(2,1)S(1)} %collective-permute-done.36.refs_1_, bf16[1664,2048]{1,0:T(8,128)(2,1)S(1)} %bitcast.34, bf16[128,2048]{1,0:T(8,128)(2,1)S(1)} %fold.5.refs_3_), custom_call_target="tpu_custom_call" | custom-call | flops 17179869184 | bytes 1024 | tf_op jit(solution)/shard_map/down/pallas_call | solution.py:162
  198.4 1.7 collective-permute-done.37.refs_1_
  200.2 4.5 %collective-permute-start.38 = (bf16[128,2048]{1,0:T(8,128)(2,1)S(1)}, bf16[128,2048]{1,0:T(8,128)(2,1)S(1)}, u32[]{:S(2)}, u32[]{:S(2)}) collective-permute-start(bf16[128,2048]{1,0:T(8,128)(2,1)S(1)} %fold.7.refs_4_), channel_id=1, source_target_pairs={{0,64},{32,96},{64,0},{96,32},{1,65},{33,97},{65,1},{97,33},{2,66}... | collective-permute-start | bytes 1572872 | tf_op jit(solution)/shard_map/ppermute | solution.py:156
  204.7 5.4 %collective-permute-done.34.refs_1_ = bf16[128,2048]{1,0:T(8,128)(2,1)S(1)} collective-permute-done((bf16[128,2048]{1,0:T(8,128)(2,1)S(1)}, bf16[128,2048]{1,0:T(8,128)(2,1)S(1)}, u32[]{:S(2)}, u32[]{:S(2)}) %collective-permute-start.34) | collective-permute-done | bytes 524320 | tf_op jit(solution)/shard_map/ppermute | solution.py:156
  210.1 12.4 %collective-permute-done.38.refs_3_ = bf16[128,2048]{1,0:T(8,128)(2,1)S(1)} collective-permute-done((bf16[128,2048]{1,0:T(8,128)(2,1)S(1)}, bf16[128,2048]{1,0:T(8,128)(2,1)S(1)}, u32[]{:S(2)}, u32[]{:S(2)}) %collective-permute-start.38) | collective-permute-done | bytes 524320 | tf_op jit(solution)/shard_map/ppermute | solution.py:156
  222.8 3.3 %collective-permute-start.39 = (bf16[64,2048]{1,0:T(8,128)(2,1)S(1)}, bf16[64,2048]{1,0:T(8,128)(2,1)S(1)}, u32[]{:S(2)}, u32[]{:S(2)}) collective-permute-start(bf16[64,2048]{1,0:T(8,128)(2,1)S(1)} %select_convert_fusion), channel_id=1, source_target_pairs={{0,16},{16,0},{1,17},{17,1},{2,18},{18,2},{3,19},{19,3},{4,20},{20... | collective-permute-start | bytes 786440 | tf_op jit(solution)/shard_map/ppermute | solution.py:152
  226.1 6.0 %collective-permute-done.39 = bf16[64,2048]{1,0:T(8,128)(2,1)S(1)} collective-permute-done((bf16[64,2048]{1,0:T(8,128)(2,1)S(1)}, bf16[64,2048]{1,0:T(8,128)(2,1)S(1)}, u32[]{:S(2)}, u32[]{:S(2)}) %collective-permute-start.39) | collective-permute-done | bytes 262176 | tf_op jit(solution)/shard_map/ppermute | solution.py:152
  (149 shorter events, 22.4 us)
Async XLA Ops:
  3.5 35.2 %all-to-all-start = ((bf16[32,2,16,1024]{3,2,1,0:T(8,128)(2,1)}), bf16[32,2,16,1024]{3,2,1,0:T(8,128)(2,1)S(1)}, u32[]{:S(2)}, u32[]{:S(2)}) async-start(bf16[32,2,16,1024]{3,2,1,0:T(8,128)(2,1)} %gather_fusion), calls=%async_computation | async-start | bytes 4194304 | tf_op jit(solution)/shard_map/all_to_all | solution.py:69
  20.6 18.1 %copy-start.6 = (s32[8,8]{1,0:T(8,128)S(1)}, s32[8,8]{1,0:T(8,128)}, u32[]{:S(2)}) copy-start(s32[8,8]{1,0:T(8,128)} %table.1) | copy-start | bytes 772
  20.6 18.1 %copy-start.7 = (s32[8]{0:T(128)S(1)}, s32[8]{0:T(128)}, u32[]{:S(2)}) copy-start(s32[8]{0:T(128)} %context.1) | copy-start | bytes 100
  40.3 8.6 %copy-start.14 = (bf16[8,16384]{1,0:T(8,128)(2,1)S(1)}, bf16[8,16384]{1,0:T(8,128)(2,1)}, u32[]{:S(2)}) copy-start(bf16[8,16384]{1,0:T(8,128)(2,1)} %param.11) | copy-start | bytes 786436
  50.4 12.1 %all-to-all-start.1 = ((bf16[8,8,2176]{2,0,1:T(8,128)(2,1)}), bf16[8,8,2176]{2,0,1:T(8,128)(2,1)S(1)}, u32[]{:S(2)}, u32[]{:S(2)}) async-start(bf16[8,8,2176]{2,0,1:T(8,128)(2,1)} %pad_maximum_fusion.1), calls=%async_computation.1 | async-start | bytes 557056 | tf_op jit(solution)/shard_map/all_to_all | solution.py:107
  62.5 9.0 %copy-start.11 = (bf16[8,8,2176]{2,0,1:T(8,128)(2,1)}, bf16[8,8,2176]{2,0,1:T(8,128)(2,1)S(1)}, u32[]{:S(2)}) copy-start(bf16[8,8,2176]{2,0,1:T(8,128)(2,1)S(1)} %all-to-all-done.1) | copy-start | bytes 835588
  62.9 8.4 %collective-permute-start = (bf16[64,2048]{1,0:T(8,128)(2,1)S(1)}, bf16[64,2048]{1,0:T(8,128)(2,1)S(1)}, u32[]{:S(2)}, u32[]{:S(2)}) collective-permute-start(bf16[64,2048]{1,0:T(8,128)(2,1)S(1)} %pad_maximum_fusion.2), channel_id=1, source_target_pairs={{0,16},{16,0},{1,17},{17,1},{2,18},{18,2},{3,19},{19,3},{4,20},{20... | collective-permute-start | bytes 786440 | tf_op jit(solution)/shard_map/ppermute | solution.py:152
  71.5 4.1 %collective-permute-start.2 = (bf16[128,2048]{1,0:T(8,128)(2,1)S(1)}, bf16[128,2048]{1,0:T(8,128)(2,1)S(1)}, u32[]{:S(2)}, u32[]{:S(2)}) collective-permute-start(bf16[128,2048]{1,0:T(8,128)(2,1)S(1)} %piece.4.refs_0_.refs_4_), channel_id=1, source_target_pairs={{0,8},{8,0},{1,9},{9,1},{2,10},{10,2},{3,11},{11,3},{4,12},{12,4},... | collective-permute-start | bytes 1572872 | tf_op jit(solution)/shard_map/ppermute | solution.py:152
  71.6 19.4 %collective-permute-start.4 = (bf16[128,2048]{1,0:T(8,128)(2,1)S(1)}, bf16[128,2048]{1,0:T(8,128)(2,1)S(1)}, u32[]{:S(2)}, u32[]{:S(2)}) collective-permute-start(bf16[128,2048]{1,0:T(8,128)(2,1)S(1)} %pad_maximum_fusion.refs_0_), channel_id=1, source_target_pairs={{0,32},{32,64},{64,96},{96,0},{1,33},{33,65},{65,97},{97,1},{2,34}... | collective-permute-start | bytes 1572872 | tf_op jit(solution)/shard_map/ppermute | solution.py:156
  75.7 15.2 %collective-permute-start.1 = (bf16[128,2048]{1,0:T(8,128)(2,1)S(1)}, bf16[128,2048]{1,0:T(8,128)(2,1)S(1)}, u32[]{:S(2)}, u32[]{:S(2)}) collective-permute-start(bf16[128,2048]{1,0:T(8,128)(2,1)S(1)} %pad_maximum_fusion.refs_0_), channel_id=1, source_target_pairs={{0,96},{32,0},{64,32},{96,64},{1,97},{33,1},{65,33},{97,65},{2,98}... | collective-permute-start | bytes 1572872 | tf_op jit(solution)/shard_map/ppermute | solution.py:156
  90.9 2.0 collective-permute-start.3
  91.1 6.8 %collective-permute-start.7 = (bf16[128,2048]{1,0:T(8,128)(2,1)S(1)}, bf16[128,2048]{1,0:T(8,128)(2,1)S(1)}, u32[]{:S(2)}, u32[]{:S(2)}) collective-permute-start(bf16[128,2048]{1,0:T(8,128)(2,1)S(1)} %piece.6.refs_1_.refs_0_), channel_id=1, source_target_pairs={{0,8},{8,0},{1,9},{9,1},{2,10},{10,2},{3,11},{11,3},{4,12},{12,4},... | collective-permute-start | bytes 1572872 | tf_op jit(solution)/shard_map/ppermute | solution.py:152
  91.7 15.4 %collective-permute-start.6 = (bf16[128,2048]{1,0:T(8,128)(2,1)S(1)}, bf16[128,2048]{1,0:T(8,128)(2,1)S(1)}, u32[]{:S(2)}, u32[]{:S(2)}) collective-permute-start(bf16[128,2048]{1,0:T(8,128)(2,1)S(1)} %far.1.refs_4_), channel_id=1, source_target_pairs={{0,64},{32,96},{64,0},{96,32},{1,65},{33,97},{65,1},{97,33},{2,66}... | collective-permute-start | bytes 1572872 | tf_op jit(solution)/shard_map/ppermute | solution.py:156
  91.7 22.2 %collective-permute-start.9 = (bf16[128,3328]{1,0:T(8,128)(2,1)S(1)}, bf16[128,3328]{1,0:T(8,128)(2,1)S(1)}, u32[]{:S(2)}, u32[]{:S(2)}) collective-permute-start(bf16[128,3328]{1,0:T(8,128)(2,1)S(1)} %get-tuple-element.50), channel_id=1, source_target_pairs={{0,3},{1,2},{2,1},{3,0},{4,7},{5,6},{6,5},{7,4},{8,11},{9,10},{10,... | collective-permute-start | bytes 2555912 | tf_op jit(solution)/shard_map/ppermute | solution.py:207
  97.8 22.0 %collective-permute-start.5 = (bf16[128,3328]{1,0:T(8,128)(2,1)S(1)}, bf16[128,3328]{1,0:T(8,128)(2,1)S(1)}, u32[]{:S(2)}, u32[]{:S(2)}) collective-permute-start(bf16[128,3328]{1,0:T(8,128)(2,1)S(1)} %get-tuple-element.48), channel_id=1, source_target_pairs={{0,4},{4,0},{1,5},{5,1},{2,6},{6,2},{3,7},{7,3},{8,12},{12,8},{9,1... | collective-permute-start | bytes 2555912 | tf_op jit(solution)/shard_map/ppermute | solution.py:206
  107.1 7.0 %collective-permute-start.8 = (bf16[128,2048]{1,0:T(8,128)(2,1)S(1)}, bf16[128,2048]{1,0:T(8,128)(2,1)S(1)}, u32[]{:S(2)}, u32[]{:S(2)}) collective-permute-start(bf16[128,2048]{1,0:T(8,128)(2,1)S(1)} %piece.7.refs_2_.refs_0_), channel_id=1, source_target_pairs={{0,8},{8,0},{1,9},{9,1},{2,10},{10,2},{3,11},{11,3},{4,12},{12,4},... | collective-permute-start | bytes 1572872 | tf_op jit(solution)/shard_map/ppermute | solution.py:152
  107.2 21.8 %collective-permute-start.12 = (bf16[128,3328]{1,0:T(8,128)(2,1)S(1)}, bf16[128,3328]{1,0:T(8,128)(2,1)S(1)}, u32[]{:S(2)}, u32[]{:S(2)}) collective-permute-start(bf16[128,3328]{1,0:T(8,128)(2,1)S(1)} %get-tuple-element.56), channel_id=1, source_target_pairs={{0,1},{1,0},{2,3},{3,2},{4,5},{5,4},{6,7},{7,6},{8,9},{9,8},{10,11... | collective-permute-start | bytes 2555912 | tf_op jit(solution)/shard_map/ppermute | solution.py:207
  114.0 15.1 %collective-permute-start.11 = (bf16[64,3328]{1,0:T(8,128)(2,1)S(1)}, bf16[64,3328]{1,0:T(8,128)(2,1)S(1)}, u32[]{:S(2)}, u32[]{:S(2)}) collective-permute-start(bf16[64,3328]{1,0:T(8,128)(2,1)S(1)} %get-tuple-element.55), channel_id=1, source_target_pairs={{0,4},{4,0},{1,5},{5,1},{2,6},{6,2},{3,7},{7,3},{8,12},{12,8},{9,1... | collective-permute-start | bytes 1277960 | tf_op jit(solution)/shard_map/ppermute | solution.py:206
  119.0 21.5 %collective-permute-start.16 = (bf16[128,3328]{1,0:T(8,128)(2,1)S(1)}, bf16[128,3328]{1,0:T(8,128)(2,1)S(1)}, u32[]{:S(2)}, u32[]{:S(2)}) collective-permute-start(bf16[128,3328]{1,0:T(8,128)(2,1)S(1)} %get-tuple-element.63), channel_id=1, source_target_pairs={{0,3},{1,2},{2,1},{3,0},{4,7},{5,6},{6,5},{7,4},{8,11},{9,10},{10,... | collective-permute-start | bytes 2555912 | tf_op jit(solution)/shard_map/ppermute | solution.py:207
  119.9 18.3 %collective-permute-start.10 = (bf16[64,3328]{1,0:T(8,128)(2,1)S(1)}, bf16[64,3328]{1,0:T(8,128)(2,1)S(1)}, u32[]{:S(2)}, u32[]{:S(2)}) collective-permute-start(bf16[64,3328]{1,0:T(8,128)(2,1)S(1)} %get-tuple-element.54), channel_id=1, source_target_pairs={{0,1},{1,0},{2,3},{3,2},{4,5},{5,4},{6,7},{7,6},{8,9},{9,8},{10,11... | collective-permute-start | bytes 1277960 | tf_op jit(solution)/shard_map/ppermute | solution.py:207
  129.3 13.5 %collective-permute-start.14 = (bf16[32,3328]{1,0:T(8,128)(2,1)S(1)}, bf16[32,3328]{1,0:T(8,128)(2,1)S(1)}, u32[]{:S(2)}, u32[]{:S(2)}) collective-permute-start(bf16[32,3328]{1,0:T(8,128)(2,1)S(1)} %get-tuple-element.61), channel_id=1, source_target_pairs={{0,1},{1,0},{2,3},{3,2},{4,5},{5,4},{6,7},{7,6},{8,9},{9,8},{10,11... | collective-permute-start | bytes 638984 | tf_op jit(solution)/shard_map/ppermute | solution.py:207
  129.5 11.3 %collective-permute-start.15 = (bf16[64,3328]{1,0:T(8,128)(2,1)S(1)}, bf16[64,3328]{1,0:T(8,128)(2,1)S(1)}, u32[]{:S(2)}, u32[]{:S(2)}) collective-permute-start(bf16[64,3328]{1,0:T(8,128)(2,1)S(1)} %get-tuple-element.62), channel_id=1, source_target_pairs={{0,4},{4,0},{1,5},{5,1},{2,6},{6,2},{3,7},{7,3},{8,12},{12,8},{9,1... | collective-permute-start | bytes 1277960 | tf_op jit(solution)/shard_map/ppermute | solution.py:206
  138.2 7.6 %collective-permute-start.13 = (bf16[32,3328]{1,0:T(8,128)(2,1)S(1)}, bf16[32,3328]{1,0:T(8,128)(2,1)S(1)}, u32[]{:S(2)}, u32[]{:S(2)}) collective-permute-start(bf16[32,3328]{1,0:T(8,128)(2,1)S(1)} %get-tuple-element.60), channel_id=1, source_target_pairs={{0,3},{1,2},{2,1},{3,0},{4,7},{5,6},{6,5},{7,4},{8,11},{9,10},{10,... | collective-permute-start | bytes 638984 | tf_op jit(solution)/shard_map/ppermute | solution.py:207
  140.7 12.5 %collective-permute-start.22 = (bf16[64,3328]{1,0:T(8,128)(2,1)S(1)}, bf16[64,3328]{1,0:T(8,128)(2,1)S(1)}, u32[]{:S(2)}, u32[]{:S(2)}) collective-permute-start(bf16[64,3328]{1,0:T(8,128)(2,1)S(1)} %get-tuple-element.67), channel_id=1, source_target_pairs={{0,1},{1,0},{2,3},{3,2},{4,5},{5,4},{6,7},{7,6},{8,9},{9,8},{10,11... | collective-permute-start | bytes 1277960 | tf_op jit(solution)/shard_map/ppermute | solution.py:207
  142.8 12.6 %collective-permute-start.21 = (bf16[32,1664]{1,0:T(8,128)(2,1)S(1)}, bf16[32,1664]{1,0:T(8,128)(2,1)S(1)}, u32[]{:S(2)}, u32[]{:S(2)}) collective-permute-start(bf16[32,1664]{1,0:T(8,128)(2,1)S(1)} %hidden.4.refs_2_.refs_0_), channel_id=1, source_target_pairs={{0,1},{1,0},{2,3},{3,2},{4,5},{5,4},{6,7},{7,6},{8,9},{9,8},{10,11... | collective-permute-start | bytes 319496 | tf_op jit(solution)/shard_map/ppermute | solution.py:207
  143.2 7.5 %collective-permute-start.18 = (bf16[32,3328]{1,0:T(8,128)(2,1)S(1)}, bf16[32,3328]{1,0:T(8,128)(2,1)S(1)}, u32[]{:S(2)}, u32[]{:S(2)}) collective-permute-start(bf16[32,3328]{1,0:T(8,128)(2,1)S(1)} %get-tuple-element.66), channel_id=1, source_target_pairs={{0,3},{1,2},{2,1},{3,0},{4,7},{5,6},{6,5},{7,4},{8,11},{9,10},{10,... | collective-permute-start | bytes 638984 | tf_op jit(solution)/shard_map/ppermute | solution.py:207
  146.0 5.5 %collective-permute-start.17 = (bf16[32,1664]{1,0:T(8,128)(2,1)S(1)}, bf16[32,1664]{1,0:T(8,128)(2,1)S(1)}, u32[]{:S(2)}, u32[]{:S(2)}) collective-permute-start(bf16[32,1664]{1,0:T(8,128)(2,1)S(1)} %hidden.5.refs_2_.refs_0_), channel_id=1, source_target_pairs={{0,4},{4,0},{1,5},{5,1},{2,6},{6,2},{3,7},{7,3},{8,12},{12,8},{9,1... | collective-permute-start | bytes 319496 | tf_op jit(solution)/shard_map/ppermute | solution.py:206
  150.8 7.1 %collective-permute-start.20 = (bf16[32,1664]{1,0:T(8,128)(2,1)S(1)}, bf16[32,1664]{1,0:T(8,128)(2,1)S(1)}, u32[]{:S(2)}, u32[]{:S(2)}) collective-permute-start(bf16[32,1664]{1,0:T(8,128)(2,1)S(1)} %hidden.6.refs_2_.refs_0_), channel_id=1, source_target_pairs={{0,3},{1,2},{2,1},{3,0},{4,7},{5,6},{6,5},{7,4},{8,11},{9,10},{10,... | collective-permute-start | bytes 319496 | tf_op jit(solution)/shard_map/ppermute | solution.py:207
  151.5 8.6 %collective-permute-start.19 = (bf16[64,1664]{1,0:T(8,128)(2,1)S(1)}, bf16[64,1664]{1,0:T(8,128)(2,1)S(1)}, u32[]{:S(2)}, u32[]{:S(2)}) collective-permute-start(bf16[64,1664]{1,0:T(8,128)(2,1)S(1)} %join.8.refs_2_.refs_0_), channel_id=1, source_target_pairs={{0,1},{1,0},{2,3},{3,2},{4,5},{5,4},{6,7},{7,6},{8,9},{9,8},{10,11... | collective-permute-start | bytes 638984 | tf_op jit(solution)/shard_map/ppermute | solution.py:207
  155.4 12.9 %collective-permute-start.27 = (bf16[64,1664]{1,0:T(8,128)(2,1)S(1)}, bf16[64,1664]{1,0:T(8,128)(2,1)S(1)}, u32[]{:S(2)}, u32[]{:S(2)}) collective-permute-start(bf16[64,1664]{1,0:T(8,128)(2,1)S(1)} %join.9.refs_2_.refs_0_), channel_id=1, source_target_pairs={{0,3},{1,2},{2,1},{3,0},{4,7},{5,6},{6,5},{7,4},{8,11},{9,10},{10,... | collective-permute-start | bytes 638984 | tf_op jit(solution)/shard_map/ppermute | solution.py:207
  158.0 12.2 %collective-permute-start.26 = (bf16[64,1664]{1,0:T(8,128)(2,1)S(1)}, bf16[64,1664]{1,0:T(8,128)(2,1)S(1)}, u32[]{:S(2)}, u32[]{:S(2)}) collective-permute-start(bf16[64,1664]{1,0:T(8,128)(2,1)S(1)} %join.10.refs_2_.refs_0_), channel_id=1, source_target_pairs={{0,4},{4,0},{1,5},{5,1},{2,6},{6,2},{3,7},{7,3},{8,12},{12,8},{9,1... | collective-permute-start | bytes 638984 | tf_op jit(solution)/shard_map/ppermute | solution.py:206
  159.1 9.0 %collective-permute-start.24 = (bf16[32,3328]{1,0:T(8,128)(2,1)S(1)}, bf16[32,3328]{1,0:T(8,128)(2,1)S(1)}, u32[]{:S(2)}, u32[]{:S(2)}) collective-permute-start(bf16[32,3328]{1,0:T(8,128)(2,1)S(1)} %get-tuple-element.70), channel_id=1, source_target_pairs={{0,4},{4,0},{1,5},{5,1},{2,6},{6,2},{3,7},{7,3},{8,12},{12,8},{9,1... | collective-permute-start | bytes 638984 | tf_op jit(solution)/shard_map/ppermute | solution.py:206
  160.1 13.8 %collective-permute-start.23 = (bf16[128,1664]{1,0:T(8,128)(2,1)S(1)}, bf16[128,1664]{1,0:T(8,128)(2,1)S(1)}, u32[]{:S(2)}, u32[]{:S(2)}) collective-permute-start(bf16[128,1664]{1,0:T(8,128)(2,1)S(1)} %join.11.refs_2_.refs_0_), channel_id=1, source_target_pairs={{0,3},{1,2},{2,1},{3,0},{4,7},{5,6},{6,5},{7,4},{8,11},{9,10},{10,... | collective-permute-start | bytes 1277960 | tf_op jit(solution)/shard_map/ppermute | solution.py:207
  168.2 4.8 %collective-permute-start.25 = (bf16[32,1664]{1,0:T(8,128)(2,1)S(1)}, bf16[32,1664]{1,0:T(8,128)(2,1)S(1)}, u32[]{:S(2)}, u32[]{:S(2)}) collective-permute-start(bf16[32,1664]{1,0:T(8,128)(2,1)S(1)} %hidden.7.refs_2_.refs_0_), channel_id=1, source_target_pairs={{0,1},{1,0},{2,3},{3,2},{4,5},{5,4},{6,7},{7,6},{8,9},{9,8},{10,11... | collective-permute-start | bytes 319496 | tf_op jit(solution)/shard_map/ppermute | solution.py:207
  168.4 22.3 %collective-permute-start.33 = (bf16[128,1664]{1,0:T(8,128)(2,1)S(1)}, bf16[128,1664]{1,0:T(8,128)(2,1)S(1)}, u32[]{:S(2)}, u32[]{:S(2)}) collective-permute-start(bf16[128,1664]{1,0:T(8,128)(2,1)S(1)} %join.12.refs_2_.refs_0_), channel_id=1, source_target_pairs={{0,4},{4,0},{1,5},{5,1},{2,6},{6,2},{3,7},{7,3},{8,12},{12,8},{9,1... | collective-permute-start | bytes 1277960 | tf_op jit(solution)/shard_map/ppermute | solution.py:206
  170.3 11.8 %collective-permute-start.29 = (bf16[128,1664]{1,0:T(8,128)(2,1)S(1)}, bf16[128,1664]{1,0:T(8,128)(2,1)S(1)}, u32[]{:S(2)}, u32[]{:S(2)}) collective-permute-start(bf16[128,1664]{1,0:T(8,128)(2,1)S(1)} %join.13.refs_2_.refs_0_), channel_id=1, source_target_pairs={{0,1},{1,0},{2,3},{3,2},{4,5},{5,4},{6,7},{7,6},{8,9},{9,8},{10,11... | collective-permute-start | bytes 1277960 | tf_op jit(solution)/shard_map/ppermute | solution.py:207
  173.0 7.1 %collective-permute-start.30 = (bf16[64,1664]{1,0:T(8,128)(2,1)S(1)}, bf16[64,1664]{1,0:T(8,128)(2,1)S(1)}, u32[]{:S(2)}, u32[]{:S(2)}) collective-permute-start(bf16[64,1664]{1,0:T(8,128)(2,1)S(1)} %join.14.refs_3_.refs_0_), channel_id=1, source_target_pairs={{0,3},{1,2},{2,1},{3,0},{4,7},{5,6},{6,5},{7,4},{8,11},{9,10},{10,... | collective-permute-start | bytes 638984 | tf_op jit(solution)/shard_map/ppermute | solution.py:207
  177.4 8.2 %collective-permute-start.28 = (bf16[128,2048]{1,0:T(8,128)(2,1)S(1)}, bf16[128,2048]{1,0:T(8,128)(2,1)S(1)}, u32[]{:S(2)}, u32[]{:S(2)}) collective-permute-start(bf16[128,2048]{1,0:T(8,128)(2,1)S(1)} %get-tuple-element.72), channel_id=1, source_target_pairs={{0,8},{8,0},{1,9},{9,1},{2,10},{10,2},{3,11},{11,3},{4,12},{12,4},... | collective-permute-start | bytes 1572872 | tf_op jit(solution)/shard_map/ppermute | solution.py:152
  180.2 14.5 %collective-permute-start.36 = (bf16[128,1664]{1,0:T(8,128)(2,1)S(1)}, bf16[128,1664]{1,0:T(8,128)(2,1)S(1)}, u32[]{:S(2)}, u32[]{:S(2)}) collective-permute-start(bf16[128,1664]{1,0:T(8,128)(2,1)S(1)} %join.15.refs_3_.refs_0_), channel_id=1, source_target_pairs={{0,4},{4,0},{1,5},{5,1},{2,6},{6,2},{3,7},{7,3},{8,12},{12,8},{9,1... | collective-permute-start | bytes 1277960 | tf_op jit(solution)/shard_map/ppermute | solution.py:206
  185.5 8.9 %collective-permute-start.32 = (bf16[128,2048]{1,0:T(8,128)(2,1)S(1)}, bf16[128,2048]{1,0:T(8,128)(2,1)S(1)}, u32[]{:S(2)}, u32[]{:S(2)}) collective-permute-start(bf16[128,2048]{1,0:T(8,128)(2,1)S(1)} %get-tuple-element.74), channel_id=1, source_target_pairs={{0,8},{8,0},{1,9},{9,1},{2,10},{10,2},{3,11},{11,3},{4,12},{12,4},... | collective-permute-start | bytes 1572872 | tf_op jit(solution)/shard_map/ppermute | solution.py:152
  185.7 19.0 %collective-permute-start.31 = (bf16[128,2048]{1,0:T(8,128)(2,1)S(1)}, bf16[128,2048]{1,0:T(8,128)(2,1)S(1)}, u32[]{:S(2)}, u32[]{:S(2)}) collective-permute-start(bf16[128,2048]{1,0:T(8,128)(2,1)S(1)} %fold.4.refs_3_), channel_id=1, source_target_pairs={{0,32},{32,64},{64,96},{96,0},{1,33},{33,65},{65,97},{97,1},{2,34}... | collective-permute-start | bytes 1572872 | tf_op jit(solution)/shard_map/ppermute | solution.py:156
  194.1 4.3 %collective-permute-start.35 = (bf16[128,2048]{1,0:T(8,128)(2,1)S(1)}, bf16[128,2048]{1,0:T(8,128)(2,1)S(1)}, u32[]{:S(2)}, u32[]{:S(2)}) collective-permute-start(bf16[128,2048]{1,0:T(8,128)(2,1)S(1)} %get-tuple-element.76), channel_id=1, source_target_pairs={{0,8},{8,0},{1,9},{9,1},{2,10},{10,2},{3,11},{11,3},{4,12},{12,4},... | collective-permute-start | bytes 1572872 | tf_op jit(solution)/shard_map/ppermute | solution.py:152
  194.4 15.6 %collective-permute-start.34 = (bf16[128,2048]{1,0:T(8,128)(2,1)S(1)}, bf16[128,2048]{1,0:T(8,128)(2,1)S(1)}, u32[]{:S(2)}, u32[]{:S(2)}) collective-permute-start(bf16[128,2048]{1,0:T(8,128)(2,1)S(1)} %fold.5.refs_3_), channel_id=1, source_target_pairs={{0,96},{32,0},{64,32},{96,64},{1,97},{33,1},{65,33},{97,65},{2,98}... | collective-permute-start | bytes 1572872 | tf_op jit(solution)/shard_map/ppermute | solution.py:156
  198.1 2.0 collective-permute-start.37
  200.2 22.3 %collective-permute-start.38 = (bf16[128,2048]{1,0:T(8,128)(2,1)S(1)}, bf16[128,2048]{1,0:T(8,128)(2,1)S(1)}, u32[]{:S(2)}, u32[]{:S(2)}) collective-permute-start(bf16[128,2048]{1,0:T(8,128)(2,1)S(1)} %fold.7.refs_4_), channel_id=1, source_target_pairs={{0,64},{32,96},{64,0},{96,32},{1,65},{33,97},{65,1},{97,33},{2,66}... | collective-permute-start | bytes 1572872 | tf_op jit(solution)/shard_map/ppermute | solution.py:156
  222.7 9.5 %copy-start.12 = (bf16[8,8,2176]{2,0,1:T(8,128)(2,1)S(1)}, bf16[8,8,2176]{2,0,1:T(8,128)(2,1)}, u32[]{:S(2)}) copy-start(bf16[8,8,2176]{2,0,1:T(8,128)(2,1)} %copy-done.11) | copy-start | bytes 835588
  222.7 10.3 %copy-start.1 = (bf16[16,2,16,1024]{3,2,1,0:T(8,128)(2,1)S(1)}, bf16[16,2,16,1024]{3,2,1,0:T(8,128)(2,1)}, u32[]{:S(2)}) copy-start(bf16[16,2,16,1024]{3,2,1,0:T(8,128)(2,1)} %param.14) | copy-start | bytes 3145732
  222.8 9.3 %collective-permute-start.39 = (bf16[64,2048]{1,0:T(8,128)(2,1)S(1)}, bf16[64,2048]{1,0:T(8,128)(2,1)S(1)}, u32[]{:S(2)}, u32[]{:S(2)}) collective-permute-start(bf16[64,2048]{1,0:T(8,128)(2,1)S(1)} %select_convert_fusion), channel_id=1, source_target_pairs={{0,16},{16,0},{1,17},{17,1},{2,18},{18,2},{3,19},{19,3},{4,20},{20... | collective-permute-start | bytes 786440 | tf_op jit(solution)/shard_map/ppermute | solution.py:152
  (15 other events, 53.4 us)

commit v3 on v2

--- a/solution.py
+++ b/solution.py
@@ -104,16 +104,23 @@
         ],
         axis=2,
     )
-    block = lax.all_to_all(payload, GY, split_axis=1, concat_axis=0, tiled=True)
-    block = block.reshape(row_count * parts, width + 128)
-    resid = block[:, :width].astype(jnp.float32)
+    near = ("zh",) + GY
+    payload = jnp.concatenate([payload, payload], axis=1)
+    block = lax.all_to_all(payload, near, split_axis=1, concat_axis=0, tiled=True)
+    block = block.reshape(2, row_count * parts, width + 128)
+    mixed = block[:, :, :width].astype(jnp.float32)
     scale = (
-        block[:, width : width + 1].astype(jnp.float32)
-        + block[:, width + 1 : width + 2].astype(jnp.float32)
-        + block[:, width + 2 : width + 3].astype(jnp.float32)
+        block[:, :, width : width + 1].astype(jnp.float32)
+        + block[:, :, width + 1 : width + 2].astype(jnp.float32)
+        + block[:, :, width + 2 : width + 3].astype(jnp.float32)
     )
     gain = lax.dynamic_slice(norm_gain, (lax.axis_index(GY) * width,), (width,))
-    return resid, (resid * scale * gain).astype(jnp.bfloat16)
+    normed = (mixed * scale * gain).astype(jnp.bfloat16)
+    zh, zl = lax.axis_index("zh"), lax.axis_index("zl")
+    resid = jnp.where(zh == 0, mixed[0], mixed[1])
+    in_order = zh == zl
+    pair = [jnp.where(in_order, normed[0], normed[1]), jnp.where(in_order, normed[1], normed[0])]
+    return resid, jnp.concatenate([by_x(half) for half in pair], axis=0)
 
 
 def on_device(
@@ -131,9 +138,9 @@
 ):
     gate_weight, up_weight, down_weight, mark = load(gate_weight, up_weight, down_weight)
     mixed_rows = attend(tokens, queries, page_pool, new_pages, page_table, block_table, context, mark)
-    resid, normed_block = spread(mixed_rows, norm_gain)
-
-    return feed_forward(resid, normed_block, gate_weight, up_weight, down_weight)
+    resid, pair = spread(mixed_rows, norm_gain)
+
+    return feed_forward(resid, pair, gate_weight, up_weight, down_weight)
 
 
 def dot(a, b):
@@ -154,6 +161,11 @@
 
 def send(a, axis, shift):
     return lax.ppermute(a, axis, [(i, (i + shift) % 4) for i in range(4)])
+
+
+def home(a, shift, cross):
+    pairs = [(y * 2 + h, (y + shift) % 4 * 2 + (h ^ cross)) for y in range(4) for h in range(2)]
+    return lax.ppermute(a, CHIPS, pairs)
 
 
 def call(kernel, name, outs, *operands, after=()):
@@ -292,11 +304,11 @@
 
 
 SHIFTS = (1, 3, 2, 0)
-SUM_MASKS = ((4, 1, 3), (1, 4, 3), (3, 1, 4), (3, 4, 1))
-GATHER_MASKS = ((4, 1, 3), (3, 4, 1), (1, 3, 4), (1, 3, 4))
+SUM_MASKS = ((3, 1, 4), (1, 4, 3), (3, 4, 1), (1, 4, 3))
+GATHER_MASKS = ((3, 4, 1), (1, 4, 3), (3, 4, 1), (4, 3, 1))
 ORDER = (
-    "P3", "U3", "P0", "P1", "Q2", "U0", "U1", "P2", "A3", "U2", "A0", "A1",
-    "B3", "B0", "A2", "B1", "S3", "S0", "S1", "J0", "B2", "J3", "J1", "K0",
+    "P3", "U3", "Q2", "P0", "P1", "U0", "U1", "P2", "A3", "U2", "A0", "B3",
+    "A1", "B0", "A2", "B1", "S3", "S0", "S1", "J0", "B2", "J3", "J1", "K0",
     "S2", "K3", "K1", "J2", "D0", "K2", "D1", "F0", "D3", "F1", "D2", "F3",
     "F2",
 )
@@ -312,16 +324,13 @@
     return jnp.concatenate(b, axis=0)
 
 
-def feed_forward(resid, normed_block, gate_weight, up_weight, down_weight):
-    rows, width = normed_block.shape
+def feed_forward(resid, pair, gate_weight, up_weight, down_weight):
+    rows, width = resid.shape
     hidden_width = gate_weight.shape[1]
     z = lax.axis_index("zl")
     b16, f32 = jnp.bfloat16, jnp.float32
-    normed_block = by_x(normed_block)
-    near = swap(normed_block, "zh")
-    pair = jnp.concatenate([jnp.where(z == 0, normed_block, near), jnp.where(z == 0, near, normed_block)], axis=0)
     pieces = [send(pair, "y", -shift) if shift % 2 else pair for shift in SHIFTS]
-    state, parts = {}, {}
+    state, parts = {}, []
     last = ()
 
     def run(kernel, name, outs, *operands):
@@ -362,14 +371,13 @@
             keep, away = run(kernel, "down", [(part, f32), (part, b16)], *state[k], down_weight)
             state[k] = [keep, swap(away, "c")]
         else:
-            (part,) = run(fold_kernel, "fold", [((128, width), b16 if SHIFTS[k] else f32)], *state[k])
-            parts[k] = send(part, "y", SHIFTS[k]) if SHIFTS[k] else part
-    (total,) = run(total_kernel, "total", [((128, width), f32)], *parts.values())
-    total = total.reshape(2, rows, width)
-    mine = jnp.where(z == 0, total[0], total[1])
-    theirs = jnp.where(z == 0, total[1], total[0])
-    ffn_block = by_x(mine + wide(swap(narrow(theirs), "zh")))
-    return narrow(resid + ffn_block)
+            (part,) = run(fold_kernel, "fold", [((128, width), f32)], *state[k])
+            mine = jnp.where(z == 0, part[:rows], part[rows:])
+            theirs = narrow(jnp.where(z == 0, part[rows:], part[:rows]))
+            parts.append(home(theirs, SHIFTS[k], 1))
+            parts.append(home(narrow(mine), SHIFTS[k], 0) if SHIFTS[k] else mine)
+    (total,) = run(total_kernel, "total", [((rows, width), f32)], *parts)
+    return narrow(resid + by_x(total))
 
 
 def solution(mesh):

time: 233 us -> 225 us (0.966)
  waiting for transfers between devices: 112 us -> 87.6 us
  starting transfers between devices: 48 us -> 54.8 us
  local copies, waits for them, and re-layouts: 22.6 us -> 28.9 us
    ppermute x6 -> x3, waiting for transfers between devices: 31.7 us -> 1.17 us  [send(): return lax.ppermute(a, axis, [(i, (i + shift) % 4) for i in range(4)])]
    ppermute x0 -> x7, waiting for transfers between devices: none -> 18.3 us  [home(): return lax.ppermute(a, CHIPS, pairs)]
    ppermute x10 -> x8, waiting for transfers between devices: 15.7 us -> 0.73 us  [swap(): return lax.ppermute(a, axis, [(0, 1), (1, 0)])]
    ppermute x0 -> x7, starting transfers between devices: none -> 13.1 us  [home(): return lax.ppermute(a, CHIPS, pairs)]
    ppermute x16, starting transfers between devices: 7.51 us -> 16.8 us  [exchange(): return lax.ppermute(a, 'x', [(i, i ^ mask) for i in range(4)])]
    ppermute x6 -> x3, starting transfers between devices: 13.8 us -> 6.19 us  [send(): return lax.ppermute(a, axis, [(i, (i + shift) % 4) for i in range(4)])]
    unnamed x43 -> x41, local copies, waits for them, and re-layouts: 19.5 us -> 25.8 us
    ppermute x8, waiting for transfers between devices: 7.16 us -> 2.32 us  [exchange(): return lax.ppermute(a, 'zl', [(0, 1), (1, 0)])]
  transfers between devices with their start and end apart: 42 -> 44, of which waited for: 24 -> 22; matrix products, arithmetic and copies ran while one was open for 0% -> 1% of each run, Pallas kernels for 16% -> 16%
where the time goes in v3:
time: 225 us; the launch traced here: 223 us
  waiting for transfers between devices  87.6 us (39%)
  starting transfers between devices  54.8 us (24%)
  Pallas kernels  45.3 us (20%)
  local copies, waits for them, and re-layouts  28.9 us (13%)
  other arithmetic  5.72 us (3%)
    ppermute x16, waiting for transfers between devices, exchange(): return lax.ppermute(a, 'x', [(i, i ^ mask) for i in range(4)])  45.5 us
    pallas_call x38, Pallas kernels, call(): pl.pallas_call(lambda *refs: kernel(*refs[:count], *refs[count + len(afte...  35.3 us
    unnamed x41, local copies, waits for them, and re-layouts  25.8 us
    ppermute x7, waiting for transfers between devices, home(): return lax.ppermute(a, CHIPS, pairs)  18.3 us
    ppermute x16, starting transfers between devices, exchange(): return lax.ppermute(a, 'x', [(i, i ^ mask) for i in range(4)])  16.8 us
    ppermute x7, starting transfers between devices, home(): return lax.ppermute(a, CHIPS, pairs)  13.1 us
    all_to_all x1, waiting for transfers between devices, spread(): lax.all_to_all(payload, near, split_axis=1, concat_axis=0, tiled=True)  11.2 us
    pallas_call x1, Pallas kernels, attend(): pl.pallas_call(attend_kernel, name='attend', out_shape=jax.ShapeDtypeStru...  8.54 us
  transfers between devices with their start and end apart: 44, of which 22 were waited for; matrix products, arithmetic and copies ran while one was open for 1% of the time, Pallas kernels for 16%

profile of v3, /device:TPU:24, one launch (start us, length us, event | category | flops | bytes accessed | tf_op | source)
XLA Modules:
  0.0 223.0 jit_solution(10652140007185671533)
XLA Ops:
  1.4 2.1 gather_fusion
  3.5 8.2 %all-to-all-start = ((bf16[32,2,16,1024]{3,2,1,0:T(8,128)(2,1)}), bf16[32,2,16,1024]{3,2,1,0:T(8,128)(2,1)S(1)}, u32[]{:S(2)}, u32[]{:S(2)}) async-start(bf16[32,2,16,1024]{3,2,1,0:T(8,128)(2,1)} %gather_fusion), calls=%async_computation | async-start | bytes 4194304 | tf_op jit(solution)/shard_map/all_to_all | solution.py:69
  11.8 2.9 %copy-done.2 = bf16[2048,1664]{1,0:T(8,128)(2,1)S(1)} copy-done((bf16[2048,1664]{1,0:T(8,128)(2,1)S(1)}, bf16[2048,1664]{1,0:T(8,128)(2,1)}, u32[]{:S(2)}) %copy-start.2) | copy-done | bytes 6815768
  14.7 2.9 %copy-done.3 = bf16[2048,1664]{1,0:T(8,128)(2,1)S(1)} copy-done((bf16[2048,1664]{1,0:T(8,128)(2,1)S(1)}, bf16[2048,1664]{1,0:T(8,128)(2,1)}, u32[]{:S(2)}) %copy-start.3) | copy-done | bytes 6815768
  17.6 2.9 %copy-done.4 = bf16[1664,2048]{1,0:T(8,128)(2,1)S(1)} copy-done((bf16[1664,2048]{1,0:T(8,128)(2,1)S(1)}, bf16[1664,2048]{1,0:T(8,128)(2,1)}, u32[]{:S(2)}) %copy-start.4) | copy-done | bytes 6815768
  22.0 2.7 %copy-done.8 = bf16[1664,2048]{1,0:T(8,128)(2,1)} copy-done((bf16[1664,2048]{1,0:T(8,128)(2,1)}, bf16[1664,2048]{1,0:T(8,128)(2,1)S(1)}, u32[]{:S(2)}) %copy-start.8) | copy-done | bytes 6815768
  24.7 2.8 %copy-done.9 = bf16[2048,1664]{1,0:T(8,128)(2,1)} copy-done((bf16[2048,1664]{1,0:T(8,128)(2,1)}, bf16[2048,1664]{1,0:T(8,128)(2,1)S(1)}, u32[]{:S(2)}) %copy-start.9) | copy-done | bytes 6815768
  27.6 2.7 %copy-done.11 = bf16[2048,1664]{1,0:T(8,128)(2,1)} copy-done((bf16[2048,1664]{1,0:T(8,128)(2,1)}, bf16[2048,1664]{1,0:T(8,128)(2,1)S(1)}, u32[]{:S(2)}) %copy-start.11) | copy-done | bytes 6815768
  30.3 8.4 %all-to-all-done.arrived = bf16[32,2,16,1024]{3,2,1,0:T(8,128)(2,1)S(1)} async-done(((bf16[32,2,16,1024]{3,2,1,0:T(8,128)(2,1)}), bf16[32,2,16,1024]{3,2,1,0:T(8,128)(2,1)S(1)}, u32[]{:S(2)}, u32[]{:S(2)}) %all-to-all-start) | async-done | bytes 2097184 | tf_op jit(solution)/shard_map/all_to_all | solution.py:69
  38.7 1.6 copy-done.5
  40.3 8.5 %attend.2 = f32[8,128,128]{2,1,0:T(8,128)S(1)} custom-call(s32[8,8]{1,0:T(8,128)S(1)} %copy-done.6, s32[8]{0:T(128)S(1)} %copy-done.7, bf16[8,128,128]{2,1,0:T(8,128)(2,1)S(1)} %bitcast.54, bf16[32,2,16,1024]{3,2,1,0:T(8,128)(2,1)S(1)} %copy-done.5, bf16[32,2,16,1024]{3,2,1,0:T(8,128)(2,1)S(1)} %all-to-all-done.arrived, f32[8,128]{1,0:T(8,128)S(1)} %get-tuple-element.43._), custom_call_target="tpu_custom_call" | custom-call | flops 134217728 | bytes 8388608 | tf_op jit(solution)/shard_map/attend/pallas_call | solution.py:73
  50.5 4.9 %all-to-all-start.1 = ((bf16[8,16,2176]{2,0,1:T(8,128)(2,1)}), bf16[8,16,2176]{2,0,1:T(8,128)(2,1)S(1)}, u32[]{:S(2)}, u32[]{:S(2)}) async-start(bf16[8,16,2176]{2,0,1:T(8,128)(2,1)} %maximum_maximum_fusion), calls=%async_computation.1 | async-start | bytes 1114112 | tf_op jit(solution)/shard_map/all_to_all | solution.py:109
  56.1 11.2 %all-to-all-done.1 = bf16[8,16,2176]{2,0,1:T(8,128)(2,1)S(1)} async-done(((bf16[8,16,2176]{2,0,1:T(8,128)(2,1)}), bf16[8,16,2176]{2,0,1:T(8,128)(2,1)S(1)}, u32[]{:S(2)}, u32[]{:S(2)}) %all-to-all-start.1) | async-done | bytes 557088 | tf_op jit(solution)/shard_map/all_to_all | solution.py:109
  68.2 3.4 %collective-permute-start = (bf16[128,2048]{1,0:T(8,128)(2,1)S(1)}, bf16[128,2048]{1,0:T(8,128)(2,1)S(1)}, u32[]{:S(2)}, u32[]{:S(2)}) collective-permute-start(bf16[128,2048]{1,0:T(8,128)(2,1)S(1)} %bitcast_dynamic-update-slice_fusion.refs_0_), channel_id=1, source_target_pairs={{0,96},{32,0},{64,32},{96,64},{1,97},{33,1},{65,33},{97,65},{2,98}... | collective-permute-start | bytes 1572872 | tf_op jit(solution)/shard_map/ppermute | solution.py:163
  74.0 2.9 %copy-done.10 = bf16[2048,1664]{1,0:T(8,128)(2,1)S(1)} copy-done((bf16[2048,1664]{1,0:T(8,128)(2,1)S(1)}, bf16[2048,1664]{1,0:T(8,128)(2,1)}, u32[]{:S(2)}) %copy-start.10) | copy-done | bytes 6815768
  77.0 2.9 %copy-done.12 = bf16[2048,1664]{1,0:T(8,128)(2,1)S(1)} copy-done((bf16[2048,1664]{1,0:T(8,128)(2,1)S(1)}, bf16[2048,1664]{1,0:T(8,128)(2,1)}, u32[]{:S(2)}) %copy-start.12) | copy-done | bytes 6815768
  79.9 4.9 %up.4 = (f32[128,3328]{1,0:T(8,128)S(1)}, bf16[128,3328]{1,0:T(8,128)(2,1)S(1)}) custom-call(bf16[128,2048]{1,0:T(8,128)(2,1)S(1)} %piece.4.refs_0_.refs_4_, bf16[128,2048]{1,0:T(8,128)(2,1)S(1)} %collective-permute-done.1.refs_1_, bf16[2048,1664]{1,0:T(8,128)(2,1)S(1)} %copy-done.10, bf16[2048,1664]{1,0:T(8,128)(2,1)S(1)} %copy-done.12, ...), custom_call_target="tpu_custom_call" | custom-call | flops 17179869184 | bytes 1024 | tf_op jit(solution)/shard_map/up/pallas_call | solution.py:174
  84.9 1.5 collective-permute-start.5
  89.4 4.9 %up.5 = (f32[128,3328]{1,0:T(8,128)S(1)}, bf16[128,3328]{1,0:T(8,128)(2,1)S(1)}) custom-call(bf16[128,2048]{1,0:T(8,128)(2,1)S(1)} %piece.5.refs_1_.refs_0_, bf16[128,2048]{1,0:T(8,128)(2,1)S(1)} %collective-permute-done.2.refs_1_, bf16[2048,1664]{1,0:T(8,128)(2,1)S(1)} %bitcast.58, bf16[2048,1664]{1,0:T(8,128)(2,1)S(1)} %copy-done.12, ...), custom_call_target="tpu_custom_call" | custom-call | flops 17179869184 | bytes 1024 | tf_op jit(solution)/shard_map/up/pallas_call | solution.py:174
  94.2 4.9 %up.6 = (f32[128,3328]{1,0:T(8,128)S(1)}, bf16[128,3328]{1,0:T(8,128)(2,1)S(1)}) custom-call(bf16[128,2048]{1,0:T(8,128)(2,1)S(1)} %piece.6.refs_4_.refs_0_, bf16[128,2048]{1,0:T(8,128)(2,1)S(1)} %collective-permute-done.6.refs_1_, bf16[2048,1664]{1,0:T(8,128)(2,1)S(1)} %bitcast.58, bf16[2048,1664]{1,0:T(8,128)(2,1)S(1)} %copy-done.12, ...), custom_call_target="tpu_custom_call" | custom-call | flops 17179869184 | bytes 1024 | tf_op jit(solution)/shard_map/up/pallas_call | solution.py:174
  101.3 7.6 %collective-permute-done.8.refs_1_ = bf16[128,3328]{1,0:T(8,128)(2,1)S(1)} collective-permute-done((bf16[128,3328]{1,0:T(8,128)(2,1)S(1)}, bf16[128,3328]{1,0:T(8,128)(2,1)S(1)}, u32[]{:S(2)}, u32[]{:S(2)}) %collective-permute-start.8) | collective-permute-done | bytes 852000 | tf_op jit(solution)/shard_map/ppermute | solution.py:219
  109.1 4.9 %up.7 = (f32[128,3328]{1,0:T(8,128)S(1)}, bf16[128,3328]{1,0:T(8,128)(2,1)S(1)}) custom-call(bf16[128,2048]{1,0:T(8,128)(2,1)S(1)} %piece.7.refs_2_.refs_0_, bf16[128,2048]{1,0:T(8,128)(2,1)S(1)} %collective-permute-done.7.refs_1_, bf16[2048,1664]{1,0:T(8,128)(2,1)S(1)} %bitcast.58, bf16[2048,1664]{1,0:T(8,128)(2,1)S(1)} %copy-done.12, ...), custom_call_target="tpu_custom_call" | custom-call | flops 17179869184 | bytes 1024 | tf_op jit(solution)/shard_map/up/pallas_call | solution.py:174
  115.2 8.3 %collective-permute-done.4.refs_1_ = bf16[128,3328]{1,0:T(8,128)(2,1)S(1)} collective-permute-done((bf16[128,3328]{1,0:T(8,128)(2,1)S(1)}, bf16[128,3328]{1,0:T(8,128)(2,1)S(1)}, u32[]{:S(2)}, u32[]{:S(2)}) %collective-permute-start.4) | collective-permute-done | bytes 852000 | tf_op jit(solution)/shard_map/ppermute | solution.py:219
  123.8 3.2 %collective-permute-done.10.refs_1_ = bf16[128,3328]{1,0:T(8,128)(2,1)S(1)} collective-permute-done((bf16[128,3328]{1,0:T(8,128)(2,1)S(1)}, bf16[128,3328]{1,0:T(8,128)(2,1)S(1)}, u32[]{:S(2)}, u32[]{:S(2)}) %collective-permute-start.10) | collective-permute-done | bytes 852000 | tf_op jit(solution)/shard_map/ppermute | solution.py:219
  128.4 7.1 %collective-permute-done.9.refs_1_ = bf16[64,3328]{1,0:T(8,128)(2,1)S(1)} collective-permute-done((bf16[64,3328]{1,0:T(8,128)(2,1)S(1)}, bf16[64,3328]{1,0:T(8,128)(2,1)S(1)}, u32[]{:S(2)}, u32[]{:S(2)}) %collective-permute-start.9) | collective-permute-done | bytes 426016 | tf_op jit(solution)/shard_map/ppermute | solution.py:219
  135.6 6.2 %collective-permute-done.15.refs_1_ = bf16[128,3328]{1,0:T(8,128)(2,1)S(1)} collective-permute-done((bf16[128,3328]{1,0:T(8,128)(2,1)S(1)}, bf16[128,3328]{1,0:T(8,128)(2,1)S(1)}, u32[]{:S(2)}, u32[]{:S(2)}) %collective-permute-start.15) | collective-permute-done | bytes 852000 | tf_op jit(solution)/shard_map/ppermute | solution.py:219
  143.2 3.1 %collective-permute-done.13.refs_1_ = bf16[32,3328]{1,0:T(8,128)(2,1)S(1)} collective-permute-done((bf16[32,3328]{1,0:T(8,128)(2,1)S(1)}, bf16[32,3328]{1,0:T(8,128)(2,1)S(1)}, u32[]{:S(2)}, u32[]{:S(2)}) %collective-permute-start.13) | collective-permute-done | bytes 213024 | tf_op jit(solution)/shard_map/ppermute | solution.py:219
  147.8 3.3 %collective-permute-done.17.refs_1_ = bf16[32,3328]{1,0:T(8,128)(2,1)S(1)} collective-permute-done((bf16[32,3328]{1,0:T(8,128)(2,1)S(1)}, bf16[32,3328]{1,0:T(8,128)(2,1)S(1)}, u32[]{:S(2)}, u32[]{:S(2)}) %collective-permute-start.17) | collective-permute-done | bytes 213024 | tf_op jit(solution)/shard_map/ppermute | solution.py:219
  151.3 1.4 collective-permute-done.16.refs_1_
  152.7 2.0 collective-permute-start.18
  154.9 1.7 collective-permute-done.20.refs_1_
  156.6 3.8 %collective-permute-start.26 = (bf16[64,1664]{1,0:T(8,128)(2,1)S(1)}, bf16[64,1664]{1,0:T(8,128)(2,1)S(1)}, u32[]{:S(2)}, u32[]{:S(2)}) collective-permute-start(bf16[64,1664]{1,0:T(8,128)(2,1)S(1)} %join.9.refs_2_.refs_0_), channel_id=1, source_target_pairs={{0,3},{1,2},{2,1},{3,0},{4,7},{5,6},{6,5},{7,4},{8,11},{9,10},{10,... | collective-permute-start | bytes 638984 | tf_op jit(solution)/shard_map/ppermute | solution.py:219
  161.4 3.8 %collective-permute-start.24 = (bf16[32,1664]{1,0:T(8,128)(2,1)S(1)}, bf16[32,1664]{1,0:T(8,128)(2,1)S(1)}, u32[]{:S(2)}, u32[]{:S(2)}) collective-permute-start(bf16[32,1664]{1,0:T(8,128)(2,1)S(1)} %hidden.7.refs_2_.refs_0_), channel_id=1, source_target_pairs={{0,3},{1,2},{2,1},{3,0},{4,7},{5,6},{6,5},{7,4},{8,11},{9,10},{10,... | collective-permute-start | bytes 319496 | tf_op jit(solution)/shard_map/ppermute | solution.py:219
  165.3 1.4 collective-permute-start.33
  166.8 1.8 collective-permute-start.28
  170.0 4.0 %collective-permute-done.22.refs_1_ = bf16[128,1664]{1,0:T(8,128)(2,1)S(1)} collective-permute-done((bf16[128,1664]{1,0:T(8,128)(2,1)S(1)}, bf16[128,1664]{1,0:T(8,128)(2,1)S(1)}, u32[]{:S(2)}, u32[]{:S(2)}) %collective-permute-start.22) | collective-permute-done | bytes 426016 | tf_op jit(solution)/shard_map/ppermute | solution.py:219
  174.1 3.4 %down.4 = (f32[128,2048]{1,0:T(8,128)S(1)}, bf16[128,2048]{1,0:T(8,128)(2,1)S(1)}) custom-call(bf16[128,1664]{1,0:T(8,128)(2,1)S(1)} %join.11.refs_2_.refs_0_, bf16[128,1664]{1,0:T(8,128)(2,1)S(1)} %collective-permute-done.22.refs_1_, bf16[1664,2048]{1,0:T(8,128)(2,1)S(1)} %bitcast.56, bf16[64,1664]{1,0:T(8,128)(2,1)S(1)} %join.14.refs_3_.refs_0_), custom_call_target="tpu_custom_call" | custom-call | flops 17179869184 | bytes 1024 | tf_op jit(solution)/shard_map/down/pallas_call | solution.py:174
  177.7 3.4 %down.5 = (f32[128,2048]{1,0:T(8,128)S(1)}, bf16[128,2048]{1,0:T(8,128)(2,1)S(1)}) custom-call(bf16[128,1664]{1,0:T(8,128)(2,1)S(1)} %join.13.refs_2_.refs_0_, bf16[128,1664]{1,0:T(8,128)(2,1)S(1)} %collective-permute-done.28.refs_1_, bf16[1664,2048]{1,0:T(8,128)(2,1)S(1)} %bitcast.56, bf16[128,1664]{1,0:T(8,128)(2,1)S(1)} %join.15.refs_3_.refs_0_), custom_call_target="tpu_custom_call" | custom-call | flops 17179869184 | bytes 1024 | tf_op jit(solution)/shard_map/down/pallas_call | solution.py:174
  181.8 3.4 %down.6 = (f32[128,2048]{1,0:T(8,128)S(1)}, bf16[128,2048]{1,0:T(8,128)(2,1)S(1)}) custom-call(bf16[128,1664]{1,0:T(8,128)(2,1)S(1)} %join.12.refs_2_.refs_0_, bf16[128,1664]{1,0:T(8,128)(2,1)S(1)} %collective-permute-done.33.refs_1_, bf16[1664,2048]{1,0:T(8,128)(2,1)S(1)} %bitcast.56, f32[128,2048]{1,0:T(8,128)S(1)} %fold.4.refs_3_), custom_call_target="tpu_custom_call" | custom-call | flops 17179869184 | bytes 1024 | tf_op jit(solution)/shard_map/down/pallas_call | solution.py:174
  185.4 3.2 %collective-permute-start.30 = (bf16[64,2048]{1,0:T(8,128)(2,1)S(1)}, bf16[64,2048]{1,0:T(8,128)(2,1)S(1)}, u32[]{:S(2)}, u32[]{:S(2)}) collective-permute-start(bf16[64,2048]{1,0:T(8,128)(2,1)S(1)} %get-tuple-element.86), channel_id=1, source_target_pairs={{0,48},{16,32},{32,80},{48,64},{64,112},{80,96},{96,16},{112,0},{1... | collective-permute-start | bytes 786440 | tf_op jit(solution)/shard_map/ppermute | solution.py:168
  189.9 3.4 %down.7 = (f32[128,2048]{1,0:T(8,128)S(1)}, bf16[128,2048]{1,0:T(8,128)(2,1)S(1)}) custom-call(bf16[128,1664]{1,0:T(8,128)(2,1)S(1)} %join.15.refs_3_.refs_0_, bf16[128,1664]{1,0:T(8,128)(2,1)S(1)} %collective-permute-done.37.refs_1_, bf16[1664,2048]{1,0:T(8,128)(2,1)S(1)} %bitcast.56, f32[128,2048]{1,0:T(8,128)S(1)} %fold.5.refs_3_), custom_call_target="tpu_custom_call" | custom-call | flops 17179869184 | bytes 1024 | tf_op jit(solution)/shard_map/down/pallas_call | solution.py:174
  193.4 2.0 collective-permute-start.34
  196.5 1.6 collective-permute-start.38
  198.3 4.8 %collective-permute-start.40 = (bf16[64,2048]{1,0:T(8,128)(2,1)S(1)}, bf16[64,2048]{1,0:T(8,128)(2,1)S(1)}, u32[]{:S(2)}, u32[]{:S(2)}) collective-permute-start(bf16[64,2048]{1,0:T(8,128)(2,1)S(1)} %get-tuple-element.82), channel_id=1, source_target_pairs={{0,80},{16,64},{32,112},{48,96},{64,16},{80,0},{96,48},{112,32},{1... | collective-permute-start | bytes 786440 | tf_op jit(solution)/shard_map/ppermute | solution.py:168
  203.4 2.8 %collective-permute-done.34.refs_2_ = bf16[64,2048]{1,0:T(8,128)(2,1)S(1)} collective-permute-done((bf16[64,2048]{1,0:T(8,128)(2,1)S(1)}, bf16[64,2048]{1,0:T(8,128)(2,1)S(1)}, u32[]{:S(2)}, u32[]{:S(2)}) %collective-permute-start.34) | collective-permute-done | bytes 262176 | tf_op jit(solution)/shard_map/ppermute | solution.py:168
  206.3 4.6 %collective-permute-done.35.refs_3_ = bf16[64,2048]{1,0:T(8,128)(2,1)S(1)} collective-permute-done((bf16[64,2048]{1,0:T(8,128)(2,1)S(1)}, bf16[64,2048]{1,0:T(8,128)(2,1)S(1)}, u32[]{:S(2)}, u32[]{:S(2)}) %collective-permute-start.35) | collective-permute-done | bytes 262176 | tf_op jit(solution)/shard_map/ppermute | solution.py:168
  211.8 5.7 %collective-permute-done.40.refs_6_ = bf16[64,2048]{1,0:T(8,128)(2,1)S(1)} collective-permute-done((bf16[64,2048]{1,0:T(8,128)(2,1)S(1)}, bf16[64,2048]{1,0:T(8,128)(2,1)S(1)}, u32[]{:S(2)}, u32[]{:S(2)}) %collective-permute-start.40) | collective-permute-done | bytes 262176 | tf_op jit(solution)/shard_map/ppermute | solution.py:168
  217.5 4.2 %collective-permute-done.41.refs_7_ = bf16[64,2048]{1,0:T(8,128)(2,1)S(1)} collective-permute-done((bf16[64,2048]{1,0:T(8,128)(2,1)S(1)}, bf16[64,2048]{1,0:T(8,128)(2,1)S(1)}, u32[]{:S(2)}, u32[]{:S(2)}) %collective-permute-start.41) | collective-permute-done | bytes 262176 | tf_op jit(solution)/shard_map/ppermute | solution.py:168
  (159 shorter events, 29.0 us)
Async XLA Ops:
  3.5 35.2 %all-to-all-start = ((bf16[32,2,16,1024]{3,2,1,0:T(8,128)(2,1)}), bf16[32,2,16,1024]{3,2,1,0:T(8,128)(2,1)S(1)}, u32[]{:S(2)}, u32[]{:S(2)}) async-start(bf16[32,2,16,1024]{3,2,1,0:T(8,128)(2,1)} %gather_fusion), calls=%async_computation | async-start | bytes 4194304 | tf_op jit(solution)/shard_map/all_to_all | solution.py:69
  20.6 18.1 %copy-start.6 = (s32[8,8]{1,0:T(8,128)S(1)}, s32[8,8]{1,0:T(8,128)}, u32[]{:S(2)}) copy-start(s32[8,8]{1,0:T(8,128)} %table.1) | copy-start | bytes 772
  20.6 18.1 %copy-start.7 = (s32[8]{0:T(128)S(1)}, s32[8]{0:T(128)}, u32[]{:S(2)}) copy-start(s32[8]{0:T(128)} %context.1) | copy-start | bytes 100
  40.3 8.6 %copy-start.15 = (bf16[8,16384]{1,0:T(8,128)(2,1)S(1)}, bf16[8,16384]{1,0:T(8,128)(2,1)}, u32[]{:S(2)}) copy-start(bf16[8,16384]{1,0:T(8,128)(2,1)} %param.11) | copy-start | bytes 786436
  50.5 16.8 %all-to-all-start.1 = ((bf16[8,16,2176]{2,0,1:T(8,128)(2,1)}), bf16[8,16,2176]{2,0,1:T(8,128)(2,1)S(1)}, u32[]{:S(2)}, u32[]{:S(2)}) async-start(bf16[8,16,2176]{2,0,1:T(8,128)(2,1)} %maximum_maximum_fusion), calls=%async_computation.1 | async-start | bytes 1114112 | tf_op jit(solution)/shard_map/all_to_all | solution.py:109
  68.1 5.9 %collective-permute-start.1 = (bf16[128,2048]{1,0:T(8,128)(2,1)S(1)}, bf16[128,2048]{1,0:T(8,128)(2,1)S(1)}, u32[]{:S(2)}, u32[]{:S(2)}) collective-permute-start(bf16[128,2048]{1,0:T(8,128)(2,1)S(1)} %piece.4.refs_0_.refs_4_), channel_id=1, source_target_pairs={{0,8},{8,0},{1,9},{9,1},{2,10},{10,2},{3,11},{11,3},{4,12},{12,4},... | collective-permute-start | bytes 1572872 | tf_op jit(solution)/shard_map/ppermute | solution.py:159
  68.2 18.2 %collective-permute-start = (bf16[128,2048]{1,0:T(8,128)(2,1)S(1)}, bf16[128,2048]{1,0:T(8,128)(2,1)S(1)}, u32[]{:S(2)}, u32[]{:S(2)}) collective-permute-start(bf16[128,2048]{1,0:T(8,128)(2,1)S(1)} %bitcast_dynamic-update-slice_fusion.refs_0_), channel_id=1, source_target_pairs={{0,96},{32,0},{64,32},{96,64},{1,97},{33,1},{65,33},{97,65},{2,98}... | collective-permute-start | bytes 1572872 | tf_op jit(solution)/shard_map/ppermute | solution.py:163
  71.5 14.9 %collective-permute-start.3 = (bf16[128,2048]{1,0:T(8,128)(2,1)S(1)}, bf16[128,2048]{1,0:T(8,128)(2,1)S(1)}, u32[]{:S(2)}, u32[]{:S(2)}) collective-permute-start(bf16[128,2048]{1,0:T(8,128)(2,1)S(1)} %bitcast_dynamic-update-slice_fusion.refs_0_), channel_id=1, source_target_pairs={{0,32},{32,64},{64,96},{96,0},{1,33},{33,65},{65,97},{97,1},{2,34}... | collective-permute-start | bytes 1572872 | tf_op jit(solution)/shard_map/ppermute | solution.py:163
  84.9 15.5 %collective-permute-start.5 = (bf16[128,2048]{1,0:T(8,128)(2,1)S(1)}, bf16[128,2048]{1,0:T(8,128)(2,1)S(1)}, u32[]{:S(2)}, u32[]{:S(2)}) collective-permute-start(bf16[128,2048]{1,0:T(8,128)(2,1)S(1)} %far.1.refs_1_), channel_id=1, source_target_pairs={{0,64},{32,96},{64,0},{96,32},{1,65},{33,97},{65,1},{97,33},{2,66}... | collective-permute-start | bytes 1572872 | tf_op jit(solution)/shard_map/ppermute | solution.py:163
  86.4 2.0 collective-permute-start.2
  86.5 7.7 %collective-permute-start.6 = (bf16[128,2048]{1,0:T(8,128)(2,1)S(1)}, bf16[128,2048]{1,0:T(8,128)(2,1)S(1)}, u32[]{:S(2)}, u32[]{:S(2)}) collective-permute-start(bf16[128,2048]{1,0:T(8,128)(2,1)S(1)} %piece.6.refs_4_.refs_0_), channel_id=1, source_target_pairs={{0,8},{8,0},{1,9},{9,1},{2,10},{10,2},{3,11},{11,3},{4,12},{12,4},... | collective-permute-start | bytes 1572872 | tf_op jit(solution)/shard_map/ppermute | solution.py:159
  87.1 21.8 %collective-permute-start.8 = (bf16[128,3328]{1,0:T(8,128)(2,1)S(1)}, bf16[128,3328]{1,0:T(8,128)(2,1)S(1)}, u32[]{:S(2)}, u32[]{:S(2)}) collective-permute-start(bf16[128,3328]{1,0:T(8,128)(2,1)S(1)} %get-tuple-element.50), channel_id=1, source_target_pairs={{0,1},{1,0},{2,3},{3,2},{4,5},{5,4},{6,7},{7,6},{8,9},{9,8},{10,11... | collective-permute-start | bytes 2555912 | tf_op jit(solution)/shard_map/ppermute | solution.py:219
  100.4 8.8 %collective-permute-start.7 = (bf16[128,2048]{1,0:T(8,128)(2,1)S(1)}, bf16[128,2048]{1,0:T(8,128)(2,1)S(1)}, u32[]{:S(2)}, u32[]{:S(2)}) collective-permute-start(bf16[128,2048]{1,0:T(8,128)(2,1)S(1)} %piece.7.refs_2_.refs_0_), channel_id=1, source_target_pairs={{0,8},{8,0},{1,9},{9,1},{2,10},{10,2},{3,11},{11,3},{4,12},{12,4},... | collective-permute-start | bytes 1572872 | tf_op jit(solution)/shard_map/ppermute | solution.py:159
  100.5 23.0 %collective-permute-start.4 = (bf16[128,3328]{1,0:T(8,128)(2,1)S(1)}, bf16[128,3328]{1,0:T(8,128)(2,1)S(1)}, u32[]{:S(2)}, u32[]{:S(2)}) collective-permute-start(bf16[128,3328]{1,0:T(8,128)(2,1)S(1)} %get-tuple-element.48), channel_id=1, source_target_pairs={{0,3},{1,2},{2,1},{3,0},{4,7},{5,6},{6,5},{7,4},{8,11},{9,10},{10,... | collective-permute-start | bytes 2555912 | tf_op jit(solution)/shard_map/ppermute | solution.py:219
  101.1 26.0 %collective-permute-start.10 = (bf16[128,3328]{1,0:T(8,128)(2,1)S(1)}, bf16[128,3328]{1,0:T(8,128)(2,1)S(1)}, u32[]{:S(2)}, u32[]{:S(2)}) collective-permute-start(bf16[128,3328]{1,0:T(8,128)(2,1)S(1)} %get-tuple-element.55), channel_id=1, source_target_pairs={{0,1},{1,0},{2,3},{3,2},{4,5},{5,4},{6,7},{7,6},{8,9},{9,8},{10,11... | collective-permute-start | bytes 2555912 | tf_op jit(solution)/shard_map/ppermute | solution.py:219
  109.0 14.7 %collective-permute-start.11 = (bf16[64,3328]{1,0:T(8,128)(2,1)S(1)}, bf16[64,3328]{1,0:T(8,128)(2,1)S(1)}, u32[]{:S(2)}, u32[]{:S(2)}) collective-permute-start(bf16[64,3328]{1,0:T(8,128)(2,1)S(1)} %get-tuple-element.56), channel_id=1, source_target_pairs={{0,4},{4,0},{1,5},{5,1},{2,6},{6,2},{3,7},{7,3},{8,12},{12,8},{9,1... | collective-permute-start | bytes 1277960 | tf_op jit(solution)/shard_map/ppermute | solution.py:218
  114.0 27.8 %collective-permute-start.15 = (bf16[128,3328]{1,0:T(8,128)(2,1)S(1)}, bf16[128,3328]{1,0:T(8,128)(2,1)S(1)}, u32[]{:S(2)}, u32[]{:S(2)}) collective-permute-start(bf16[128,3328]{1,0:T(8,128)(2,1)S(1)} %get-tuple-element.63), channel_id=1, source_target_pairs={{0,3},{1,2},{2,1},{3,0},{4,7},{5,6},{6,5},{7,4},{8,11},{9,10},{10,... | collective-permute-start | bytes 2555912 | tf_op jit(solution)/shard_map/ppermute | solution.py:219
  123.7 11.8 %collective-permute-start.9 = (bf16[64,3328]{1,0:T(8,128)(2,1)S(1)}, bf16[64,3328]{1,0:T(8,128)(2,1)S(1)}, u32[]{:S(2)}, u32[]{:S(2)}) collective-permute-start(bf16[64,3328]{1,0:T(8,128)(2,1)S(1)} %get-tuple-element.54), channel_id=1, source_target_pairs={{0,1},{1,0},{2,3},{3,2},{4,5},{5,4},{6,7},{7,6},{8,9},{9,8},{10,11... | collective-permute-start | bytes 1277960 | tf_op jit(solution)/shard_map/ppermute | solution.py:219
  127.2 14.7 %collective-permute-start.14 = (bf16[64,3328]{1,0:T(8,128)(2,1)S(1)}, bf16[64,3328]{1,0:T(8,128)(2,1)S(1)}, u32[]{:S(2)}, u32[]{:S(2)}) collective-permute-start(bf16[64,3328]{1,0:T(8,128)(2,1)S(1)} %get-tuple-element.62), channel_id=1, source_target_pairs={{0,4},{4,0},{1,5},{5,1},{2,6},{6,2},{3,7},{7,3},{8,12},{12,8},{9,1... | collective-permute-start | bytes 1277960 | tf_op jit(solution)/shard_map/ppermute | solution.py:218
  127.3 19.1 %collective-permute-start.13 = (bf16[32,3328]{1,0:T(8,128)(2,1)S(1)}, bf16[32,3328]{1,0:T(8,128)(2,1)S(1)}, u32[]{:S(2)}, u32[]{:S(2)}) collective-permute-start(bf16[32,3328]{1,0:T(8,128)(2,1)S(1)} %get-tuple-element.61), channel_id=1, source_target_pairs={{0,3},{1,2},{2,1},{3,0},{4,7},{5,6},{6,5},{7,4},{8,11},{9,10},{10,... | collective-permute-start | bytes 638984 | tf_op jit(solution)/shard_map/ppermute | solution.py:219
  135.5 11.0 %collective-permute-start.12 = (bf16[32,3328]{1,0:T(8,128)(2,1)S(1)}, bf16[32,3328]{1,0:T(8,128)(2,1)S(1)}, u32[]{:S(2)}, u32[]{:S(2)}) collective-permute-start(bf16[32,3328]{1,0:T(8,128)(2,1)S(1)} %get-tuple-element.60), channel_id=1, source_target_pairs={{0,4},{4,0},{1,5},{5,1},{2,6},{6,2},{3,7},{7,3},{8,12},{12,8},{9,1... | collective-permute-start | bytes 638984 | tf_op jit(solution)/shard_map/ppermute | solution.py:218
  142.0 9.1 %collective-permute-start.17 = (bf16[32,3328]{1,0:T(8,128)(2,1)S(1)}, bf16[32,3328]{1,0:T(8,128)(2,1)S(1)}, u32[]{:S(2)}, u32[]{:S(2)}) collective-permute-start(bf16[32,3328]{1,0:T(8,128)(2,1)S(1)} %get-tuple-element.66), channel_id=1, source_target_pairs={{0,3},{1,2},{2,1},{3,0},{4,7},{5,6},{6,5},{7,4},{8,11},{9,10},{10,... | collective-permute-start | bytes 638984 | tf_op jit(solution)/shard_map/ppermute | solution.py:219
  142.6 12.1 %collective-permute-start.21 = (bf16[64,3328]{1,0:T(8,128)(2,1)S(1)}, bf16[64,3328]{1,0:T(8,128)(2,1)S(1)}, u32[]{:S(2)}, u32[]{:S(2)}) collective-permute-start(bf16[64,3328]{1,0:T(8,128)(2,1)S(1)} %get-tuple-element.67), channel_id=1, source_target_pairs={{0,4},{4,0},{1,5},{5,1},{2,6},{6,2},{3,7},{7,3},{8,12},{12,8},{9,1... | collective-permute-start | bytes 1277960 | tf_op jit(solution)/shard_map/ppermute | solution.py:218
  146.4 10.2 %collective-permute-start.20 = (bf16[32,1664]{1,0:T(8,128)(2,1)S(1)}, bf16[32,1664]{1,0:T(8,128)(2,1)S(1)}, u32[]{:S(2)}, u32[]{:S(2)}) collective-permute-start(bf16[32,1664]{1,0:T(8,128)(2,1)S(1)} %hidden.4.refs_2_.refs_0_), channel_id=1, source_target_pairs={{0,4},{4,0},{1,5},{5,1},{2,6},{6,2},{3,7},{7,3},{8,12},{12,8},{9,1... | collective-permute-start | bytes 319496 | tf_op jit(solution)/shard_map/ppermute | solution.py:218
  146.6 6.1 %collective-permute-start.16 = (bf16[32,1664]{1,0:T(8,128)(2,1)S(1)}, bf16[32,1664]{1,0:T(8,128)(2,1)S(1)}, u32[]{:S(2)}, u32[]{:S(2)}) collective-permute-start(bf16[32,1664]{1,0:T(8,128)(2,1)S(1)} %hidden.5.refs_2_.refs_0_), channel_id=1, source_target_pairs={{0,3},{1,2},{2,1},{3,0},{4,7},{5,6},{6,5},{7,4},{8,11},{9,10},{10,... | collective-permute-start | bytes 319496 | tf_op jit(solution)/shard_map/ppermute | solution.py:219
  151.2 9.3 %collective-permute-start.19 = (bf16[32,1664]{1,0:T(8,128)(2,1)S(1)}, bf16[32,1664]{1,0:T(8,128)(2,1)S(1)}, u32[]{:S(2)}, u32[]{:S(2)}) collective-permute-start(bf16[32,1664]{1,0:T(8,128)(2,1)S(1)} %hidden.6.refs_2_.refs_0_), channel_id=1, source_target_pairs={{0,1},{1,0},{2,3},{3,2},{4,5},{5,4},{6,7},{7,6},{8,9},{9,8},{10,11... | collective-permute-start | bytes 319496 | tf_op jit(solution)/shard_map/ppermute | solution.py:219
  152.7 8.4 %collective-permute-start.18 = (bf16[64,1664]{1,0:T(8,128)(2,1)S(1)}, bf16[64,1664]{1,0:T(8,128)(2,1)S(1)}, u32[]{:S(2)}, u32[]{:S(2)}) collective-permute-start(bf16[64,1664]{1,0:T(8,128)(2,1)S(1)} %join.8.refs_2_.refs_0_), channel_id=1, source_target_pairs={{0,4},{4,0},{1,5},{5,1},{2,6},{6,2},{3,7},{7,3},{8,12},{12,8},{9,1... | collective-permute-start | bytes 638984 | tf_op jit(solution)/shard_map/ppermute | solution.py:218
  154.8 6.5 %collective-permute-start.23 = (bf16[32,3328]{1,0:T(8,128)(2,1)S(1)}, bf16[32,3328]{1,0:T(8,128)(2,1)S(1)}, u32[]{:S(2)}, u32[]{:S(2)}) collective-permute-start(bf16[32,3328]{1,0:T(8,128)(2,1)S(1)} %get-tuple-element.70), channel_id=1, source_target_pairs={{0,1},{1,0},{2,3},{3,2},{4,5},{5,4},{6,7},{7,6},{8,9},{9,8},{10,11... | collective-permute-start | bytes 638984 | tf_op jit(solution)/shard_map/ppermute | solution.py:219
  156.6 8.7 %collective-permute-start.26 = (bf16[64,1664]{1,0:T(8,128)(2,1)S(1)}, bf16[64,1664]{1,0:T(8,128)(2,1)S(1)}, u32[]{:S(2)}, u32[]{:S(2)}) collective-permute-start(bf16[64,1664]{1,0:T(8,128)(2,1)S(1)} %join.9.refs_2_.refs_0_), channel_id=1, source_target_pairs={{0,3},{1,2},{2,1},{3,0},{4,7},{5,6},{6,5},{7,4},{8,11},{9,10},{10,... | collective-permute-start | bytes 638984 | tf_op jit(solution)/shard_map/ppermute | solution.py:219
  160.5 6.3 %collective-permute-start.25 = (bf16[64,1664]{1,0:T(8,128)(2,1)S(1)}, bf16[64,1664]{1,0:T(8,128)(2,1)S(1)}, u32[]{:S(2)}, u32[]{:S(2)}) collective-permute-start(bf16[64,1664]{1,0:T(8,128)(2,1)S(1)} %join.10.refs_2_.refs_0_), channel_id=1, source_target_pairs={{0,4},{4,0},{1,5},{5,1},{2,6},{6,2},{3,7},{7,3},{8,12},{12,8},{9,1... | collective-permute-start | bytes 638984 | tf_op jit(solution)/shard_map/ppermute | solution.py:218
  161.2 12.8 %collective-permute-start.22 = (bf16[128,1664]{1,0:T(8,128)(2,1)S(1)}, bf16[128,1664]{1,0:T(8,128)(2,1)S(1)}, u32[]{:S(2)}, u32[]{:S(2)}) collective-permute-start(bf16[128,1664]{1,0:T(8,128)(2,1)S(1)} %join.11.refs_2_.refs_0_), channel_id=1, source_target_pairs={{0,1},{1,0},{2,3},{3,2},{4,5},{5,4},{6,7},{7,6},{8,9},{9,8},{10,11... | collective-permute-start | bytes 1277960 | tf_op jit(solution)/shard_map/ppermute | solution.py:219
  161.4 7.5 %collective-permute-start.24 = (bf16[32,1664]{1,0:T(8,128)(2,1)S(1)}, bf16[32,1664]{1,0:T(8,128)(2,1)S(1)}, u32[]{:S(2)}, u32[]{:S(2)}) collective-permute-start(bf16[32,1664]{1,0:T(8,128)(2,1)S(1)} %hidden.7.refs_2_.refs_0_), channel_id=1, source_target_pairs={{0,3},{1,2},{2,1},{3,0},{4,7},{5,6},{6,5},{7,4},{8,11},{9,10},{10,... | collective-permute-start | bytes 319496 | tf_op jit(solution)/shard_map/ppermute | solution.py:219
  165.3 16.4 %collective-permute-start.33 = (bf16[128,1664]{1,0:T(8,128)(2,1)S(1)}, bf16[128,1664]{1,0:T(8,128)(2,1)S(1)}, u32[]{:S(2)}, u32[]{:S(2)}) collective-permute-start(bf16[128,1664]{1,0:T(8,128)(2,1)S(1)} %join.12.refs_2_.refs_0_), channel_id=1, source_target_pairs={{0,1},{1,0},{2,3},{3,2},{4,5},{5,4},{6,7},{7,6},{8,9},{9,8},{10,11... | collective-permute-start | bytes 1277960 | tf_op jit(solution)/shard_map/ppermute | solution.py:219
  166.8 10.9 %collective-permute-start.28 = (bf16[128,1664]{1,0:T(8,128)(2,1)S(1)}, bf16[128,1664]{1,0:T(8,128)(2,1)S(1)}, u32[]{:S(2)}, u32[]{:S(2)}) collective-permute-start(bf16[128,1664]{1,0:T(8,128)(2,1)S(1)} %join.13.refs_2_.refs_0_), channel_id=1, source_target_pairs={{0,3},{1,2},{2,1},{3,0},{4,7},{5,6},{6,5},{7,4},{8,11},{9,10},{10,... | collective-permute-start | bytes 1277960 | tf_op jit(solution)/shard_map/ppermute | solution.py:219
  169.0 8.5 %collective-permute-start.29 = (bf16[64,1664]{1,0:T(8,128)(2,1)S(1)}, bf16[64,1664]{1,0:T(8,128)(2,1)S(1)}, u32[]{:S(2)}, u32[]{:S(2)}) collective-permute-start(bf16[64,1664]{1,0:T(8,128)(2,1)S(1)} %join.14.refs_3_.refs_0_), channel_id=1, source_target_pairs={{0,4},{4,0},{1,5},{5,1},{2,6},{6,2},{3,7},{7,3},{8,12},{12,8},{9,1... | collective-permute-start | bytes 638984 | tf_op jit(solution)/shard_map/ppermute | solution.py:218
  177.4 4.2 %collective-permute-start.27 = (bf16[128,2048]{1,0:T(8,128)(2,1)S(1)}, bf16[128,2048]{1,0:T(8,128)(2,1)S(1)}, u32[]{:S(2)}, u32[]{:S(2)}) collective-permute-start(bf16[128,2048]{1,0:T(8,128)(2,1)S(1)} %get-tuple-element.72), channel_id=1, source_target_pairs={{0,8},{8,0},{1,9},{9,1},{2,10},{10,2},{3,11},{11,3},{4,12},{12,4},... | collective-permute-start | bytes 1572872 | tf_op jit(solution)/shard_map/ppermute | solution.py:159
  177.6 12.3 %collective-permute-start.37 = (bf16[128,1664]{1,0:T(8,128)(2,1)S(1)}, bf16[128,1664]{1,0:T(8,128)(2,1)S(1)}, u32[]{:S(2)}, u32[]{:S(2)}) collective-permute-start(bf16[128,1664]{1,0:T(8,128)(2,1)S(1)} %join.15.refs_3_.refs_0_), channel_id=1, source_target_pairs={{0,1},{1,0},{2,3},{3,2},{4,5},{5,4},{6,7},{7,6},{8,9},{9,8},{10,11... | collective-permute-start | bytes 1277960 | tf_op jit(solution)/shard_map/ppermute | solution.py:219
  181.1 7.7 %collective-permute-start.32 = (bf16[128,2048]{1,0:T(8,128)(2,1)S(1)}, bf16[128,2048]{1,0:T(8,128)(2,1)S(1)}, u32[]{:S(2)}, u32[]{:S(2)}) collective-permute-start(bf16[128,2048]{1,0:T(8,128)(2,1)S(1)} %get-tuple-element.74), channel_id=1, source_target_pairs={{0,8},{8,0},{1,9},{9,1},{2,10},{10,2},{3,11},{11,3},{4,12},{12,4},... | collective-permute-start | bytes 1572872 | tf_op jit(solution)/shard_map/ppermute | solution.py:159
  185.1 10.3 %collective-permute-start.36 = (bf16[128,2048]{1,0:T(8,128)(2,1)S(1)}, bf16[128,2048]{1,0:T(8,128)(2,1)S(1)}, u32[]{:S(2)}, u32[]{:S(2)}) collective-permute-start(bf16[128,2048]{1,0:T(8,128)(2,1)S(1)} %get-tuple-element.76), channel_id=1, source_target_pairs={{0,8},{8,0},{1,9},{9,1},{2,10},{10,2},{3,11},{11,3},{4,12},{12,4},... | collective-permute-start | bytes 1572872 | tf_op jit(solution)/shard_map/ppermute | solution.py:159
  185.4 12.9 %collective-permute-start.30 = (bf16[64,2048]{1,0:T(8,128)(2,1)S(1)}, bf16[64,2048]{1,0:T(8,128)(2,1)S(1)}, u32[]{:S(2)}, u32[]{:S(2)}) collective-permute-start(bf16[64,2048]{1,0:T(8,128)(2,1)S(1)} %get-tuple-element.86), channel_id=1, source_target_pairs={{0,48},{16,32},{32,80},{48,64},{64,112},{80,96},{96,16},{112,0},{1... | collective-permute-start | bytes 786440 | tf_op jit(solution)/shard_map/ppermute | solution.py:168
  188.6 14.5 %collective-permute-start.31 = (bf16[64,2048]{1,0:T(8,128)(2,1)S(1)}, bf16[64,2048]{1,0:T(8,128)(2,1)S(1)}, u32[]{:S(2)}, u32[]{:S(2)}) collective-permute-start(bf16[64,2048]{1,0:T(8,128)(2,1)S(1)} %get-tuple-element.85), channel_id=1, source_target_pairs={{0,32},{16,48},{32,64},{48,80},{64,96},{80,112},{96,0},{112,16},{1... | collective-permute-start | bytes 786440 | tf_op jit(solution)/shard_map/ppermute | solution.py:168
  193.3 3.2 %collective-permute-start.39 = (bf16[128,2048]{1,0:T(8,128)(2,1)S(1)}, bf16[128,2048]{1,0:T(8,128)(2,1)S(1)}, u32[]{:S(2)}, u32[]{:S(2)}) collective-permute-start(bf16[128,2048]{1,0:T(8,128)(2,1)S(1)} %get-tuple-element.78), channel_id=1, source_target_pairs={{0,8},{8,0},{1,9},{9,1},{2,10},{10,2},{3,11},{11,3},{4,12},{12,4},... | collective-permute-start | bytes 1572872 | tf_op jit(solution)/shard_map/ppermute | solution.py:159
  193.4 12.8 %collective-permute-start.34 = (bf16[64,2048]{1,0:T(8,128)(2,1)S(1)}, bf16[64,2048]{1,0:T(8,128)(2,1)S(1)}, u32[]{:S(2)}, u32[]{:S(2)}) collective-permute-start(bf16[64,2048]{1,0:T(8,128)(2,1)S(1)} %get-tuple-element.84), channel_id=1, source_target_pairs={{0,112},{16,96},{32,16},{48,0},{64,48},{80,32},{96,80},{112,64},{1... | collective-permute-start | bytes 786440 | tf_op jit(solution)/shard_map/ppermute | solution.py:168
  195.4 15.4 %collective-permute-start.35 = (bf16[64,2048]{1,0:T(8,128)(2,1)S(1)}, bf16[64,2048]{1,0:T(8,128)(2,1)S(1)}, u32[]{:S(2)}, u32[]{:S(2)}) collective-permute-start(bf16[64,2048]{1,0:T(8,128)(2,1)S(1)} %get-tuple-element.83), channel_id=1, source_target_pairs={{0,96},{16,112},{32,0},{48,16},{64,32},{80,48},{96,64},{112,80},{1... | collective-permute-start | bytes 786440 | tf_op jit(solution)/shard_map/ppermute | solution.py:168
  196.5 15.3 %collective-permute-start.38 = (bf16[64,2048]{1,0:T(8,128)(2,1)S(1)}, bf16[64,2048]{1,0:T(8,128)(2,1)S(1)}, u32[]{:S(2)}, u32[]{:S(2)}) collective-permute-start(bf16[64,2048]{1,0:T(8,128)(2,1)S(1)} %select_convert_fusion.2), channel_id=1, source_target_pairs={{0,16},{16,0},{32,48},{48,32},{64,80},{80,64},{96,112},{112,96},{1... | collective-permute-start | bytes 786440 | tf_op jit(solution)/shard_map/ppermute | solution.py:168
  198.3 19.2 %collective-permute-start.40 = (bf16[64,2048]{1,0:T(8,128)(2,1)S(1)}, bf16[64,2048]{1,0:T(8,128)(2,1)S(1)}, u32[]{:S(2)}, u32[]{:S(2)}) collective-permute-start(bf16[64,2048]{1,0:T(8,128)(2,1)S(1)} %get-tuple-element.82), channel_id=1, source_target_pairs={{0,80},{16,64},{32,112},{48,96},{64,16},{80,0},{96,48},{112,32},{1... | collective-permute-start | bytes 786440 | tf_op jit(solution)/shard_map/ppermute | solution.py:168
  203.1 18.7 %collective-permute-start.41 = (bf16[64,2048]{1,0:T(8,128)(2,1)S(1)}, bf16[64,2048]{1,0:T(8,128)(2,1)S(1)}, u32[]{:S(2)}, u32[]{:S(2)}) collective-permute-start(bf16[64,2048]{1,0:T(8,128)(2,1)S(1)} %get-tuple-element.81), channel_id=1, source_target_pairs={{0,64},{16,80},{32,96},{48,112},{64,0},{80,16},{96,32},{112,48},{1... | collective-permute-start | bytes 786440 | tf_op jit(solution)/shard_map/ppermute | solution.py:168
  203.4 18.6 %copy-start.13 = (f32[2,64,2048]{2,1,0:T(8,128)S(1)}, f32[2,64,2048]{2,1,0:T(8,128)}, u32[]{:S(2)}) copy-start(f32[2,64,2048]{2,1,0:T(8,128)} %slice_convert_fusion) | copy-start | bytes 3145732
  (16 other events, 55.1 us)

commit v4 on v3

--- a/solution.py
+++ b/solution.py
@@ -37,9 +37,7 @@
             def _():
                 pltpu.make_async_copy(arrived.at[page - resident], place, sems.at[t]).start()
 
-    @pl.loop(0, row_count)
-    def _(t):
-        pltpu.make_async_copy(store.at[t], store.at[t], sems.at[t]).wait()
+    def attend_row(t):
         scores = jnp.concatenate(
             [
                 lax.dot_general(
@@ -59,6 +57,13 @@
         for k in range(KVH):
             rows = slice(k * heads, (k + 1) * heads)
             out[t, rows, :] = dot(probs[rows], store[t, 1, :, k * HD : (k + 1) * HD])
+
+    @pl.loop(0, row_count // 4)
+    def _(i):
+        for t in range(4):
+            pltpu.make_async_copy(store.at[i * 4 + t], store.at[i * 4 + t], sems.at[i * 4 + t]).wait()
+        for t in range(4):
+            attend_row(i * 4 + t)
 
 
 def attend(tokens, queries, page_pool, new_pages, page_table, block_table, context, after):

time: 225 us -> 224 us (level)
  no operation moved by 1% of the time
where the time goes in v4:
time: 224 us; the launch traced here: 222 us
  waiting for transfers between devices  87.1 us (39%)
  starting transfers between devices  55.3 us (25%)
  Pallas kernels  44.5 us (20%)
  local copies, waits for them, and re-layouts  28.9 us (13%)
  other arithmetic  5.72 us (3%)
    ppermute x16, waiting for transfers between devices, exchange(): return lax.ppermute(a, 'x', [(i, i ^ mask) for i in range(4)])  45.2 us
    pallas_call x38, Pallas kernels, call(): pl.pallas_call(lambda *refs: kernel(*refs[:count], *refs[count + len(afte...  35.3 us
    unnamed x41, local copies, waits for them, and re-layouts  25.8 us
    ppermute x7, waiting for transfers between devices, home(): return lax.ppermute(a, CHIPS, pairs)  18.3 us
    ppermute x16, starting transfers between devices, exchange(): return lax.ppermute(a, 'x', [(i, i ^ mask) for i in range(4)])  16.9 us
    ppermute x7, starting transfers between devices, home(): return lax.ppermute(a, CHIPS, pairs)  13.3 us
    all_to_all x1, waiting for transfers between devices, spread(): lax.all_to_all(payload, near, split_axis=1, concat_axis=0, tiled=True)  11.2 us
    all_to_all x1, waiting for transfers between devices, attend(): lax.all_to_all(new_pages[holder], GX, split_axis=0, concat_axis=0, tiled=...  8.35 us
  transfers between devices with their start and end apart: 44, of which 22 were waited for; matrix products, arithmetic and copies ran while one was open for 1% of the time, Pallas kernels for 16%

profile of v4, /device:TPU:24, one launch (start us, length us, event | category | flops | bytes accessed | tf_op | source)
XLA Modules:
  0.0 222.3 jit_solution(8518783681752624478)
XLA Ops:
  1.4 2.1 gather_fusion
  3.5 8.2 %all-to-all-start = ((bf16[32,2,16,1024]{3,2,1,0:T(8,128)(2,1)}), bf16[32,2,16,1024]{3,2,1,0:T(8,128)(2,1)S(1)}, u32[]{:S(2)}, u32[]{:S(2)}) async-start(bf16[32,2,16,1024]{3,2,1,0:T(8,128)(2,1)} %gather_fusion), calls=%async_computation | async-start | bytes 4194304 | tf_op jit(solution)/shard_map/all_to_all | solution.py:74
  11.8 2.9 %copy-done.2 = bf16[2048,1664]{1,0:T(8,128)(2,1)S(1)} copy-done((bf16[2048,1664]{1,0:T(8,128)(2,1)S(1)}, bf16[2048,1664]{1,0:T(8,128)(2,1)}, u32[]{:S(2)}) %copy-start.2) | copy-done | bytes 6815768
  14.7 2.9 %copy-done.3 = bf16[2048,1664]{1,0:T(8,128)(2,1)S(1)} copy-done((bf16[2048,1664]{1,0:T(8,128)(2,1)S(1)}, bf16[2048,1664]{1,0:T(8,128)(2,1)}, u32[]{:S(2)}) %copy-start.3) | copy-done | bytes 6815768
  17.6 2.9 %copy-done.4 = bf16[1664,2048]{1,0:T(8,128)(2,1)S(1)} copy-done((bf16[1664,2048]{1,0:T(8,128)(2,1)S(1)}, bf16[1664,2048]{1,0:T(8,128)(2,1)}, u32[]{:S(2)}) %copy-start.4) | copy-done | bytes 6815768
  22.0 2.7 %copy-done.8 = bf16[1664,2048]{1,0:T(8,128)(2,1)} copy-done((bf16[1664,2048]{1,0:T(8,128)(2,1)}, bf16[1664,2048]{1,0:T(8,128)(2,1)S(1)}, u32[]{:S(2)}) %copy-start.8) | copy-done | bytes 6815768
  24.7 2.8 %copy-done.9 = bf16[2048,1664]{1,0:T(8,128)(2,1)} copy-done((bf16[2048,1664]{1,0:T(8,128)(2,1)}, bf16[2048,1664]{1,0:T(8,128)(2,1)S(1)}, u32[]{:S(2)}) %copy-start.9) | copy-done | bytes 6815768
  27.6 2.7 %copy-done.11 = bf16[2048,1664]{1,0:T(8,128)(2,1)} copy-done((bf16[2048,1664]{1,0:T(8,128)(2,1)}, bf16[2048,1664]{1,0:T(8,128)(2,1)S(1)}, u32[]{:S(2)}) %copy-start.11) | copy-done | bytes 6815768
  30.3 8.4 %all-to-all-done.arrived = bf16[32,2,16,1024]{3,2,1,0:T(8,128)(2,1)S(1)} async-done(((bf16[32,2,16,1024]{3,2,1,0:T(8,128)(2,1)}), bf16[32,2,16,1024]{3,2,1,0:T(8,128)(2,1)S(1)}, u32[]{:S(2)}, u32[]{:S(2)}) %all-to-all-start) | async-done | bytes 2097184 | tf_op jit(solution)/shard_map/all_to_all | solution.py:74
  38.7 1.6 copy-done.5
  40.3 7.8 %attend.2 = f32[8,128,128]{2,1,0:T(8,128)S(1)} custom-call(s32[8,8]{1,0:T(8,128)S(1)} %copy-done.6, s32[8]{0:T(128)S(1)} %copy-done.7, bf16[8,128,128]{2,1,0:T(8,128)(2,1)S(1)} %bitcast.54, bf16[32,2,16,1024]{3,2,1,0:T(8,128)(2,1)S(1)} %copy-done.5, bf16[32,2,16,1024]{3,2,1,0:T(8,128)(2,1)S(1)} %all-to-all-done.arrived, f32[8,128]{1,0:T(8,128)S(1)} %get-tuple-element.43._), custom_call_target="tpu_custom_call" | custom-call | flops 134217728 | bytes 8388608 | tf_op jit(solution)/shard_map/attend/pallas_call | solution.py:78
  49.8 4.9 %all-to-all-start.1 = ((bf16[8,16,2176]{2,0,1:T(8,128)(2,1)}), bf16[8,16,2176]{2,0,1:T(8,128)(2,1)S(1)}, u32[]{:S(2)}, u32[]{:S(2)}) async-start(bf16[8,16,2176]{2,0,1:T(8,128)(2,1)} %maximum_maximum_fusion), calls=%async_computation.1 | async-start | bytes 1114112 | tf_op jit(solution)/shard_map/all_to_all | solution.py:114
  55.4 11.2 %all-to-all-done.1 = bf16[8,16,2176]{2,0,1:T(8,128)(2,1)S(1)} async-done(((bf16[8,16,2176]{2,0,1:T(8,128)(2,1)}), bf16[8,16,2176]{2,0,1:T(8,128)(2,1)S(1)}, u32[]{:S(2)}, u32[]{:S(2)}) %all-to-all-start.1) | async-done | bytes 557088 | tf_op jit(solution)/shard_map/all_to_all | solution.py:114
  67.5 3.4 %collective-permute-start = (bf16[128,2048]{1,0:T(8,128)(2,1)S(1)}, bf16[128,2048]{1,0:T(8,128)(2,1)S(1)}, u32[]{:S(2)}, u32[]{:S(2)}) collective-permute-start(bf16[128,2048]{1,0:T(8,128)(2,1)S(1)} %bitcast_dynamic-update-slice_fusion.refs_0_), channel_id=1, source_target_pairs={{0,96},{32,0},{64,32},{96,64},{1,97},{33,1},{65,33},{97,65},{2,98}... | collective-permute-start | bytes 1572872 | tf_op jit(solution)/shard_map/ppermute | solution.py:168
  73.3 2.9 %copy-done.10 = bf16[2048,1664]{1,0:T(8,128)(2,1)S(1)} copy-done((bf16[2048,1664]{1,0:T(8,128)(2,1)S(1)}, bf16[2048,1664]{1,0:T(8,128)(2,1)}, u32[]{:S(2)}) %copy-start.10) | copy-done | bytes 6815768
  76.3 2.9 %copy-done.12 = bf16[2048,1664]{1,0:T(8,128)(2,1)S(1)} copy-done((bf16[2048,1664]{1,0:T(8,128)(2,1)S(1)}, bf16[2048,1664]{1,0:T(8,128)(2,1)}, u32[]{:S(2)}) %copy-start.12) | copy-done | bytes 6815768
  79.2 4.9 %up.4 = (f32[128,3328]{1,0:T(8,128)S(1)}, bf16[128,3328]{1,0:T(8,128)(2,1)S(1)}) custom-call(bf16[128,2048]{1,0:T(8,128)(2,1)S(1)} %piece.4.refs_0_.refs_4_, bf16[128,2048]{1,0:T(8,128)(2,1)S(1)} %collective-permute-done.1.refs_1_, bf16[2048,1664]{1,0:T(8,128)(2,1)S(1)} %copy-done.10, bf16[2048,1664]{1,0:T(8,128)(2,1)S(1)} %copy-done.12, ...), custom_call_target="tpu_custom_call" | custom-call | flops 17179869184 | bytes 1024 | tf_op jit(solution)/shard_map/up/pallas_call | solution.py:179
  84.2 1.5 collective-permute-start.5
  88.7 4.9 %up.5 = (f32[128,3328]{1,0:T(8,128)S(1)}, bf16[128,3328]{1,0:T(8,128)(2,1)S(1)}) custom-call(bf16[128,2048]{1,0:T(8,128)(2,1)S(1)} %piece.5.refs_1_.refs_0_, bf16[128,2048]{1,0:T(8,128)(2,1)S(1)} %collective-permute-done.2.refs_1_, bf16[2048,1664]{1,0:T(8,128)(2,1)S(1)} %bitcast.58, bf16[2048,1664]{1,0:T(8,128)(2,1)S(1)} %copy-done.12, ...), custom_call_target="tpu_custom_call" | custom-call | flops 17179869184 | bytes 1024 | tf_op jit(solution)/shard_map/up/pallas_call | solution.py:179
  93.5 4.9 %up.6 = (f32[128,3328]{1,0:T(8,128)S(1)}, bf16[128,3328]{1,0:T(8,128)(2,1)S(1)}) custom-call(bf16[128,2048]{1,0:T(8,128)(2,1)S(1)} %piece.6.refs_4_.refs_0_, bf16[128,2048]{1,0:T(8,128)(2,1)S(1)} %collective-permute-done.6.refs_1_, bf16[2048,1664]{1,0:T(8,128)(2,1)S(1)} %bitcast.58, bf16[2048,1664]{1,0:T(8,128)(2,1)S(1)} %copy-done.12, ...), custom_call_target="tpu_custom_call" | custom-call | flops 17179869184 | bytes 1024 | tf_op jit(solution)/shard_map/up/pallas_call | solution.py:179
  100.6 7.6 %collective-permute-done.8.refs_1_ = bf16[128,3328]{1,0:T(8,128)(2,1)S(1)} collective-permute-done((bf16[128,3328]{1,0:T(8,128)(2,1)S(1)}, bf16[128,3328]{1,0:T(8,128)(2,1)S(1)}, u32[]{:S(2)}, u32[]{:S(2)}) %collective-permute-start.8) | collective-permute-done | bytes 852000 | tf_op jit(solution)/shard_map/ppermute | solution.py:224
  108.4 4.9 %up.7 = (f32[128,3328]{1,0:T(8,128)S(1)}, bf16[128,3328]{1,0:T(8,128)(2,1)S(1)}) custom-call(bf16[128,2048]{1,0:T(8,128)(2,1)S(1)} %piece.7.refs_2_.refs_0_, bf16[128,2048]{1,0:T(8,128)(2,1)S(1)} %collective-permute-done.7.refs_1_, bf16[2048,1664]{1,0:T(8,128)(2,1)S(1)} %bitcast.58, bf16[2048,1664]{1,0:T(8,128)(2,1)S(1)} %copy-done.12, ...), custom_call_target="tpu_custom_call" | custom-call | flops 17179869184 | bytes 1024 | tf_op jit(solution)/shard_map/up/pallas_call | solution.py:179
  114.5 8.3 %collective-permute-done.4.refs_1_ = bf16[128,3328]{1,0:T(8,128)(2,1)S(1)} collective-permute-done((bf16[128,3328]{1,0:T(8,128)(2,1)S(1)}, bf16[128,3328]{1,0:T(8,128)(2,1)S(1)}, u32[]{:S(2)}, u32[]{:S(2)}) %collective-permute-start.4) | collective-permute-done | bytes 852000 | tf_op jit(solution)/shard_map/ppermute | solution.py:224
  123.1 3.2 %collective-permute-done.10.refs_1_ = bf16[128,3328]{1,0:T(8,128)(2,1)S(1)} collective-permute-done((bf16[128,3328]{1,0:T(8,128)(2,1)S(1)}, bf16[128,3328]{1,0:T(8,128)(2,1)S(1)}, u32[]{:S(2)}, u32[]{:S(2)}) %collective-permute-start.10) | collective-permute-done | bytes 852000 | tf_op jit(solution)/shard_map/ppermute | solution.py:224
  127.7 7.0 %collective-permute-done.9.refs_1_ = bf16[64,3328]{1,0:T(8,128)(2,1)S(1)} collective-permute-done((bf16[64,3328]{1,0:T(8,128)(2,1)S(1)}, bf16[64,3328]{1,0:T(8,128)(2,1)S(1)}, u32[]{:S(2)}, u32[]{:S(2)}) %collective-permute-start.9) | collective-permute-done | bytes 426016 | tf_op jit(solution)/shard_map/ppermute | solution.py:224
  135.1 6.0 %collective-permute-done.15.refs_1_ = bf16[128,3328]{1,0:T(8,128)(2,1)S(1)} collective-permute-done((bf16[128,3328]{1,0:T(8,128)(2,1)S(1)}, bf16[128,3328]{1,0:T(8,128)(2,1)S(1)}, u32[]{:S(2)}, u32[]{:S(2)}) %collective-permute-start.15) | collective-permute-done | bytes 852000 | tf_op jit(solution)/shard_map/ppermute | solution.py:224
  142.5 3.1 %collective-permute-done.13.refs_1_ = bf16[32,3328]{1,0:T(8,128)(2,1)S(1)} collective-permute-done((bf16[32,3328]{1,0:T(8,128)(2,1)S(1)}, bf16[32,3328]{1,0:T(8,128)(2,1)S(1)}, u32[]{:S(2)}, u32[]{:S(2)}) %collective-permute-start.13) | collective-permute-done | bytes 213024 | tf_op jit(solution)/shard_map/ppermute | solution.py:224
  147.1 3.3 %collective-permute-done.17.refs_1_ = bf16[32,3328]{1,0:T(8,128)(2,1)S(1)} collective-permute-done((bf16[32,3328]{1,0:T(8,128)(2,1)S(1)}, bf16[32,3328]{1,0:T(8,128)(2,1)S(1)}, u32[]{:S(2)}, u32[]{:S(2)}) %collective-permute-start.17) | collective-permute-done | bytes 213024 | tf_op jit(solution)/shard_map/ppermute | solution.py:224
  150.6 1.4 collective-permute-done.16.refs_1_
  152.0 2.0 collective-permute-start.18
  154.2 1.6 collective-permute-done.20.refs_1_
  155.9 3.9 %collective-permute-start.26 = (bf16[64,1664]{1,0:T(8,128)(2,1)S(1)}, bf16[64,1664]{1,0:T(8,128)(2,1)S(1)}, u32[]{:S(2)}, u32[]{:S(2)}) collective-permute-start(bf16[64,1664]{1,0:T(8,128)(2,1)S(1)} %join.9.refs_2_.refs_0_), channel_id=1, source_target_pairs={{0,3},{1,2},{2,1},{3,0},{4,7},{5,6},{6,5},{7,4},{8,11},{9,10},{10,... | collective-permute-start | bytes 638984 | tf_op jit(solution)/shard_map/ppermute | solution.py:224
  160.6 3.9 %collective-permute-start.24 = (bf16[32,1664]{1,0:T(8,128)(2,1)S(1)}, bf16[32,1664]{1,0:T(8,128)(2,1)S(1)}, u32[]{:S(2)}, u32[]{:S(2)}) collective-permute-start(bf16[32,1664]{1,0:T(8,128)(2,1)S(1)} %hidden.7.refs_2_.refs_0_), channel_id=1, source_target_pairs={{0,3},{1,2},{2,1},{3,0},{4,7},{5,6},{6,5},{7,4},{8,11},{9,10},{10,... | collective-permute-start | bytes 319496 | tf_op jit(solution)/shard_map/ppermute | solution.py:224
  164.6 1.4 collective-permute-start.33
  166.1 1.8 collective-permute-start.28
  169.3 3.9 %collective-permute-done.22.refs_1_ = bf16[128,1664]{1,0:T(8,128)(2,1)S(1)} collective-permute-done((bf16[128,1664]{1,0:T(8,128)(2,1)S(1)}, bf16[128,1664]{1,0:T(8,128)(2,1)S(1)}, u32[]{:S(2)}, u32[]{:S(2)}) %collective-permute-start.22) | collective-permute-done | bytes 426016 | tf_op jit(solution)/shard_map/ppermute | solution.py:224
  173.3 3.4 %down.4 = (f32[128,2048]{1,0:T(8,128)S(1)}, bf16[128,2048]{1,0:T(8,128)(2,1)S(1)}) custom-call(bf16[128,1664]{1,0:T(8,128)(2,1)S(1)} %join.11.refs_2_.refs_0_, bf16[128,1664]{1,0:T(8,128)(2,1)S(1)} %collective-permute-done.22.refs_1_, bf16[1664,2048]{1,0:T(8,128)(2,1)S(1)} %bitcast.56, bf16[64,1664]{1,0:T(8,128)(2,1)S(1)} %join.14.refs_3_.refs_0_), custom_call_target="tpu_custom_call" | custom-call | flops 17179869184 | bytes 1024 | tf_op jit(solution)/shard_map/down/pallas_call | solution.py:179
  176.9 3.4 %down.5 = (f32[128,2048]{1,0:T(8,128)S(1)}, bf16[128,2048]{1,0:T(8,128)(2,1)S(1)}) custom-call(bf16[128,1664]{1,0:T(8,128)(2,1)S(1)} %join.13.refs_2_.refs_0_, bf16[128,1664]{1,0:T(8,128)(2,1)S(1)} %collective-permute-done.28.refs_1_, bf16[1664,2048]{1,0:T(8,128)(2,1)S(1)} %bitcast.56, bf16[128,1664]{1,0:T(8,128)(2,1)S(1)} %join.15.refs_3_.refs_0_), custom_call_target="tpu_custom_call" | custom-call | flops 17179869184 | bytes 1024 | tf_op jit(solution)/shard_map/down/pallas_call | solution.py:179
  181.0 3.4 %down.6 = (f32[128,2048]{1,0:T(8,128)S(1)}, bf16[128,2048]{1,0:T(8,128)(2,1)S(1)}) custom-call(bf16[128,1664]{1,0:T(8,128)(2,1)S(1)} %join.12.refs_2_.refs_0_, bf16[128,1664]{1,0:T(8,128)(2,1)S(1)} %collective-permute-done.33.refs_1_, bf16[1664,2048]{1,0:T(8,128)(2,1)S(1)} %bitcast.56, f32[128,2048]{1,0:T(8,128)S(1)} %fold.4.refs_3_), custom_call_target="tpu_custom_call" | custom-call | flops 17179869184 | bytes 1024 | tf_op jit(solution)/shard_map/down/pallas_call | solution.py:179
  184.5 3.3 %collective-permute-start.30 = (bf16[64,2048]{1,0:T(8,128)(2,1)S(1)}, bf16[64,2048]{1,0:T(8,128)(2,1)S(1)}, u32[]{:S(2)}, u32[]{:S(2)}) collective-permute-start(bf16[64,2048]{1,0:T(8,128)(2,1)S(1)} %get-tuple-element.86), channel_id=1, source_target_pairs={{0,48},{16,32},{32,80},{48,64},{64,112},{80,96},{96,16},{112,0},{1... | collective-permute-start | bytes 786440 | tf_op jit(solution)/shard_map/ppermute | solution.py:173
  189.1 3.4 %down.7 = (f32[128,2048]{1,0:T(8,128)S(1)}, bf16[128,2048]{1,0:T(8,128)(2,1)S(1)}) custom-call(bf16[128,1664]{1,0:T(8,128)(2,1)S(1)} %join.15.refs_3_.refs_0_, bf16[128,1664]{1,0:T(8,128)(2,1)S(1)} %collective-permute-done.37.refs_1_, bf16[1664,2048]{1,0:T(8,128)(2,1)S(1)} %bitcast.56, f32[128,2048]{1,0:T(8,128)S(1)} %fold.5.refs_3_), custom_call_target="tpu_custom_call" | custom-call | flops 17179869184 | bytes 1024 | tf_op jit(solution)/shard_map/down/pallas_call | solution.py:179
  192.6 2.0 collective-permute-start.34
  195.8 1.6 collective-permute-start.38
  197.6 4.8 %collective-permute-start.40 = (bf16[64,2048]{1,0:T(8,128)(2,1)S(1)}, bf16[64,2048]{1,0:T(8,128)(2,1)S(1)}, u32[]{:S(2)}, u32[]{:S(2)}) collective-permute-start(bf16[64,2048]{1,0:T(8,128)(2,1)S(1)} %get-tuple-element.82), channel_id=1, source_target_pairs={{0,80},{16,64},{32,112},{48,96},{64,16},{80,0},{96,48},{112,32},{1... | collective-permute-start | bytes 786440 | tf_op jit(solution)/shard_map/ppermute | solution.py:173
  202.7 2.8 %collective-permute-done.34.refs_2_ = bf16[64,2048]{1,0:T(8,128)(2,1)S(1)} collective-permute-done((bf16[64,2048]{1,0:T(8,128)(2,1)S(1)}, bf16[64,2048]{1,0:T(8,128)(2,1)S(1)}, u32[]{:S(2)}, u32[]{:S(2)}) %collective-permute-start.34) | collective-permute-done | bytes 262176 | tf_op jit(solution)/shard_map/ppermute | solution.py:173
  205.5 4.7 %collective-permute-done.35.refs_3_ = bf16[64,2048]{1,0:T(8,128)(2,1)S(1)} collective-permute-done((bf16[64,2048]{1,0:T(8,128)(2,1)S(1)}, bf16[64,2048]{1,0:T(8,128)(2,1)S(1)}, u32[]{:S(2)}, u32[]{:S(2)}) %collective-permute-start.35) | collective-permute-done | bytes 262176 | tf_op jit(solution)/shard_map/ppermute | solution.py:173
  211.0 5.7 %collective-permute-done.40.refs_6_ = bf16[64,2048]{1,0:T(8,128)(2,1)S(1)} collective-permute-done((bf16[64,2048]{1,0:T(8,128)(2,1)S(1)}, bf16[64,2048]{1,0:T(8,128)(2,1)S(1)}, u32[]{:S(2)}, u32[]{:S(2)}) %collective-permute-start.40) | collective-permute-done | bytes 262176 | tf_op jit(solution)/shard_map/ppermute | solution.py:173
  216.7 4.3 %collective-permute-done.41.refs_7_ = bf16[64,2048]{1,0:T(8,128)(2,1)S(1)} collective-permute-done((bf16[64,2048]{1,0:T(8,128)(2,1)S(1)}, bf16[64,2048]{1,0:T(8,128)(2,1)S(1)}, u32[]{:S(2)}, u32[]{:S(2)}) %collective-permute-start.41) | collective-permute-done | bytes 262176 | tf_op jit(solution)/shard_map/ppermute | solution.py:173
  (159 shorter events, 28.8 us)
Async XLA Ops:
  3.5 8.2 %copy-start.14 = (bf16[8,16384]{1,0:T(8,128)(2,1)S(1)}, bf16[8,16384]{1,0:T(8,128)(2,1)}, u32[]{:S(2)}) copy-start(bf16[8,16384]{1,0:T(8,128)(2,1)} %param.12) | copy-start | bytes 786436
  3.5 35.2 %all-to-all-start = ((bf16[32,2,16,1024]{3,2,1,0:T(8,128)(2,1)}), bf16[32,2,16,1024]{3,2,1,0:T(8,128)(2,1)S(1)}, u32[]{:S(2)}, u32[]{:S(2)}) async-start(bf16[32,2,16,1024]{3,2,1,0:T(8,128)(2,1)} %gather_fusion), calls=%async_computation | async-start | bytes 4194304 | tf_op jit(solution)/shard_map/all_to_all | solution.py:74
  20.6 18.1 %copy-start.6 = (s32[8,8]{1,0:T(8,128)S(1)}, s32[8,8]{1,0:T(8,128)}, u32[]{:S(2)}) copy-start(s32[8,8]{1,0:T(8,128)} %table.1) | copy-start | bytes 772
  20.6 18.1 %copy-start.7 = (s32[8]{0:T(128)S(1)}, s32[8]{0:T(128)}, u32[]{:S(2)}) copy-start(s32[8]{0:T(128)} %context.1) | copy-start | bytes 100
  49.8 16.8 %all-to-all-start.1 = ((bf16[8,16,2176]{2,0,1:T(8,128)(2,1)}), bf16[8,16,2176]{2,0,1:T(8,128)(2,1)S(1)}, u32[]{:S(2)}, u32[]{:S(2)}) async-start(bf16[8,16,2176]{2,0,1:T(8,128)(2,1)} %maximum_maximum_fusion), calls=%async_computation.1 | async-start | bytes 1114112 | tf_op jit(solution)/shard_map/all_to_all | solution.py:114
  67.4 5.9 %collective-permute-start.1 = (bf16[128,2048]{1,0:T(8,128)(2,1)S(1)}, bf16[128,2048]{1,0:T(8,128)(2,1)S(1)}, u32[]{:S(2)}, u32[]{:S(2)}) collective-permute-start(bf16[128,2048]{1,0:T(8,128)(2,1)S(1)} %piece.4.refs_0_.refs_4_), channel_id=1, source_target_pairs={{0,8},{8,0},{1,9},{9,1},{2,10},{10,2},{3,11},{11,3},{4,12},{12,4},... | collective-permute-start | bytes 1572872 | tf_op jit(solution)/shard_map/ppermute | solution.py:164
  67.5 18.2 %collective-permute-start = (bf16[128,2048]{1,0:T(8,128)(2,1)S(1)}, bf16[128,2048]{1,0:T(8,128)(2,1)S(1)}, u32[]{:S(2)}, u32[]{:S(2)}) collective-permute-start(bf16[128,2048]{1,0:T(8,128)(2,1)S(1)} %bitcast_dynamic-update-slice_fusion.refs_0_), channel_id=1, source_target_pairs={{0,96},{32,0},{64,32},{96,64},{1,97},{33,1},{65,33},{97,65},{2,98}... | collective-permute-start | bytes 1572872 | tf_op jit(solution)/shard_map/ppermute | solution.py:168
  70.8 14.9 %collective-permute-start.3 = (bf16[128,2048]{1,0:T(8,128)(2,1)S(1)}, bf16[128,2048]{1,0:T(8,128)(2,1)S(1)}, u32[]{:S(2)}, u32[]{:S(2)}) collective-permute-start(bf16[128,2048]{1,0:T(8,128)(2,1)S(1)} %bitcast_dynamic-update-slice_fusion.refs_0_), channel_id=1, source_target_pairs={{0,32},{32,64},{64,96},{96,0},{1,33},{33,65},{65,97},{97,1},{2,34}... | collective-permute-start | bytes 1572872 | tf_op jit(solution)/shard_map/ppermute | solution.py:168
  84.2 15.5 %collective-permute-start.5 = (bf16[128,2048]{1,0:T(8,128)(2,1)S(1)}, bf16[128,2048]{1,0:T(8,128)(2,1)S(1)}, u32[]{:S(2)}, u32[]{:S(2)}) collective-permute-start(bf16[128,2048]{1,0:T(8,128)(2,1)S(1)} %far.1.refs_1_), channel_id=1, source_target_pairs={{0,64},{32,96},{64,0},{96,32},{1,65},{33,97},{65,1},{97,33},{2,66}... | collective-permute-start | bytes 1572872 | tf_op jit(solution)/shard_map/ppermute | solution.py:168
  85.7 2.0 collective-permute-start.2
  85.8 7.7 %collective-permute-start.6 = (bf16[128,2048]{1,0:T(8,128)(2,1)S(1)}, bf16[128,2048]{1,0:T(8,128)(2,1)S(1)}, u32[]{:S(2)}, u32[]{:S(2)}) collective-permute-start(bf16[128,2048]{1,0:T(8,128)(2,1)S(1)} %piece.6.refs_4_.refs_0_), channel_id=1, source_target_pairs={{0,8},{8,0},{1,9},{9,1},{2,10},{10,2},{3,11},{11,3},{4,12},{12,4},... | collective-permute-start | bytes 1572872 | tf_op jit(solution)/shard_map/ppermute | solution.py:164
  86.4 21.8 %collective-permute-start.8 = (bf16[128,3328]{1,0:T(8,128)(2,1)S(1)}, bf16[128,3328]{1,0:T(8,128)(2,1)S(1)}, u32[]{:S(2)}, u32[]{:S(2)}) collective-permute-start(bf16[128,3328]{1,0:T(8,128)(2,1)S(1)} %get-tuple-element.50), channel_id=1, source_target_pairs={{0,1},{1,0},{2,3},{3,2},{4,5},{5,4},{6,7},{7,6},{8,9},{9,8},{10,11... | collective-permute-start | bytes 2555912 | tf_op jit(solution)/shard_map/ppermute | solution.py:224
  99.7 8.8 %collective-permute-start.7 = (bf16[128,2048]{1,0:T(8,128)(2,1)S(1)}, bf16[128,2048]{1,0:T(8,128)(2,1)S(1)}, u32[]{:S(2)}, u32[]{:S(2)}) collective-permute-start(bf16[128,2048]{1,0:T(8,128)(2,1)S(1)} %piece.7.refs_2_.refs_0_), channel_id=1, source_target_pairs={{0,8},{8,0},{1,9},{9,1},{2,10},{10,2},{3,11},{11,3},{4,12},{12,4},... | collective-permute-start | bytes 1572872 | tf_op jit(solution)/shard_map/ppermute | solution.py:164
  99.8 23.0 %collective-permute-start.4 = (bf16[128,3328]{1,0:T(8,128)(2,1)S(1)}, bf16[128,3328]{1,0:T(8,128)(2,1)S(1)}, u32[]{:S(2)}, u32[]{:S(2)}) collective-permute-start(bf16[128,3328]{1,0:T(8,128)(2,1)S(1)} %get-tuple-element.48), channel_id=1, source_target_pairs={{0,3},{1,2},{2,1},{3,0},{4,7},{5,6},{6,5},{7,4},{8,11},{9,10},{10,... | collective-permute-start | bytes 2555912 | tf_op jit(solution)/shard_map/ppermute | solution.py:224
  100.4 26.0 %collective-permute-start.10 = (bf16[128,3328]{1,0:T(8,128)(2,1)S(1)}, bf16[128,3328]{1,0:T(8,128)(2,1)S(1)}, u32[]{:S(2)}, u32[]{:S(2)}) collective-permute-start(bf16[128,3328]{1,0:T(8,128)(2,1)S(1)} %get-tuple-element.55), channel_id=1, source_target_pairs={{0,1},{1,0},{2,3},{3,2},{4,5},{5,4},{6,7},{7,6},{8,9},{9,8},{10,11... | collective-permute-start | bytes 2555912 | tf_op jit(solution)/shard_map/ppermute | solution.py:224
  108.3 14.7 %collective-permute-start.11 = (bf16[64,3328]{1,0:T(8,128)(2,1)S(1)}, bf16[64,3328]{1,0:T(8,128)(2,1)S(1)}, u32[]{:S(2)}, u32[]{:S(2)}) collective-permute-start(bf16[64,3328]{1,0:T(8,128)(2,1)S(1)} %get-tuple-element.56), channel_id=1, source_target_pairs={{0,4},{4,0},{1,5},{5,1},{2,6},{6,2},{3,7},{7,3},{8,12},{12,8},{9,1... | collective-permute-start | bytes 1277960 | tf_op jit(solution)/shard_map/ppermute | solution.py:223
  113.3 27.8 %collective-permute-start.15 = (bf16[128,3328]{1,0:T(8,128)(2,1)S(1)}, bf16[128,3328]{1,0:T(8,128)(2,1)S(1)}, u32[]{:S(2)}, u32[]{:S(2)}) collective-permute-start(bf16[128,3328]{1,0:T(8,128)(2,1)S(1)} %get-tuple-element.63), channel_id=1, source_target_pairs={{0,3},{1,2},{2,1},{3,0},{4,7},{5,6},{6,5},{7,4},{8,11},{9,10},{10,... | collective-permute-start | bytes 2555912 | tf_op jit(solution)/shard_map/ppermute | solution.py:224
  123.0 11.8 %collective-permute-start.9 = (bf16[64,3328]{1,0:T(8,128)(2,1)S(1)}, bf16[64,3328]{1,0:T(8,128)(2,1)S(1)}, u32[]{:S(2)}, u32[]{:S(2)}) collective-permute-start(bf16[64,3328]{1,0:T(8,128)(2,1)S(1)} %get-tuple-element.54), channel_id=1, source_target_pairs={{0,1},{1,0},{2,3},{3,2},{4,5},{5,4},{6,7},{7,6},{8,9},{9,8},{10,11... | collective-permute-start | bytes 1277960 | tf_op jit(solution)/shard_map/ppermute | solution.py:224
  126.5 14.7 %collective-permute-start.14 = (bf16[64,3328]{1,0:T(8,128)(2,1)S(1)}, bf16[64,3328]{1,0:T(8,128)(2,1)S(1)}, u32[]{:S(2)}, u32[]{:S(2)}) collective-permute-start(bf16[64,3328]{1,0:T(8,128)(2,1)S(1)} %get-tuple-element.62), channel_id=1, source_target_pairs={{0,4},{4,0},{1,5},{5,1},{2,6},{6,2},{3,7},{7,3},{8,12},{12,8},{9,1... | collective-permute-start | bytes 1277960 | tf_op jit(solution)/shard_map/ppermute | solution.py:223
  126.6 19.1 %collective-permute-start.13 = (bf16[32,3328]{1,0:T(8,128)(2,1)S(1)}, bf16[32,3328]{1,0:T(8,128)(2,1)S(1)}, u32[]{:S(2)}, u32[]{:S(2)}) collective-permute-start(bf16[32,3328]{1,0:T(8,128)(2,1)S(1)} %get-tuple-element.61), channel_id=1, source_target_pairs={{0,3},{1,2},{2,1},{3,0},{4,7},{5,6},{6,5},{7,4},{8,11},{9,10},{10,... | collective-permute-start | bytes 638984 | tf_op jit(solution)/shard_map/ppermute | solution.py:224
  134.8 11.0 %collective-permute-start.12 = (bf16[32,3328]{1,0:T(8,128)(2,1)S(1)}, bf16[32,3328]{1,0:T(8,128)(2,1)S(1)}, u32[]{:S(2)}, u32[]{:S(2)}) collective-permute-start(bf16[32,3328]{1,0:T(8,128)(2,1)S(1)} %get-tuple-element.60), channel_id=1, source_target_pairs={{0,4},{4,0},{1,5},{5,1},{2,6},{6,2},{3,7},{7,3},{8,12},{12,8},{9,1... | collective-permute-start | bytes 638984 | tf_op jit(solution)/shard_map/ppermute | solution.py:223
  141.3 9.1 %collective-permute-start.17 = (bf16[32,3328]{1,0:T(8,128)(2,1)S(1)}, bf16[32,3328]{1,0:T(8,128)(2,1)S(1)}, u32[]{:S(2)}, u32[]{:S(2)}) collective-permute-start(bf16[32,3328]{1,0:T(8,128)(2,1)S(1)} %get-tuple-element.66), channel_id=1, source_target_pairs={{0,3},{1,2},{2,1},{3,0},{4,7},{5,6},{6,5},{7,4},{8,11},{9,10},{10,... | collective-permute-start | bytes 638984 | tf_op jit(solution)/shard_map/ppermute | solution.py:224
  141.9 12.1 %collective-permute-start.21 = (bf16[64,3328]{1,0:T(8,128)(2,1)S(1)}, bf16[64,3328]{1,0:T(8,128)(2,1)S(1)}, u32[]{:S(2)}, u32[]{:S(2)}) collective-permute-start(bf16[64,3328]{1,0:T(8,128)(2,1)S(1)} %get-tuple-element.67), channel_id=1, source_target_pairs={{0,4},{4,0},{1,5},{5,1},{2,6},{6,2},{3,7},{7,3},{8,12},{12,8},{9,1... | collective-permute-start | bytes 1277960 | tf_op jit(solution)/shard_map/ppermute | solution.py:223
  145.7 10.1 %collective-permute-start.20 = (bf16[32,1664]{1,0:T(8,128)(2,1)S(1)}, bf16[32,1664]{1,0:T(8,128)(2,1)S(1)}, u32[]{:S(2)}, u32[]{:S(2)}) collective-permute-start(bf16[32,1664]{1,0:T(8,128)(2,1)S(1)} %hidden.4.refs_2_.refs_0_), channel_id=1, source_target_pairs={{0,4},{4,0},{1,5},{5,1},{2,6},{6,2},{3,7},{7,3},{8,12},{12,8},{9,1... | collective-permute-start | bytes 319496 | tf_op jit(solution)/shard_map/ppermute | solution.py:223
  145.9 6.1 %collective-permute-start.16 = (bf16[32,1664]{1,0:T(8,128)(2,1)S(1)}, bf16[32,1664]{1,0:T(8,128)(2,1)S(1)}, u32[]{:S(2)}, u32[]{:S(2)}) collective-permute-start(bf16[32,1664]{1,0:T(8,128)(2,1)S(1)} %hidden.5.refs_2_.refs_0_), channel_id=1, source_target_pairs={{0,3},{1,2},{2,1},{3,0},{4,7},{5,6},{6,5},{7,4},{8,11},{9,10},{10,... | collective-permute-start | bytes 319496 | tf_op jit(solution)/shard_map/ppermute | solution.py:224
  150.5 9.3 %collective-permute-start.19 = (bf16[32,1664]{1,0:T(8,128)(2,1)S(1)}, bf16[32,1664]{1,0:T(8,128)(2,1)S(1)}, u32[]{:S(2)}, u32[]{:S(2)}) collective-permute-start(bf16[32,1664]{1,0:T(8,128)(2,1)S(1)} %hidden.6.refs_2_.refs_0_), channel_id=1, source_target_pairs={{0,1},{1,0},{2,3},{3,2},{4,5},{5,4},{6,7},{7,6},{8,9},{9,8},{10,11... | collective-permute-start | bytes 319496 | tf_op jit(solution)/shard_map/ppermute | solution.py:224
  152.0 8.4 %collective-permute-start.18 = (bf16[64,1664]{1,0:T(8,128)(2,1)S(1)}, bf16[64,1664]{1,0:T(8,128)(2,1)S(1)}, u32[]{:S(2)}, u32[]{:S(2)}) collective-permute-start(bf16[64,1664]{1,0:T(8,128)(2,1)S(1)} %join.8.refs_2_.refs_0_), channel_id=1, source_target_pairs={{0,4},{4,0},{1,5},{5,1},{2,6},{6,2},{3,7},{7,3},{8,12},{12,8},{9,1... | collective-permute-start | bytes 638984 | tf_op jit(solution)/shard_map/ppermute | solution.py:223
  154.1 6.4 %collective-permute-start.23 = (bf16[32,3328]{1,0:T(8,128)(2,1)S(1)}, bf16[32,3328]{1,0:T(8,128)(2,1)S(1)}, u32[]{:S(2)}, u32[]{:S(2)}) collective-permute-start(bf16[32,3328]{1,0:T(8,128)(2,1)S(1)} %get-tuple-element.70), channel_id=1, source_target_pairs={{0,1},{1,0},{2,3},{3,2},{4,5},{5,4},{6,7},{7,6},{8,9},{9,8},{10,11... | collective-permute-start | bytes 638984 | tf_op jit(solution)/shard_map/ppermute | solution.py:224
  155.9 8.7 %collective-permute-start.26 = (bf16[64,1664]{1,0:T(8,128)(2,1)S(1)}, bf16[64,1664]{1,0:T(8,128)(2,1)S(1)}, u32[]{:S(2)}, u32[]{:S(2)}) collective-permute-start(bf16[64,1664]{1,0:T(8,128)(2,1)S(1)} %join.9.refs_2_.refs_0_), channel_id=1, source_target_pairs={{0,3},{1,2},{2,1},{3,0},{4,7},{5,6},{6,5},{7,4},{8,11},{9,10},{10,... | collective-permute-start | bytes 638984 | tf_op jit(solution)/shard_map/ppermute | solution.py:224
  159.8 6.3 %collective-permute-start.25 = (bf16[64,1664]{1,0:T(8,128)(2,1)S(1)}, bf16[64,1664]{1,0:T(8,128)(2,1)S(1)}, u32[]{:S(2)}, u32[]{:S(2)}) collective-permute-start(bf16[64,1664]{1,0:T(8,128)(2,1)S(1)} %join.10.refs_2_.refs_0_), channel_id=1, source_target_pairs={{0,4},{4,0},{1,5},{5,1},{2,6},{6,2},{3,7},{7,3},{8,12},{12,8},{9,1... | collective-permute-start | bytes 638984 | tf_op jit(solution)/shard_map/ppermute | solution.py:223
  160.4 12.8 %collective-permute-start.22 = (bf16[128,1664]{1,0:T(8,128)(2,1)S(1)}, bf16[128,1664]{1,0:T(8,128)(2,1)S(1)}, u32[]{:S(2)}, u32[]{:S(2)}) collective-permute-start(bf16[128,1664]{1,0:T(8,128)(2,1)S(1)} %join.11.refs_2_.refs_0_), channel_id=1, source_target_pairs={{0,1},{1,0},{2,3},{3,2},{4,5},{5,4},{6,7},{7,6},{8,9},{9,8},{10,11... | collective-permute-start | bytes 1277960 | tf_op jit(solution)/shard_map/ppermute | solution.py:224
  160.6 7.6 %collective-permute-start.24 = (bf16[32,1664]{1,0:T(8,128)(2,1)S(1)}, bf16[32,1664]{1,0:T(8,128)(2,1)S(1)}, u32[]{:S(2)}, u32[]{:S(2)}) collective-permute-start(bf16[32,1664]{1,0:T(8,128)(2,1)S(1)} %hidden.7.refs_2_.refs_0_), channel_id=1, source_target_pairs={{0,3},{1,2},{2,1},{3,0},{4,7},{5,6},{6,5},{7,4},{8,11},{9,10},{10,... | collective-permute-start | bytes 319496 | tf_op jit(solution)/shard_map/ppermute | solution.py:224
  164.6 16.4 %collective-permute-start.33 = (bf16[128,1664]{1,0:T(8,128)(2,1)S(1)}, bf16[128,1664]{1,0:T(8,128)(2,1)S(1)}, u32[]{:S(2)}, u32[]{:S(2)}) collective-permute-start(bf16[128,1664]{1,0:T(8,128)(2,1)S(1)} %join.12.refs_2_.refs_0_), channel_id=1, source_target_pairs={{0,1},{1,0},{2,3},{3,2},{4,5},{5,4},{6,7},{7,6},{8,9},{9,8},{10,11... | collective-permute-start | bytes 1277960 | tf_op jit(solution)/shard_map/ppermute | solution.py:224
  166.1 10.8 %collective-permute-start.28 = (bf16[128,1664]{1,0:T(8,128)(2,1)S(1)}, bf16[128,1664]{1,0:T(8,128)(2,1)S(1)}, u32[]{:S(2)}, u32[]{:S(2)}) collective-permute-start(bf16[128,1664]{1,0:T(8,128)(2,1)S(1)} %join.13.refs_2_.refs_0_), channel_id=1, source_target_pairs={{0,3},{1,2},{2,1},{3,0},{4,7},{5,6},{6,5},{7,4},{8,11},{9,10},{10,... | collective-permute-start | bytes 1277960 | tf_op jit(solution)/shard_map/ppermute | solution.py:224
  168.3 8.5 %collective-permute-start.29 = (bf16[64,1664]{1,0:T(8,128)(2,1)S(1)}, bf16[64,1664]{1,0:T(8,128)(2,1)S(1)}, u32[]{:S(2)}, u32[]{:S(2)}) collective-permute-start(bf16[64,1664]{1,0:T(8,128)(2,1)S(1)} %join.14.refs_3_.refs_0_), channel_id=1, source_target_pairs={{0,4},{4,0},{1,5},{5,1},{2,6},{6,2},{3,7},{7,3},{8,12},{12,8},{9,1... | collective-permute-start | bytes 638984 | tf_op jit(solution)/shard_map/ppermute | solution.py:223
  176.7 4.2 %collective-permute-start.27 = (bf16[128,2048]{1,0:T(8,128)(2,1)S(1)}, bf16[128,2048]{1,0:T(8,128)(2,1)S(1)}, u32[]{:S(2)}, u32[]{:S(2)}) collective-permute-start(bf16[128,2048]{1,0:T(8,128)(2,1)S(1)} %get-tuple-element.72), channel_id=1, source_target_pairs={{0,8},{8,0},{1,9},{9,1},{2,10},{10,2},{3,11},{11,3},{4,12},{12,4},... | collective-permute-start | bytes 1572872 | tf_op jit(solution)/shard_map/ppermute | solution.py:164
  176.8 12.3 %collective-permute-start.37 = (bf16[128,1664]{1,0:T(8,128)(2,1)S(1)}, bf16[128,1664]{1,0:T(8,128)(2,1)S(1)}, u32[]{:S(2)}, u32[]{:S(2)}) collective-permute-start(bf16[128,1664]{1,0:T(8,128)(2,1)S(1)} %join.15.refs_3_.refs_0_), channel_id=1, source_target_pairs={{0,1},{1,0},{2,3},{3,2},{4,5},{5,4},{6,7},{7,6},{8,9},{9,8},{10,11... | collective-permute-start | bytes 1277960 | tf_op jit(solution)/shard_map/ppermute | solution.py:224
  180.3 7.8 %collective-permute-start.32 = (bf16[128,2048]{1,0:T(8,128)(2,1)S(1)}, bf16[128,2048]{1,0:T(8,128)(2,1)S(1)}, u32[]{:S(2)}, u32[]{:S(2)}) collective-permute-start(bf16[128,2048]{1,0:T(8,128)(2,1)S(1)} %get-tuple-element.74), channel_id=1, source_target_pairs={{0,8},{8,0},{1,9},{9,1},{2,10},{10,2},{3,11},{11,3},{4,12},{12,4},... | collective-permute-start | bytes 1572872 | tf_op jit(solution)/shard_map/ppermute | solution.py:164
  184.4 10.3 %collective-permute-start.36 = (bf16[128,2048]{1,0:T(8,128)(2,1)S(1)}, bf16[128,2048]{1,0:T(8,128)(2,1)S(1)}, u32[]{:S(2)}, u32[]{:S(2)}) collective-permute-start(bf16[128,2048]{1,0:T(8,128)(2,1)S(1)} %get-tuple-element.76), channel_id=1, source_target_pairs={{0,8},{8,0},{1,9},{9,1},{2,10},{10,2},{3,11},{11,3},{4,12},{12,4},... | collective-permute-start | bytes 1572872 | tf_op jit(solution)/shard_map/ppermute | solution.py:164
  184.5 13.0 %collective-permute-start.30 = (bf16[64,2048]{1,0:T(8,128)(2,1)S(1)}, bf16[64,2048]{1,0:T(8,128)(2,1)S(1)}, u32[]{:S(2)}, u32[]{:S(2)}) collective-permute-start(bf16[64,2048]{1,0:T(8,128)(2,1)S(1)} %get-tuple-element.86), channel_id=1, source_target_pairs={{0,48},{16,32},{32,80},{48,64},{64,112},{80,96},{96,16},{112,0},{1... | collective-permute-start | bytes 786440 | tf_op jit(solution)/shard_map/ppermute | solution.py:173
  187.9 14.5 %collective-permute-start.31 = (bf16[64,2048]{1,0:T(8,128)(2,1)S(1)}, bf16[64,2048]{1,0:T(8,128)(2,1)S(1)}, u32[]{:S(2)}, u32[]{:S(2)}) collective-permute-start(bf16[64,2048]{1,0:T(8,128)(2,1)S(1)} %get-tuple-element.85), channel_id=1, source_target_pairs={{0,32},{16,48},{32,64},{48,80},{64,96},{80,112},{96,0},{112,16},{1... | collective-permute-start | bytes 786440 | tf_op jit(solution)/shard_map/ppermute | solution.py:173
  192.5 3.3 %collective-permute-start.39 = (bf16[128,2048]{1,0:T(8,128)(2,1)S(1)}, bf16[128,2048]{1,0:T(8,128)(2,1)S(1)}, u32[]{:S(2)}, u32[]{:S(2)}) collective-permute-start(bf16[128,2048]{1,0:T(8,128)(2,1)S(1)} %get-tuple-element.78), channel_id=1, source_target_pairs={{0,8},{8,0},{1,9},{9,1},{2,10},{10,2},{3,11},{11,3},{4,12},{12,4},... | collective-permute-start | bytes 1572872 | tf_op jit(solution)/shard_map/ppermute | solution.py:164
  192.6 12.8 %collective-permute-start.34 = (bf16[64,2048]{1,0:T(8,128)(2,1)S(1)}, bf16[64,2048]{1,0:T(8,128)(2,1)S(1)}, u32[]{:S(2)}, u32[]{:S(2)}) collective-permute-start(bf16[64,2048]{1,0:T(8,128)(2,1)S(1)} %get-tuple-element.84), channel_id=1, source_target_pairs={{0,112},{16,96},{32,16},{48,0},{64,48},{80,32},{96,80},{112,64},{1... | collective-permute-start | bytes 786440 | tf_op jit(solution)/shard_map/ppermute | solution.py:173
  194.7 15.5 %collective-permute-start.35 = (bf16[64,2048]{1,0:T(8,128)(2,1)S(1)}, bf16[64,2048]{1,0:T(8,128)(2,1)S(1)}, u32[]{:S(2)}, u32[]{:S(2)}) collective-permute-start(bf16[64,2048]{1,0:T(8,128)(2,1)S(1)} %get-tuple-element.83), channel_id=1, source_target_pairs={{0,96},{16,112},{32,0},{48,16},{64,32},{80,48},{96,64},{112,80},{1... | collective-permute-start | bytes 786440 | tf_op jit(solution)/shard_map/ppermute | solution.py:173
  195.8 15.2 %collective-permute-start.38 = (bf16[64,2048]{1,0:T(8,128)(2,1)S(1)}, bf16[64,2048]{1,0:T(8,128)(2,1)S(1)}, u32[]{:S(2)}, u32[]{:S(2)}) collective-permute-start(bf16[64,2048]{1,0:T(8,128)(2,1)S(1)} %select_convert_fusion.2), channel_id=1, source_target_pairs={{0,16},{16,0},{32,48},{48,32},{64,80},{80,64},{96,112},{112,96},{1... | collective-permute-start | bytes 786440 | tf_op jit(solution)/shard_map/ppermute | solution.py:173
  197.6 19.1 %collective-permute-start.40 = (bf16[64,2048]{1,0:T(8,128)(2,1)S(1)}, bf16[64,2048]{1,0:T(8,128)(2,1)S(1)}, u32[]{:S(2)}, u32[]{:S(2)}) collective-permute-start(bf16[64,2048]{1,0:T(8,128)(2,1)S(1)} %get-tuple-element.82), channel_id=1, source_target_pairs={{0,80},{16,64},{32,112},{48,96},{64,16},{80,0},{96,48},{112,32},{1... | collective-permute-start | bytes 786440 | tf_op jit(solution)/shard_map/ppermute | solution.py:173
  202.4 18.7 %collective-permute-start.41 = (bf16[64,2048]{1,0:T(8,128)(2,1)S(1)}, bf16[64,2048]{1,0:T(8,128)(2,1)S(1)}, u32[]{:S(2)}, u32[]{:S(2)}) collective-permute-start(bf16[64,2048]{1,0:T(8,128)(2,1)S(1)} %get-tuple-element.81), channel_id=1, source_target_pairs={{0,64},{16,80},{32,96},{48,112},{64,0},{80,16},{96,32},{112,48},{1... | collective-permute-start | bytes 786440 | tf_op jit(solution)/shard_map/ppermute | solution.py:173
  202.7 18.6 %copy-start.13 = (f32[2,64,2048]{2,1,0:T(8,128)S(1)}, f32[2,64,2048]{2,1,0:T(8,128)}, u32[]{:S(2)}) copy-start(f32[2,64,2048]{2,1,0:T(8,128)} %slice_convert_fusion) | copy-start | bytes 3145732
  (16 other events, 54.6 us)
